TPU v7x, 128 devices: a whole 4x4x4 slice. The times are simulated.
128 devices in a mesh: gy: 16 (over x, y), gz: 8 (over z, core).
Axes of the slice: x: 4, y: 4, z: 4, core: 2. Of those that a mesh axis runs over, the one named last changes fastest.
Arguments:
- adjoint: float32 [19, 128, 256, 128], P(None, 'gy', 'gz'), may hold values from -6 to 6
- collision: float32 [19, 19], replicated, may hold values from -0.25 to 0.85
- link_cell: int32 [128, 128, 8], P(('gy', 'gz')), may hold values from 0 to 255
- link_dir: int32 [128, 128, 8], P(('gy', 'gz')), may hold values from 1 to 18
- link_panel: int32 [128, 128, 8], P(('gy', 'gz')), may hold values from -1 to 63, as said below
Outputs:
- adjoint_out: float32 [19, 128, 256, 128], P(None, 'gy', 'gz')
- panel_sens: float32 [8192, 128], P(('gy', 'gz'))
Inputs may be any that keep to these rules, and one draw needn't show every extreme that they name: `link_panel`: -1 marks an empty slot.
All inputs are finite; a program needn't handle non-finite values.
Results may differ from a plain program's by a relative error of at most 0.0001.
Values sent between devices are 32-bit elements; how exact they have to be, the bound alone decides.
No kernel may reach another device: no remote copies, remote signals or barrier semaphores. Data moves between devices by JAX's collectives and lax.ppermute only.
A program may use at most 64 MiB of HBM per device.

v0:
```python
import functools

import jax
import jax.numpy as jnp
from jax import lax
from jax.experimental import pallas as pl
from jax.experimental.pallas import tpu as pltpu
from jax.sharding import PartitionSpec as P

Q = 19
QP = 20
P_DEV = 64
CAP = 8
CY = 8
CZ = 32
X = 128
ROWS = 48
Z0 = 8

DIRS = [
    (0, 0, 0),
    (1, 0, 0),
    (-1, 0, 0),
    (0, 1, 0),
    (0, -1, 0),
    (0, 0, 1),
    (0, 0, -1),
    (1, 1, 0),
    (-1, -1, 0),
    (1, -1, 0),
    (-1, 1, 0),
    (1, 0, 1),
    (-1, 0, -1),
    (1, 0, -1),
    (-1, 0, 1),
    (0, 1, 1),
    (0, -1, -1),
    (0, 1, -1),
    (0, -1, 1),
]
LINK_WEIGHTS = [2.0] + [1.0 / 3.0] * 6 + [1.0 / 6.0] * 12

Y_UP = [q for q in range(Q) if DIRS[q][1] == 1]
Y_DOWN = [q for q in range(Q) if DIRS[q][1] == -1]
Z_UP = [q for q in range(Q) if DIRS[q][2] == 1]
Z_DOWN = [q for q in range(Q) if DIRS[q][2] == -1]
Z_FLAT = [q for q in range(Q) if DIRS[q][2] == 0]
SEND_LOW = [(q, 0) for q in Z_FLAT] + [(q, 0) for q in Z_UP] + [(q, 1) for q in Z_UP]
SEND_HIGH = [(q, 0) for q in Z_FLAT] + [(q, 0) for q in Z_DOWN] + [(q, 1) for q in Z_DOWN]

RAW = 0
ENDS = 5 * CZ
MIXED = ENDS + 16
Y_ROWS = MIXED + 5 * CZ

f32 = jnp.float32
bf16 = jnp.bfloat16


def along_x(value, q):
    cx = DIRS[q][0]
    if cx == 0:
        return value
    return pltpu.roll(value, (-cx) % X, value.ndim - 1)


def split(value):
    high = value.astype(bf16)
    return high, (value - high.astype(f32)).astype(bf16)


def mix(weights, reads):
    wh, wl = weights
    rh, rl = split(reads)
    dot = functools.partial(jnp.dot, preferred_element_type=f32)
    return dot(wh, rh) + (dot(wl, rh) + dot(wh, rl))


def stacked(tiles):
    count = max(len(t) for t in tiles if t is not None)
    zero = jnp.zeros((8, X), f32)
    full = [t if t is not None else [zero] * count for t in tiles]
    return jnp.concatenate(
        [jnp.concatenate([t[c] for t in full], axis=0) for c in range(count)], axis=1
    )


def line_tiles(line):
    return [line[8 * t : 8 * t + 8, :] for t in range(CZ // 8)]


def read_line(ref, p, y, shift=0):
    cx, cy, cz = DIRS[p]
    return ref[p, y + 1 + cy, pl.ds(Z0 + cz + shift, CZ), :]


def read_row(ref, y):
    return stacked([line_tiles(read_line(ref, p, y)) for p in range(Q)] + [None])


def group(w_ref, channels):
    rows = [w_ref[8 * q : 8 * q + 8, :] for q in channels]
    rows += [jnp.zeros_like(rows[0])] * ((-len(rows)) % 2)
    return split(jnp.concatenate(rows, axis=0))


def load_column(ref, q, y, z):
    flat = ref.reshape(Q, (CY + 2) * ROWS, X)
    return flat[q, pl.ds((1 + y) * ROWS + Z0 + z, CY, stride=ROWS), :]


def store_column(ref, q, y, z, value):
    flat = ref.reshape(Q, (CY + 2) * ROWS, X)
    flat[q, pl.ds((1 + y) * ROWS + Z0 + z, CY, stride=ROWS), :] = value


def pack_z_kernel(field, to_pair, to_next):
    even = lax.rem(lax.axis_index("gz"), 2) == 0
    for i in range(Q):
        q, d = SEND_LOW[i]
        low = field[q, pl.ds(d, CY, stride=CZ), :]
        q, d = SEND_HIGH[i]
        high = field[q, pl.ds(CZ - 1 - d, CY, stride=CZ), :]
        to_pair[8 * i : 8 * i + 8, :] = jnp.where(even, high, low)
        to_next[8 * i : 8 * i + 8, :] = jnp.where(even, low, high)


def prepare_kernel(field, collision, cell, direction, s0, w, pick):
    for q in range(Q):
        for y in range(CY):
            s0[q, 1 + y, Z0 : Z0 + CZ, :] = along_x(field[q, CZ * y : CZ * y + CZ, :], q)
    zero = jnp.zeros((ROWS, X), f32)
    for q in Y_DOWN:
        s0[q, 0, :, :] = zero
    for q in Y_UP:
        s0[q, CY + 1, :, :] = zero
    n = QP * 8
    spread = (
        lax.broadcasted_iota(jnp.int32, (n, Q), 0) // 8 == lax.broadcasted_iota(jnp.int32, (n, Q), 1)
    ).astype(f32)
    turned = lax.dot_general(
        spread, collision[...], (((1,), (1,)), ((), ())),
        precision=lax.Precision.HIGHEST, preferred_element_type=f32,
    )
    wide = lax.dot_general(
        turned, spread, (((1,), (1,)), ((), ())),
        precision=lax.Precision.HIGHEST, preferred_element_type=f32,
    )
    same = (
        lax.broadcasted_iota(jnp.int32, (n, n), 0) % 8
        == lax.broadcasted_iota(jnp.int32, (n, n), 1) % 8
    )
    w[...] = jnp.where(same, wide, 0.0)
    pick[...] = direction[...] * (CY * CZ) + cell[...]


def edge_rows_kernel(s0_in, w, from_pair, from_next, s0, s1, to_low, to_high):
    del s0_in
    iz = lax.axis_index("gz")
    even = lax.rem(iz, 2) == 0
    above = iz < lax.axis_size("gz") - 1
    below = iz > 0
    for i in range(Q):
        pair = from_pair[8 * i : 8 * i + 8, :]
        following = from_next[8 * i : 8 * i + 8, :]
        q, d = SEND_LOW[i]
        value = jnp.where(above, jnp.where(even, pair, following), 0.0)
        store_column(s0, q, 0, CZ + d, along_x(value, q))
        q, d = SEND_HIGH[i]
        value = jnp.where(below, jnp.where(even, following, pair), 0.0)
        store_column(s0, q, 0, -1 - d, along_x(value, q))
    weights = split(w[...])
    for z, channels, valid in ((CZ, Z_UP, above), (-1, Z_DOWN, below)):
        reads = stacked(
            [[load_column(s0, p, DIRS[p][1], z + DIRS[p][2])] for p in range(Q)] + [None]
        )
        out = mix(group(w, channels), reads)
        for i, q in enumerate(channels):
            value = jnp.where(valid, out[8 * i : 8 * i + 8, :], 0.0)
            store_column(s1, q, 0, z, along_x(value, q))
    for y in (0, CY - 1):
        store_line(s1, y, mix(weights, read_row(s0, y)))
    for y, channels, message in ((0, Y_UP, to_low), (CY - 1, Y_DOWN, to_high)):
        message[ENDS : ENDS + 16, :] = jnp.zeros((16, X), f32)
        for i, q in enumerate(channels):
            cz = DIRS[q][2]
            message[RAW + CZ * i : RAW + CZ * i + CZ, :] = s0[q, 1 + y, pl.ds(Z0 + cz, CZ), :]
            message[pl.ds(ENDS + 2 * i, 1), :] = s0[q, 1 + y, pl.ds(Z0 + cz - 1, 1), :]
            message[pl.ds(ENDS + 2 * i + 1, 1), :] = s0[q, 1 + y, pl.ds(Z0 + cz + CZ, 1), :]
            message[MIXED + CZ * i : MIXED + CZ * i + CZ, :] = s1[q, 1 + y, pl.ds(Z0 + cz, CZ), :]


def store_line(s1, y, out):
    for q in range(Q):
        for t in range(CZ // 8):
            s1[q, 1 + y, Z0 + 8 * t : Z0 + 8 * t + 8, :] = along_x(
                out[8 * q : 8 * q + 8, X * t : X * t + X], q
            )


def inner_rows_kernel(s0, w, s1_in, s1, beyond, out, kept, sem):
    del s1_in
    iz = lax.axis_index("gz")
    above = iz < lax.axis_size("gz") - 1
    below = iz > 0
    weights = split(w[...])

    @pl.loop(1, CY - 1)
    def _(y):
        store_line(s1, y, mix(weights, read_row(s0, y)))

    @pl.loop(2, CY - 2)
    def _(y):
        mixed = mix(weights, read_row(s1, y))
        for q in range(Q):
            for t in range(CZ // 8):
                kept[q, y - 2, 8 * t : 8 * t + 8, :] = mixed[8 * q : 8 * q + 8, X * t : X * t + X]

    copy = pltpu.make_async_copy(kept, out.at[:, pl.ds(2, CY - 4), :, :], sem)
    copy.start()
    for side, (y, channels, sources) in enumerate(((CY - 1, Y_UP, Y_DOWN), (0, Y_DOWN, Y_UP))):
        for shift in (0, 1, -1):
            wanted = [q for q in channels if DIRS[q][2] == shift]
            reads = stacked(
                [
                    line_tiles(s0[p, 1 + y, pl.ds(Z0 + DIRS[p][2] + shift, CZ), :])
                    if p in sources
                    else None
                    for p in range(Q)
                ]
                + [None]
            )
            mixed = mix(group(w, wanted), reads)
            cells = lax.broadcasted_iota(jnp.int32, (8, X), 0)
            for i, q in enumerate(wanted):
                at = CZ * (5 * side + channels.index(q))
                for t in range(CZ // 8):
                    value = mixed[8 * i : 8 * i + 8, X * t : X * t + X]
                    if shift == 1 and t == CZ // 8 - 1:
                        value = jnp.where(jnp.logical_or(above, cells < 7), value, 0.0)
                    if shift == -1 and t == 0:
                        value = jnp.where(jnp.logical_or(below, cells > 0), value, 0.0)
                    beyond[at + 8 * t : at + 8 * t + 8, :] = along_x(value, q)
    copy.wait()


def outer_rows_kernel(
    s1_in, w, beyond, from_high, from_low, panel, pick, out_in,
    s1, rows, out, kept, inner, scaled, ends, numbers, in_sem, out_sem,
):
    del s1_in
    iy = lax.axis_index("gy")
    iz = lax.axis_index("gz")
    fetch = pltpu.make_async_copy(out_in.at[:, pl.ds(2, CY - 4), :, :], inner, in_sem)
    fetch.start()
    weights = split(w[...])
    numbers[...] = jnp.zeros((128, X), f32)
    numbers[:, 0:CAP] = panel[...].astype(f32).T
    z_ok = (iz > 0, iz < lax.axis_size("gz") - 1)
    sides = (
        (0, CY - 1, CY, Y_UP, from_high, iy < lax.axis_size("gy") - 1),
        (1, 0, -1, Y_DOWN, from_low, iy > 0),
    )
    for side, y, halo, channels, arrived, valid in sides:
        ends[...] = jnp.zeros((5 * 8, X), f32)
        for i in range(5):
            ends[8 * i : 8 * i + 2, :] = arrived[ENDS + 2 * i : ENDS + 2 * i + 2, :]
        tiles = [None] * (Q + 1)
        for i, p in enumerate(channels):
            tiles[p] = line_tiles(arrived[RAW + CZ * i : RAW + CZ * i + CZ, :]) + [
                ends[8 * i : 8 * i + 8, :]
            ]
        mixed = mix(weights, jnp.where(valid, stacked(tiles), 0.0))
        for q in range(Q):
            for t in range(CZ // 8):
                at = pl.ds(Z0 + 8 * t, 8)
                s1[q, 1 + y, at, :] += along_x(mixed[8 * q : 8 * q + 8, X * t : X * t + X], q)
            cz = DIRS[q][2]
            if cz:
                row = 0 if cz < 0 else 1
                end = along_x(mixed[8 * q : 8 * q + 8, X * (CZ // 8) :], q)[row : row + 1, :]
                at = pl.ds(Z0 - 1 if cz < 0 else Z0 + CZ, 1)
                s1[q, 1 + y, at, :] += jnp.where(z_ok[row], end, 0.0)
        for i, q in enumerate(channels):
            line = beyond[CZ * (5 * side + i) : CZ * (5 * side + i) + CZ, :]
            line = line + arrived[MIXED + CZ * i : MIXED + CZ * i + CZ, :]
            s1[q, 1 + halo, pl.ds(Z0 + DIRS[q][2], CZ), :] = jnp.where(valid, line, 0.0)

    for k, y in enumerate((0, 1, CY - 2, CY - 1)):
        mixed = mix(weights, read_row(s1, y))
        for q in range(Q):
            for t in range(CZ // 8):
                value = mixed[8 * q : 8 * q + 8, X * t : X * t + X]
                kept[q, k, 8 * t : 8 * t + 8, :] = value
                at = q * (CY * CZ) + y * CZ + 8 * t
                scaled[at : at + 8, :] = value * LINK_WEIGHTS[q]
    copies = [
        pltpu.make_async_copy(
            kept.at[:, pl.ds(2 * h, 2), :, :], out.at[:, pl.ds(6 * h, 2), :, :], out_sem.at[h]
        )
        for h in range(2)
    ]
    for copy in copies:
        copy.start()
    fetch.wait()
    for q in range(Q):
        for y in range(2, CY - 2):
            at = q * (CY * CZ) + y * CZ
            scaled[at : at + CZ, :] = inner[q, y - 2, :, :] * LINK_WEIGHTS[q]

    @pl.loop(0, 128, unroll=4)
    def _(d):
        for k in range(CAP):
            rows[pl.ds(d * (CAP + 1) + k, 1), 0, :] = scaled[pl.ds(pick[k, d], 1), :]
        rows[pl.ds(d * (CAP + 1) + CAP, 1), 0, :] = numbers[pl.ds(d, 1), :]

    for copy in copies:
        copy.wait()


def sum_kernel(arrived, out):
    devices = arrived.shape[0] // (CAP + 1)
    numbers = arrived[pl.ds(CAP, devices, stride=CAP + 1), :].T
    panels = lax.broadcasted_iota(jnp.int32, (P_DEV, devices), 0).astype(f32)
    hot, rows = [], []
    for k in range(CAP):
        hot.append((numbers[k : k + 1, :] == panels).astype(f32).astype(bf16))
        rows.append(arrived[pl.ds(k, devices, stride=CAP + 1), :])
    hot = jnp.concatenate(hot, axis=1)
    high, low = split(jnp.concatenate(rows, axis=0))
    dot = functools.partial(jnp.dot, preferred_element_type=f32)
    out[...] = dot(hot, high) + dot(hot, low)


VMEM = pl.BlockSpec(memory_space=pltpu.VMEM)
SMEM = pl.BlockSpec(memory_space=pltpu.SMEM)
ANY = pl.BlockSpec(memory_space=pl.ANY)
LIMIT = 32 * 1024 * 1024


def call(kernel, name, ins, outs, shapes, scratch=(), aliases=None):
    return pl.pallas_call(
        kernel,
        out_shape=[jax.ShapeDtypeStruct(*s) for s in shapes],
        in_specs=ins,
        out_specs=outs,
        scratch_shapes=list(scratch),
        input_output_aliases=aliases or {},
        compiler_params=pltpu.CompilerParams(vmem_limit_bytes=LIMIT),
        name=name,
    )


def on_device(adjoint, collision, link_cell, link_dir, link_panel):
    gz = lax.axis_size("gz")
    gy = lax.axis_size("gy")
    devices = gy * gz
    flat = adjoint.reshape(Q, CY * CZ, X)
    pad = (Q, CY + 2, ROWS, X)
    to_pair, to_next = call(
        pack_z_kernel, "pack_z", [VMEM], [VMEM] * 2, [((Q * 8, X), f32)] * 2
    )(flat)
    pairs = [(i, i ^ 1) for i in range(gz)]
    nexts = [(i, (i - 1) % gz if i % 2 == 0 else (i + 1) % gz) for i in range(gz)]
    from_pair = lax.ppermute(to_pair, "gz", pairs)
    from_next = lax.ppermute(to_next, "gz", nexts)
    s0, w, pick = call(
        prepare_kernel, "prepare", [VMEM] * 4, [VMEM] * 3,
        [(pad, f32), ((QP * 8, QP * 8), f32), ((CAP, devices), jnp.int32)],
    )(flat, collision, link_cell[0].T, link_dir[0].T)
    s0, s1, to_low, to_high = call(
        edge_rows_kernel, "edge_rows", [VMEM] * 4, [VMEM] * 4,
        [(pad, f32), (pad, f32), ((Y_ROWS, X), f32), ((Y_ROWS, X), f32)],
        aliases={0: 0},
    )(s0, w, from_pair, from_next)
    from_high = lax.ppermute(to_low, "gy", [(i, (i - 1) % gy) for i in range(gy)])
    from_low = lax.ppermute(to_high, "gy", [(i, (i + 1) % gy) for i in range(gy)])
    s1, beyond, out = call(
        inner_rows_kernel, "inner_rows", [VMEM] * 3, [VMEM, VMEM, ANY],
        [(pad, f32), ((10 * CZ, X), f32), ((Q, CY, CZ, X), f32)],
        scratch=[pltpu.VMEM((Q, CY - 4, CZ, X), f32), pltpu.SemaphoreType.DMA],
        aliases={2: 0},
    )(s0, w, s1)
    _, rows, out = call(
        outer_rows_kernel, "outer_rows", [VMEM] * 6 + [SMEM, ANY], [VMEM, VMEM, ANY],
        [(pad, f32), ((devices * (CAP + 1), 1, X), f32), ((Q, CY, CZ, X), f32)],
        scratch=[
            pltpu.VMEM((Q, 4, CZ, X), f32),
            pltpu.VMEM((Q, 4, CZ, X), f32),
            pltpu.VMEM((Q * CY * CZ, X), f32),
            pltpu.VMEM((5 * 8, X), f32),
            pltpu.VMEM((devices, X), f32),
            pltpu.SemaphoreType.DMA,
            pltpu.SemaphoreType.DMA((2,)),
        ],
        aliases={0: 0, 7: 2},
    )(s1, w, beyond, from_high, from_low, link_panel[0].T, pick, out)
    arrived = lax.all_to_all(
        rows.reshape(devices, CAP + 1, 1, X), ("gy", "gz"), split_axis=0, concat_axis=0, tiled=True
    )
    (panel_sens,) = call(sum_kernel, "sum_rows", [VMEM], [VMEM], [((P_DEV, X), f32)])(
        arrived.reshape(devices * (CAP + 1), X)
    )
    return out, panel_sens


def solution(mesh):
    placed = (
        P(None, "gy", "gz", None),
        P(),
        P(("gy", "gz"), None, None),
        P(("gy", "gz"), None, None),
        P(("gy", "gz"), None, None),
    )
    return jax.shard_map(
        on_device,
        mesh=mesh,
        in_specs=placed,
        out_specs=(P(None, "gy", "gz", None), P(("gy", "gz"), None)),
        check_vma=False,
    )
```

profile of v0, /device:TPU:1, one launch (start us, length us, event | category | flops | bytes accessed | tf_op | source)
XLA Modules:
  0.0 48.4 jit_solution(8952238834391133903)
XLA Ops:
  0.6 0.0 copy-start
  0.6 1.7 %copy-done = f32[19,8,32,128]{3,2,1,0:T(8,128)S(1)} copy-done((f32[19,8,32,128]{3,2,1,0:T(8,128)S(1)}, f32[19,8,32,128]{3,2,1,0:T(8,128)}, u32[]{:S(2)}) %copy-start) | copy-done | bytes 2490392
  2.3 0.1 pack_z.1
  2.4 1.5 %collective-permute-start = (f32[152,128]{1,0:T(8,128)S(1)}, f32[152,128]{1,0:T(8,128)S(1)}, u32[]{:S(2)}, u32[]{:S(2)}) collective-permute-start(f32[152,128]{1,0:T(8,128)S(1)} %get-tuple-element.18), channel_id=1, source_target_pairs={{0,1},{1,0},{2,3},{3,2},{4,5},{5,4},{6,7},{7,6},{8,9},{9,8},{10,11... | collective-permute-start | bytes 233480 | tf_op jit(solution)/shard_map/ppermute | solution.py:365
  3.9 1.7 %collective-permute-start.1 = (f32[152,128]{1,0:T(8,128)S(1)}, f32[152,128]{1,0:T(8,128)S(1)}, u32[]{:S(2)}, u32[]{:S(2)}) collective-permute-start(f32[152,128]{1,0:T(8,128)S(1)} %get-tuple-element.19), channel_id=1, source_target_pairs={{0,7},{1,2},{2,1},{3,4},{4,3},{5,6},{6,5},{7,0},{8,15},{9,10},{10,... | collective-permute-start | bytes 233480 | tf_op jit(solution)/shard_map/ppermute | solution.py:366
  5.6 0.0 copy-start.1
  5.6 0.7 %copy-done.1 = f32[19,19]{1,0:T(8,128)S(1)} copy-done((f32[19,19]{1,0:T(8,128)S(1)}, f32[19,19]{1,0:T(8,128)}, u32[]{:S(2)}) %copy-start.1) | copy-done | bytes 1468
  6.3 0.0 copy-start.2
  6.3 0.7 %copy-done.2 = s32[1,128,8]{1,2,0:T(8,128)S(1)} copy-done((s32[1,128,8]{1,2,0:T(8,128)S(1)}, s32[1,128,8]{1,2,0:T(8,128)}, u32[]{:S(2)}) %copy-start.2) | copy-done | bytes 4120
  7.0 0.0 copy-start.3
  7.0 0.7 %copy-done.3 = s32[1,128,8]{1,2,0:T(8,128)S(1)} copy-done((s32[1,128,8]{1,2,0:T(8,128)S(1)}, s32[1,128,8]{1,2,0:T(8,128)}, u32[]{:S(2)}) %copy-start.3) | copy-done | bytes 4120
  7.7 0.6 %prepare.1 = (f32[19,10,48,128]{3,2,1,0:T(8,128)S(1)}, f32[160,160]{1,0:T(8,128)S(1)}, s32[8,128]{1,0:T(8,128)S(1)}) custom-call(f32[19,256,128]{2,1,0:T(8,128)S(1)} %bitcast.13, f32[19,19]{1,0:T(8,128)S(1)} %copy-done.1, s32[8,128]{1,0:T(8,128)S(1)} %bitcast.16, s32[8,128]{1,0:T(8,128)S(1)} %bitcast.17), custom_call_target="tpu_custom_call" | custom-call | tf_op jit(solution)/shard_map/prepare/pallas_call | solution.py:367
  8.3 0.0 collective-permute-done.from_pair
  8.4 0.0 collective-permute-done.1.from_next
  8.4 0.7 %edge_rows.1 = (f32[19,10,48,128]{3,2,1,0:T(8,128)S(1)}, f32[19,10,48,128]{3,2,1,0:T(8,128)S(1)}, f32[336,128]{1,0:T(8,128)S(1)}, f32[336,128]{1,0:T(8,128)S(1)}) custom-call(f32[19,10,48,128]{3,2,1,0:T(8,128)S(1)} %get-tuple-element.16.s0_in, f32[160,160]{1,0:T(8,128)S(1)} %get-tuple-element.17.w, ...), custom_call_target="tpu_custom_call", output_to_operand_aliasing={{0}: (0, {})} | custom-call | tf_op jit(solution)/shard_map/edge_rows/pallas_call | solution.py:371
  9.1 5.0 %collective-permute-start.2 = (f32[336,128]{1,0:T(8,128)S(1)}, f32[336,128]{1,0:T(8,128)S(1)}, u32[]{:S(2)}, u32[]{:S(2)}) collective-permute-start(f32[336,128]{1,0:T(8,128)S(1)} %get-tuple-element.24), channel_id=1, source_target_pairs={{0,120},{8,0},{16,8},{24,16},{32,24},{40,32},{48,40},{56,48},{64,5... | collective-permute-start | bytes 516104 | tf_op jit(solution)/shard_map/ppermute | solution.py:376
  14.1 0.0 collective-permute-start.3
  14.1 0.0 copy-start.4
  14.1 4.9 %inner_rows.1 = (f32[19,10,48,128]{3,2,1,0:T(8,128)S(1)}, f32[320,128]{1,0:T(8,128)S(1)}, f32[19,8,32,128]{3,2,1,0:T(8,128)}) custom-call(f32[19,10,48,128]{3,2,1,0:T(8,128)S(1)} %get-tuple-element.20.s0, f32[160,160]{1,0:T(8,128)S(1)} %get-tuple-element.17.w, f32[19,10,48,128]{3,2,1,0:T(8,128)S(1)} %get-tuple-element.21.s1_in), custom_call_target="tpu_custom_call", output_to_operand_aliasing={{0}: (2, {})} | custom-call | tf_op jit(solution)/shard_map/inner_rows/pallas_call | solution.py:378
  19.0 0.0 collective-permute-done.2.from_high
  19.0 2.7 %collective-permute-done.3.from_low = f32[336,128]{1,0:T(8,128)S(1)} collective-permute-done((f32[336,128]{1,0:T(8,128)S(1)}, f32[336,128]{1,0:T(8,128)S(1)}, u32[]{:S(2)}, u32[]{:S(2)}) %collective-permute-start.3) | collective-permute-done | bytes 172064 | tf_op jit(solution)/shard_map/ppermute | solution.py:377
  21.7 0.0 copy-done.4
  21.7 4.1 %outer_rows.1 = (f32[19,10,48,128]{3,2,1,0:T(8,128)S(1)}, f32[1152,1,128]{2,1,0:T(1,128)S(1)}, f32[19,8,32,128]{3,2,1,0:T(8,128)}) custom-call(f32[19,10,48,128]{3,2,1,0:T(8,128)S(1)} %get-tuple-element.22.s1_in, f32[160,160]{1,0:T(8,128)S(1)} %get-tuple-element.17.w, ...), custom_call_target="tpu_custom_call", output_to_operand_aliasing={{0}: (0, {}), {2}: (7, {})} | custom-call | tf_op jit(solution)/shard_map/outer_rows/pallas_call | solution.py:384
  25.8 21.7 %all_to_all.5 = f32[128,9,1,128]{3,2,1,0:T(1,128)S(1)} all-to-all(f32[128,9,1,128]{3,2,1,0:T(1,128)S(1)} %bitcast.15), channel_id=1, replica_groups=mesh['gy'=16,'gz'=8] {'gy','gz'}, dimensions={0} | all-to-all | bytes 1179648 | tf_op jit(solution)/shard_map/all_to_all | solution.py:398
  47.5 0.9 %sum_rows.1 = f32[64,128]{1,0:T(8,128)} custom-call(f32[1152,128]{1,0:T(8,128)S(1)} %bitcast.14), custom_call_target="tpu_custom_call" | custom-call | tf_op jit(solution)/shard_map/sum_rows/pallas_call | solution.py:401
Async XLA Ops:
  0.6 1.7 %copy-start = (f32[19,8,32,128]{3,2,1,0:T(8,128)S(1)}, f32[19,8,32,128]{3,2,1,0:T(8,128)}, u32[]{:S(2)}) copy-start(f32[19,8,32,128]{3,2,1,0:T(8,128)} %param.5) | copy-start | bytes 7471108
  2.4 5.9 %collective-permute-start = (f32[152,128]{1,0:T(8,128)S(1)}, f32[152,128]{1,0:T(8,128)S(1)}, u32[]{:S(2)}, u32[]{:S(2)}) collective-permute-start(f32[152,128]{1,0:T(8,128)S(1)} %get-tuple-element.18), channel_id=1, source_target_pairs={{0,1},{1,0},{2,3},{3,2},{4,5},{5,4},{6,7},{7,6},{8,9},{9,8},{10,11... | collective-permute-start | bytes 233480 | tf_op jit(solution)/shard_map/ppermute | solution.py:365
  3.9 4.4 %collective-permute-start.1 = (f32[152,128]{1,0:T(8,128)S(1)}, f32[152,128]{1,0:T(8,128)S(1)}, u32[]{:S(2)}, u32[]{:S(2)}) collective-permute-start(f32[152,128]{1,0:T(8,128)S(1)} %get-tuple-element.19), channel_id=1, source_target_pairs={{0,7},{1,2},{2,1},{3,4},{4,3},{5,6},{6,5},{7,0},{8,15},{9,10},{10,... | collective-permute-start | bytes 233480 | tf_op jit(solution)/shard_map/ppermute | solution.py:366
  5.6 0.7 %copy-start.1 = (f32[19,19]{1,0:T(8,128)S(1)}, f32[19,19]{1,0:T(8,128)}, u32[]{:S(2)}) copy-start(f32[19,19]{1,0:T(8,128)} %collision.1) | copy-start | bytes 4336
  6.3 0.7 %copy-start.2 = (s32[1,128,8]{1,2,0:T(8,128)S(1)}, s32[1,128,8]{1,2,0:T(8,128)}, u32[]{:S(2)}) copy-start(s32[1,128,8]{1,2,0:T(8,128)} %param.7) | copy-start | bytes 12292
  7.0 0.7 %copy-start.3 = (s32[1,128,8]{1,2,0:T(8,128)S(1)}, s32[1,128,8]{1,2,0:T(8,128)}, u32[]{:S(2)}) copy-start(s32[1,128,8]{1,2,0:T(8,128)} %param.8) | copy-start | bytes 12292
  9.1 9.9 %collective-permute-start.2 = (f32[336,128]{1,0:T(8,128)S(1)}, f32[336,128]{1,0:T(8,128)S(1)}, u32[]{:S(2)}, u32[]{:S(2)}) collective-permute-start(f32[336,128]{1,0:T(8,128)S(1)} %get-tuple-element.24), channel_id=1, source_target_pairs={{0,120},{8,0},{16,8},{24,16},{32,24},{40,32},{48,40},{56,48},{64,5... | collective-permute-start | bytes 516104 | tf_op jit(solution)/shard_map/ppermute | solution.py:376
  14.1 7.6 %collective-permute-start.3 = (f32[336,128]{1,0:T(8,128)S(1)}, f32[336,128]{1,0:T(8,128)S(1)}, u32[]{:S(2)}, u32[]{:S(2)}) collective-permute-start(f32[336,128]{1,0:T(8,128)S(1)} %get-tuple-element.25), channel_id=1, source_target_pairs={{0,8},{8,16},{16,24},{24,32},{32,40},{40,48},{48,56},{56,64},{64,7... | collective-permute-start | bytes 516104 | tf_op jit(solution)/shard_map/ppermute | solution.py:377
  14.1 7.6 %copy-start.4 = (s32[1,128,8]{1,2,0:T(8,128)S(1)}, s32[1,128,8]{1,2,0:T(8,128)}, u32[]{:S(2)}) copy-start(s32[1,128,8]{1,2,0:T(8,128)} %param.9) | copy-start | bytes 12292
where the time goes:
time: 48.7 us; the launch traced here: 48.4 us
  blocking collectives  21.7 us (45%)
  Pallas kernels  11.3 us (23%)
  starting transfers between devices  8.2 us (17%)
  local copies, waits for them, and re-layouts  3.78 us (8%)
  waiting for transfers between devices  2.7 us (6%)
  between operations  0.7 us (1%)
    all_to_all x1, blocking collectives, on_device(): lax.all_to_all(rows.reshape(devices, CAP + 1, 1, X), ('gy', 'gz'), split_...  21.7 us
    ppermute x1, starting transfers between devices, on_device(): lax.ppermute(to_low, 'gy', [(i, (i - 1) % gy) for i in range(gy)])  5 us
    pallas_call x1, Pallas kernels, on_device(): call(inner_rows_kernel, 'inner_rows', [VMEM] * 3, [VMEM, VMEM, ANY], [(pa...  4.86 us
    pallas_call x1, Pallas kernels, on_device(): call(outer_rows_kernel, 'outer_rows', [VMEM] * 6 + [SMEM, ANY], [VMEM, VM...  4.13 us
    unnamed x10, local copies, waits for them, and re-layouts  3.78 us
    ppermute x1, waiting for transfers between devices, on_device(): lax.ppermute(to_high, 'gy', [(i, (i + 1) % gy) for i in range(gy)])  2.69 us
    ppermute x1, starting transfers between devices, on_device(): from_next = lax.ppermute(to_next, 'gz', nexts)  1.7 us
    ppermute x1, starting transfers between devices, on_device(): from_pair = lax.ppermute(to_pair, 'gz', pairs)  1.5 us
  transfers between devices with their start and end apart: 4, of which 1 were waited for; matrix products, arithmetic and copies ran while one was open for 0% of the time, Pallas kernels for 11%

commit v1 on v0

--- a/solution.py
+++ b/solution.py
@@ -125,7 +125,7 @@
         to_next[8 * i : 8 * i + 8, :] = jnp.where(even, low, high)
 
 
-def prepare_kernel(field, collision, cell, direction, s0, w, pick):
+def prepare_kernel(field, s0):
     for q in range(Q):
         for y in range(CY):
             s0[q, 1 + y, Z0 : Z0 + CZ, :] = along_x(field[q, CZ * y : CZ * y + CZ, :], q)
@@ -134,28 +134,30 @@
         s0[q, 0, :, :] = zero
     for q in Y_UP:
         s0[q, CY + 1, :, :] = zero
+
+
+def spread_weights(collision):
     n = QP * 8
     spread = (
         lax.broadcasted_iota(jnp.int32, (n, Q), 0) // 8 == lax.broadcasted_iota(jnp.int32, (n, Q), 1)
-    ).astype(f32)
-    turned = lax.dot_general(
-        spread, collision[...], (((1,), (1,)), ((), ())),
-        precision=lax.Precision.HIGHEST, preferred_element_type=f32,
-    )
-    wide = lax.dot_general(
-        turned, spread, (((1,), (1,)), ((), ())),
-        precision=lax.Precision.HIGHEST, preferred_element_type=f32,
-    )
+    ).astype(f32).astype(bf16)
     same = (
         lax.broadcasted_iota(jnp.int32, (n, n), 0) % 8
         == lax.broadcasted_iota(jnp.int32, (n, n), 1) % 8
     )
-    w[...] = jnp.where(same, wide, 0.0)
-    pick[...] = direction[...] * (CY * CZ) + cell[...]
-
-
-def edge_rows_kernel(s0_in, w, from_pair, from_next, s0, s1, to_low, to_high):
+    dims = (((1,), (1,)), ((), ()))
+    total = 0.0
+    for part in split(collision):
+        turned = lax.dot_general(spread, part, dims, preferred_element_type=f32).astype(bf16)
+        total += lax.dot_general(turned, spread, dims, preferred_element_type=f32)
+    return jnp.where(same, total, 0.0)
+
+
+def edge_rows_kernel(
+    s0_in, collision, from_pair, from_next, s0, s1, to_low, to_high, w
+):
     del s0_in
+    w[...] = spread_weights(collision[...])
     iz = lax.axis_index("gz")
     even = lax.rem(iz, 2) == 0
     above = iz < lax.axis_size("gz") - 1
@@ -198,26 +200,29 @@
             )
 
 
-def inner_rows_kernel(s0, w, s1_in, s1, beyond, out, kept, sem):
+def inner_rows_kernel(
+    s0, w, s1_in, panel, cell, direction, s1, beyond, out, scaled, numbers, pick, kept, sem
+):
     del s1_in
     iz = lax.axis_index("gz")
     above = iz < lax.axis_size("gz") - 1
     below = iz > 0
     weights = split(w[...])
-
-    @pl.loop(1, CY - 1)
-    def _(y):
+    for y in range(1, CY - 1):
         store_line(s1, y, mix(weights, read_row(s0, y)))
-
-    @pl.loop(2, CY - 2)
-    def _(y):
+    for y in range(2, CY - 2):
         mixed = mix(weights, read_row(s1, y))
         for q in range(Q):
             for t in range(CZ // 8):
-                kept[q, y - 2, 8 * t : 8 * t + 8, :] = mixed[8 * q : 8 * q + 8, X * t : X * t + X]
-
+                value = mixed[8 * q : 8 * q + 8, X * t : X * t + X]
+                kept[q, y - 2, 8 * t : 8 * t + 8, :] = value
+                at = q * (CY * CZ) + y * CZ + 8 * t
+                scaled[at : at + 8, :] = value * LINK_WEIGHTS[q]
     copy = pltpu.make_async_copy(kept, out.at[:, pl.ds(2, CY - 4), :, :], sem)
     copy.start()
+    numbers[...] = jnp.zeros((numbers.shape[0], X), f32)
+    numbers[:, 0:CAP] = panel[...].astype(f32).T
+    pick[...] = direction[...] * (CY * CZ) + cell[...]
     for side, (y, channels, sources) in enumerate(((CY - 1, Y_UP, Y_DOWN), (0, Y_DOWN, Y_UP))):
         for shift in (0, 1, -1):
             wanted = [q for q in channels if DIRS[q][2] == shift]
@@ -245,30 +250,28 @@
 
 
 def outer_rows_kernel(
-    s1_in, w, beyond, from_high, from_low, panel, pick, out_in,
-    s1, rows, out, kept, inner, scaled, ends, numbers, in_sem, out_sem,
+    s1_in, w, beyond, from_high, from_low, pick_in, numbers, scaled_in, out_in,
+    s1, scaled, rows, out, kept, ends, pick, pick_sem, out_sem,
 ):
-    del s1_in
+    del s1_in, scaled_in, out_in
+    fetch = pltpu.make_async_copy(pick_in, pick, pick_sem)
+    fetch.start()
     iy = lax.axis_index("gy")
     iz = lax.axis_index("gz")
-    fetch = pltpu.make_async_copy(out_in.at[:, pl.ds(2, CY - 4), :, :], inner, in_sem)
-    fetch.start()
     weights = split(w[...])
-    numbers[...] = jnp.zeros((128, X), f32)
-    numbers[:, 0:CAP] = panel[...].astype(f32).T
     z_ok = (iz > 0, iz < lax.axis_size("gz") - 1)
     sides = (
         (0, CY - 1, CY, Y_UP, from_high, iy < lax.axis_size("gy") - 1),
         (1, 0, -1, Y_DOWN, from_low, iy > 0),
     )
     for side, y, halo, channels, arrived, valid in sides:
-        ends[...] = jnp.zeros((5 * 8, X), f32)
+        ends[side, :, :] = jnp.zeros((5 * 8, X), f32)
         for i in range(5):
-            ends[8 * i : 8 * i + 2, :] = arrived[ENDS + 2 * i : ENDS + 2 * i + 2, :]
+            ends[side, 8 * i : 8 * i + 2, :] = arrived[ENDS + 2 * i : ENDS + 2 * i + 2, :]
         tiles = [None] * (Q + 1)
         for i, p in enumerate(channels):
             tiles[p] = line_tiles(arrived[RAW + CZ * i : RAW + CZ * i + CZ, :]) + [
-                ends[8 * i : 8 * i + 8, :]
+                ends[side, 8 * i : 8 * i + 8, :]
             ]
         mixed = mix(weights, jnp.where(valid, stacked(tiles), 0.0))
         for q in range(Q):
@@ -286,6 +289,12 @@
             line = line + arrived[MIXED + CZ * i : MIXED + CZ * i + CZ, :]
             s1[q, 1 + halo, pl.ds(Z0 + DIRS[q][2], CZ), :] = jnp.where(valid, line, 0.0)
 
+    copies = [
+        pltpu.make_async_copy(
+            kept.at[:, pl.ds(2 * h, 2), :, :], out.at[:, pl.ds(6 * h, 2), :, :], out_sem.at[h]
+        )
+        for h in range(2)
+    ]
     for k, y in enumerate((0, 1, CY - 2, CY - 1)):
         mixed = mix(weights, read_row(s1, y))
         for q in range(Q):
@@ -294,21 +303,11 @@
                 kept[q, k, 8 * t : 8 * t + 8, :] = value
                 at = q * (CY * CZ) + y * CZ + 8 * t
                 scaled[at : at + 8, :] = value * LINK_WEIGHTS[q]
-    copies = [
-        pltpu.make_async_copy(
-            kept.at[:, pl.ds(2 * h, 2), :, :], out.at[:, pl.ds(6 * h, 2), :, :], out_sem.at[h]
-        )
-        for h in range(2)
-    ]
-    for copy in copies:
-        copy.start()
+        if k % 2:
+            copies[k // 2].start()
     fetch.wait()
-    for q in range(Q):
-        for y in range(2, CY - 2):
-            at = q * (CY * CZ) + y * CZ
-            scaled[at : at + CZ, :] = inner[q, y - 2, :, :] * LINK_WEIGHTS[q]
-
-    @pl.loop(0, 128, unroll=4)
+
+    @pl.loop(0, numbers.shape[0], unroll=4)
     def _(d):
         for k in range(CAP):
             rows[pl.ds(d * (CAP + 1) + k, 1), 0, :] = scaled[pl.ds(pick[k, d], 1), :]
@@ -333,9 +332,8 @@
 
 
 VMEM = pl.BlockSpec(memory_space=pltpu.VMEM)
-SMEM = pl.BlockSpec(memory_space=pltpu.SMEM)
-ANY = pl.BlockSpec(memory_space=pl.ANY)
-LIMIT = 32 * 1024 * 1024
+HBM = pl.BlockSpec(memory_space=pltpu.HBM)
+MIB = 1024 * 1024
 
 
 def call(kernel, name, ins, outs, shapes, scratch=(), aliases=None):
@@ -346,7 +344,7 @@
         out_specs=outs,
         scratch_shapes=list(scratch),
         input_output_aliases=aliases or {},
-        compiler_params=pltpu.CompilerParams(vmem_limit_bytes=LIMIT),
+        compiler_params=pltpu.CompilerParams(vmem_limit_bytes=32 * MIB),
         name=name,
     )
 
@@ -354,9 +352,11 @@
 def on_device(adjoint, collision, link_cell, link_dir, link_panel):
     gz = lax.axis_size("gz")
     gy = lax.axis_size("gy")
-    devices = gy * gz
+    devices = link_cell.shape[1]
+    pad = (Q, CY + 2, ROWS, X)
+    own = (Q, CY, CZ, X)
     flat = adjoint.reshape(Q, CY * CZ, X)
-    pad = (Q, CY + 2, ROWS, X)
+    dma = pltpu.SemaphoreType.DMA
     to_pair, to_next = call(
         pack_z_kernel, "pack_z", [VMEM], [VMEM] * 2, [((Q * 8, X), f32)] * 2
     )(flat)
@@ -364,37 +364,44 @@
     nexts = [(i, (i - 1) % gz if i % 2 == 0 else (i + 1) % gz) for i in range(gz)]
     from_pair = lax.ppermute(to_pair, "gz", pairs)
     from_next = lax.ppermute(to_next, "gz", nexts)
-    s0, w, pick = call(
-        prepare_kernel, "prepare", [VMEM] * 4, [VMEM] * 3,
-        [(pad, f32), ((QP * 8, QP * 8), f32), ((CAP, devices), jnp.int32)],
-    )(flat, collision, link_cell[0].T, link_dir[0].T)
-    s0, s1, to_low, to_high = call(
-        edge_rows_kernel, "edge_rows", [VMEM] * 4, [VMEM] * 4,
-        [(pad, f32), (pad, f32), ((Y_ROWS, X), f32), ((Y_ROWS, X), f32)],
+    (s0,) = call(prepare_kernel, "prepare", [VMEM], [VMEM], [(pad, f32)])(flat)
+    s0, s1, to_low, to_high, w = call(
+        edge_rows_kernel, "edge_rows", [VMEM] * 4, [VMEM] * 5,
+        [(pad, f32), (pad, f32), ((Y_ROWS, X), f32), ((Y_ROWS, X), f32), ((QP * 8, QP * 8), f32)],
         aliases={0: 0},
-    )(s0, w, from_pair, from_next)
+    )(s0, collision, from_pair, from_next)
     from_high = lax.ppermute(to_low, "gy", [(i, (i - 1) % gy) for i in range(gy)])
     from_low = lax.ppermute(to_high, "gy", [(i, (i + 1) % gy) for i in range(gy)])
-    s1, beyond, out = call(
-        inner_rows_kernel, "inner_rows", [VMEM] * 3, [VMEM, VMEM, ANY],
-        [(pad, f32), ((10 * CZ, X), f32), ((Q, CY, CZ, X), f32)],
-        scratch=[pltpu.VMEM((Q, CY - 4, CZ, X), f32), pltpu.SemaphoreType.DMA],
+    s1, beyond, out, scaled, numbers, pick = call(
+        inner_rows_kernel, "inner_rows", [VMEM] * 6, [VMEM, VMEM, HBM, VMEM, VMEM, VMEM],
+        [
+            (pad, f32),
+            ((10 * CZ, X), f32),
+            (own, f32),
+            ((Q * CY * CZ, X), f32),
+            ((devices, X), f32),
+            ((CAP, devices), jnp.int32),
+        ],
+        scratch=[pltpu.VMEM((Q, CY - 4, CZ, X), f32), dma],
         aliases={2: 0},
-    )(s0, w, s1)
-    _, rows, out = call(
-        outer_rows_kernel, "outer_rows", [VMEM] * 6 + [SMEM, ANY], [VMEM, VMEM, ANY],
-        [(pad, f32), ((devices * (CAP + 1), 1, X), f32), ((Q, CY, CZ, X), f32)],
+    )(s0, w, s1, link_panel[0].T, link_cell[0].T, link_dir[0].T)
+    _, _, rows, out = call(
+        outer_rows_kernel, "outer_rows", [VMEM] * 8 + [HBM], [VMEM] * 3 + [HBM],
+        [
+            (pad, f32),
+            ((Q * CY * CZ, X), f32),
+            ((devices * (CAP + 1), 1, X), f32),
+            (own, f32),
+        ],
         scratch=[
             pltpu.VMEM((Q, 4, CZ, X), f32),
-            pltpu.VMEM((Q, 4, CZ, X), f32),
-            pltpu.VMEM((Q * CY * CZ, X), f32),
-            pltpu.VMEM((5 * 8, X), f32),
-            pltpu.VMEM((devices, X), f32),
-            pltpu.SemaphoreType.DMA,
-            pltpu.SemaphoreType.DMA((2,)),
+            pltpu.VMEM((2, 5 * 8, X), f32),
+            pltpu.SMEM((CAP, devices), jnp.int32),
+            dma,
+            dma((2,)),
         ],
-        aliases={0: 0, 7: 2},
-    )(s1, w, beyond, from_high, from_low, link_panel[0].T, pick, out)
+        aliases={0: 0, 7: 1, 8: 3},
+    )(s1, w, beyond, from_high, from_low, pick, numbers, scaled, out)
     arrived = lax.all_to_all(
         rows.reshape(devices, CAP + 1, 1, X), ("gy", "gz"), split_axis=0, concat_axis=0, tiled=True
     )

time: 48.7 us -> 47.8 us (0.982)
  waiting for transfers between devices: 2.7 us -> 6.44 us
  Pallas kernels: 11.3 us -> 8.28 us
  local copies, waits for them, and re-layouts: 3.78 us -> 1.71 us
  blocking collectives: 21.7 us -> 22.2 us
    pallas_call x4, Pallas kernels: 10.3 us -> 7.29 us  [the longest x1 3.19 us: on_device(): call(outer_rows_kernel, 'outer_rows', [VMEM] * 8 + [HBM], [VMEM] * 3 + [H...]
    ppermute x1, waiting for transfers between devices: 2.69 us -> 4.77 us  [on_device(): lax.ppermute(to_high, 'gy', [(i, (i + 1) % gy) for i in range(gy)])]
    unnamed x10, local copies, waits for them, and re-layouts: 3.78 us -> 1.71 us
    ppermute x1, waiting for transfers between devices: 0.01 us -> 1.66 us  [on_device(): from_next = lax.ppermute(to_next, 'gz', nexts)]
    all_to_all x1, blocking collectives: 21.7 us -> 22.2 us  [on_device(): lax.all_to_all(rows.reshape(devices, CAP + 1, 1, X), ('gy', 'gz'), split_...]
  transfers between devices with their start and end apart: 4 -> 4, of which waited for: 1 -> 2; matrix products, arithmetic and copies ran while one was open for 0% -> 0% of each run, Pallas kernels for 11% -> 7%
where the time goes in v1:
time: 47.8 us; the launch traced here: 47.7 us
  blocking collectives  22.2 us (46%)
  starting transfers between devices  8.31 us (17%)
  Pallas kernels  8.28 us (17%)
  waiting for transfers between devices  6.44 us (13%)
  local copies, waits for them, and re-layouts  1.71 us (4%)
  between operations  0.7 us (1%)
    all_to_all x1, blocking collectives, on_device(): lax.all_to_all(rows.reshape(devices, CAP + 1, 1, X), ('gy', 'gz'), split_...  22.2 us
    ppermute x1, starting transfers between devices, on_device(): lax.ppermute(to_low, 'gy', [(i, (i - 1) % gy) for i in range(gy)])  5.08 us
    ppermute x1, waiting for transfers between devices, on_device(): lax.ppermute(to_high, 'gy', [(i, (i + 1) % gy) for i in range(gy)])  4.77 us
    pallas_call x1, Pallas kernels, on_device(): call(outer_rows_kernel, 'outer_rows', [VMEM] * 8 + [HBM], [VMEM] * 3 + [H...  3.19 us
    pallas_call x1, Pallas kernels, on_device(): call(inner_rows_kernel, 'inner_rows', [VMEM] * 6, [VMEM, VMEM, HBM, VMEM,...  2.77 us
    ppermute x1, starting transfers between devices, on_device(): from_next = lax.ppermute(to_next, 'gz', nexts)  1.73 us
    unnamed x10, local copies, waits for them, and re-layouts  1.71 us
    ppermute x1, waiting for transfers between devices, on_device(): from_next = lax.ppermute(to_next, 'gz', nexts)  1.66 us
  transfers between devices with their start and end apart: 4, of which 2 were waited for; matrix products, arithmetic and copies ran while one was open for 0% of the time, Pallas kernels for 7%

profile of v1, /device:TPU:1, one launch (start us, length us, event | category | flops | bytes accessed | tf_op | source)
XLA Modules:
  0.0 47.7 jit_solution(7741838842169532407)
XLA Ops:
  0.6 0.0 copy-start
  0.6 1.7 %copy-done = f32[19,8,32,128]{3,2,1,0:T(8,128)S(1)} copy-done((f32[19,8,32,128]{3,2,1,0:T(8,128)S(1)}, f32[19,8,32,128]{3,2,1,0:T(8,128)}, u32[]{:S(2)}) %copy-start) | copy-done | bytes 2490392
  2.3 0.0 copy-start.1
  2.3 0.1 pack_z.1
  2.4 1.5 %collective-permute-start = (f32[152,128]{1,0:T(8,128)S(1)}, f32[152,128]{1,0:T(8,128)S(1)}, u32[]{:S(2)}, u32[]{:S(2)}) collective-permute-start(f32[152,128]{1,0:T(8,128)S(1)} %get-tuple-element.17), channel_id=1, source_target_pairs={{0,1},{1,0},{2,3},{3,2},{4,5},{5,4},{6,7},{7,6},{8,9},{9,8},{10,11... | collective-permute-start | bytes 233480 | tf_op jit(solution)/shard_map/ppermute | solution.py:365
  3.9 0.0 copy-start.2
  3.9 0.0 copy-start.3
  3.9 0.0 copy-start.4
  3.9 1.7 %collective-permute-start.1 = (f32[152,128]{1,0:T(8,128)S(1)}, f32[152,128]{1,0:T(8,128)S(1)}, u32[]{:S(2)}, u32[]{:S(2)}) collective-permute-start(f32[152,128]{1,0:T(8,128)S(1)} %get-tuple-element.18), channel_id=1, source_target_pairs={{0,7},{1,2},{2,1},{3,4},{4,3},{5,6},{6,5},{7,0},{8,15},{9,10},{10,... | collective-permute-start | bytes 233480 | tf_op jit(solution)/shard_map/ppermute | solution.py:366
  5.7 0.4 prepare.1.s0_in
  6.1 0.0 collective-permute-done.from_pair
  6.1 1.7 %collective-permute-done.1.from_next = f32[152,128]{1,0:T(8,128)S(1)} collective-permute-done((f32[152,128]{1,0:T(8,128)S(1)}, f32[152,128]{1,0:T(8,128)S(1)}, u32[]{:S(2)}, u32[]{:S(2)}) %collective-permute-start.1) | collective-permute-done | bytes 77856 | tf_op jit(solution)/shard_map/ppermute | solution.py:366
  7.8 0.0 copy-done.1
  7.8 0.9 %edge_rows.1 = (f32[19,10,48,128]{3,2,1,0:T(8,128)S(1)}, f32[19,10,48,128]{3,2,1,0:T(8,128)S(1)}, f32[336,128]{1,0:T(8,128)S(1)}, f32[336,128]{1,0:T(8,128)S(1)}, f32[160,160]{1,0:T(8,128)S(1)}) custom-call(f32[19,10,48,128]{3,2,1,0:T(8,128)S(1)} %prepare.1.s0_in, f32[19,19]{1,0:T(8,128)S(1)} %copy-done.1, ...), custom_call_target="tpu_custom_call", output_to_operand_aliasing={{0}: (0, {})} | custom-call | tf_op jit(solution)/shard_map/edge_rows/pallas_call | solution.py:368
  8.7 5.1 %collective-permute-start.2 = (f32[336,128]{1,0:T(8,128)S(1)}, f32[336,128]{1,0:T(8,128)S(1)}, u32[]{:S(2)}, u32[]{:S(2)}) collective-permute-start(f32[336,128]{1,0:T(8,128)S(1)} %get-tuple-element.24), channel_id=1, source_target_pairs={{0,120},{8,0},{16,8},{24,16},{32,24},{40,32},{48,40},{56,48},{64,5... | collective-permute-start | bytes 516104 | tf_op jit(solution)/shard_map/ppermute | solution.py:373
  13.8 0.0 collective-permute-start.3
  13.8 0.0 copy-done.2
  13.8 0.0 copy-done.3
  13.8 0.0 copy-done.4
  13.8 2.8 %inner_rows.1 = (f32[19,10,48,128]{3,2,1,0:T(8,128)S(1)}, f32[320,128]{1,0:T(8,128)S(1)}, f32[19,8,32,128]{3,2,1,0:T(8,128)}, f32[4864,128]{1,0:T(8,128)S(1)}, f...) custom-call(f32[19,10,48,128]{3,2,1,0:T(8,128)S(1)} %get-tuple-element.19.s0, ...), custom_call_target="tpu_custom_call", output_to_operand_aliasing={{0}: (2, {})} | custom-call | tf_op jit(solution)/shard_map/inner_rows/pallas_call | solution.py:375
  16.6 0.0 collective-permute-done.2.from_high
  16.6 4.8 %collective-permute-done.3.from_low = f32[336,128]{1,0:T(8,128)S(1)} collective-permute-done((f32[336,128]{1,0:T(8,128)S(1)}, f32[336,128]{1,0:T(8,128)S(1)}, u32[]{:S(2)}, u32[]{:S(2)}) %collective-permute-start.3) | collective-permute-done | bytes 172064 | tf_op jit(solution)/shard_map/ppermute | solution.py:374
  21.3 3.2 %outer_rows.1 = (f32[19,10,48,128]{3,2,1,0:T(8,128)S(1)}, f32[4864,128]{1,0:T(8,128)S(1)}, f32[1152,1,128]{2,1,0:T(1,128)S(1)}, f32[19,8,32,128]{3,2,1,0:T(8,128)}) custom-call(f32[19,10,48,128]{3,2,1,0:T(8,128)S(1)} %get-tuple-element.22.s1_in, f32[160,160]{1,0:T(8,128)S(1)} %get-tuple-element.20.w, ...), custom_call_target="tpu_custom_call", output_to_operand_aliasing={{0}: (0, {}), {1}: (7, {}), {3}: (8, {})} | custom-call | tf_op jit(solution)/shard_map/outer_rows/pallas_call | solution.py:388
  24.5 22.2 %all_to_all.5 = f32[128,9,1,128]{3,2,1,0:T(1,128)S(1)} all-to-all(f32[128,9,1,128]{3,2,1,0:T(1,128)S(1)} %bitcast.15), channel_id=1, replica_groups=mesh['gy'=16,'gz'=8] {'gy','gz'}, dimensions={0} | all-to-all | bytes 1179648 | tf_op jit(solution)/shard_map/all_to_all | solution.py:405
  46.8 0.9 %sum_rows.1 = f32[64,128]{1,0:T(8,128)} custom-call(f32[1152,128]{1,0:T(8,128)S(1)} %bitcast.14), custom_call_target="tpu_custom_call" | custom-call | tf_op jit(solution)/shard_map/sum_rows/pallas_call | solution.py:408
Async XLA Ops:
  0.6 1.7 %copy-start = (f32[19,8,32,128]{3,2,1,0:T(8,128)S(1)}, f32[19,8,32,128]{3,2,1,0:T(8,128)}, u32[]{:S(2)}) copy-start(f32[19,8,32,128]{3,2,1,0:T(8,128)} %param.5) | copy-start | bytes 7471108
  2.3 5.4 %copy-start.1 = (f32[19,19]{1,0:T(8,128)S(1)}, f32[19,19]{1,0:T(8,128)}, u32[]{:S(2)}) copy-start(f32[19,19]{1,0:T(8,128)} %collision.1) | copy-start | bytes 4336
  2.4 3.7 %collective-permute-start = (f32[152,128]{1,0:T(8,128)S(1)}, f32[152,128]{1,0:T(8,128)S(1)}, u32[]{:S(2)}, u32[]{:S(2)}) collective-permute-start(f32[152,128]{1,0:T(8,128)S(1)} %get-tuple-element.17), channel_id=1, source_target_pairs={{0,1},{1,0},{2,3},{3,2},{4,5},{5,4},{6,7},{7,6},{8,9},{9,8},{10,11... | collective-permute-start | bytes 233480 | tf_op jit(solution)/shard_map/ppermute | solution.py:365
  3.9 9.8 %copy-start.2 = (s32[1,128,8]{1,2,0:T(8,128)S(1)}, s32[1,128,8]{1,2,0:T(8,128)}, u32[]{:S(2)}) copy-start(s32[1,128,8]{1,2,0:T(8,128)} %param.9) | copy-start | bytes 12292
  3.9 9.8 %copy-start.3 = (s32[1,128,8]{1,2,0:T(8,128)S(1)}, s32[1,128,8]{1,2,0:T(8,128)}, u32[]{:S(2)}) copy-start(s32[1,128,8]{1,2,0:T(8,128)} %param.7) | copy-start | bytes 12292
  3.9 9.8 %copy-start.4 = (s32[1,128,8]{1,2,0:T(8,128)S(1)}, s32[1,128,8]{1,2,0:T(8,128)}, u32[]{:S(2)}) copy-start(s32[1,128,8]{1,2,0:T(8,128)} %param.8) | copy-start | bytes 12292
  3.9 3.8 %collective-permute-start.1 = (f32[152,128]{1,0:T(8,128)S(1)}, f32[152,128]{1,0:T(8,128)S(1)}, u32[]{:S(2)}, u32[]{:S(2)}) collective-permute-start(f32[152,128]{1,0:T(8,128)S(1)} %get-tuple-element.18), channel_id=1, source_target_pairs={{0,7},{1,2},{2,1},{3,4},{4,3},{5,6},{6,5},{7,0},{8,15},{9,10},{10,... | collective-permute-start | bytes 233480 | tf_op jit(solution)/shard_map/ppermute | solution.py:366
  8.7 7.9 %collective-permute-start.2 = (f32[336,128]{1,0:T(8,128)S(1)}, f32[336,128]{1,0:T(8,128)S(1)}, u32[]{:S(2)}, u32[]{:S(2)}) collective-permute-start(f32[336,128]{1,0:T(8,128)S(1)} %get-tuple-element.24), channel_id=1, source_target_pairs={{0,120},{8,0},{16,8},{24,16},{32,24},{40,32},{48,40},{56,48},{64,5... | collective-permute-start | bytes 516104 | tf_op jit(solution)/shard_map/ppermute | solution.py:373
  13.8 7.6 %collective-permute-start.3 = (f32[336,128]{1,0:T(8,128)S(1)}, f32[336,128]{1,0:T(8,128)S(1)}, u32[]{:S(2)}, u32[]{:S(2)}) collective-permute-start(f32[336,128]{1,0:T(8,128)S(1)} %get-tuple-element.25), channel_id=1, source_target_pairs={{0,8},{8,16},{16,24},{24,32},{32,40},{40,48},{48,56},{56,64},{64,7... | collective-permute-start | bytes 516104 | tf_op jit(solution)/shard_map/ppermute | solution.py:374

commit v2 on v1

v2 whole, which is shorter than its diff:
```python
import functools

import jax
import jax.numpy as jnp
from jax import lax
from jax.experimental import pallas as pl
from jax.experimental.pallas import tpu as pltpu
from jax.sharding import PartitionSpec as P

Q = 19
QP = 20
P_DEV = 64
CAP = 8
CY = 8
CZ = 32
X = 128
ROWS = 48
Z0 = 8

DIRS = [
    (0, 0, 0),
    (1, 0, 0),
    (-1, 0, 0),
    (0, 1, 0),
    (0, -1, 0),
    (0, 0, 1),
    (0, 0, -1),
    (1, 1, 0),
    (-1, -1, 0),
    (1, -1, 0),
    (-1, 1, 0),
    (1, 0, 1),
    (-1, 0, -1),
    (1, 0, -1),
    (-1, 0, 1),
    (0, 1, 1),
    (0, -1, -1),
    (0, 1, -1),
    (0, -1, 1),
]
LINK_WEIGHTS = [2.0] + [1.0 / 3.0] * 6 + [1.0 / 6.0] * 12

Y_UP = [q for q in range(Q) if DIRS[q][1] == 1]
Y_DOWN = [q for q in range(Q) if DIRS[q][1] == -1]
Z_UP = [q for q in range(Q) if DIRS[q][2] == 1]
Z_DOWN = [q for q in range(Q) if DIRS[q][2] == -1]
Z_FLAT = [q for q in range(Q) if DIRS[q][2] == 0]
SEND_LOW = [(q, 0) for q in Z_FLAT] + [(q, 0) for q in Z_UP] + [(q, 1) for q in Z_UP]
SEND_HIGH = [(q, 0) for q in Z_FLAT] + [(q, 0) for q in Z_DOWN] + [(q, 1) for q in Z_DOWN]

RAW = 0
MIXED = 5 * CZ
Y_ROWS = 10 * CZ
RAW_ENDS = 0
MIXED_ENDS = 10
CORNERS = 20
END_ROWS = 24
Z_ROWS = Y_ROWS
K1 = QP * 8
K2 = 6 * 8

f32 = jnp.float32
bf16 = jnp.bfloat16


def along_x(value, q):
    cx = DIRS[q][0]
    if cx == 0:
        return value
    return pltpu.roll(value, (-cx) % X, value.ndim - 1)


def split(value):
    high = value.astype(bf16)
    return high, (value - high.astype(f32)).astype(bf16)


def mix(weights, reads):
    high, low = split(reads)
    return jnp.dot(
        weights, jnp.concatenate([high, low, high], axis=0), preferred_element_type=f32
    )


def stacked(tiles):
    count = max(len(t) for t in tiles if t is not None)
    zero = jnp.zeros((8, X), f32)
    full = [t if t is not None else [zero] * count for t in tiles]
    return jnp.concatenate(
        [jnp.concatenate([t[c] for t in full], axis=0) for c in range(count)], axis=1
    )


def line_tiles(line):
    return [line[8 * t : 8 * t + 8, :] for t in range(CZ // 8)]


def read_line(ref, p, y, shift=0):
    cx, cy, cz = DIRS[p]
    return ref[p, y + 1 + cy, pl.ds(Z0 + cz + shift, CZ), :]


def read_row(ref, y):
    return stacked([line_tiles(read_line(ref, p, y)) for p in range(Q)] + [None])


def load_column(ref, q, y, z):
    flat = ref.reshape(Q, (CY + 2) * ROWS, X)
    return flat[q, pl.ds((1 + y) * ROWS + Z0 + z, CY, stride=ROWS), :]


def store_column(ref, q, y, z, value):
    flat = ref.reshape(Q, (CY + 2) * ROWS, X)
    flat[q, pl.ds((1 + y) * ROWS + Z0 + z, CY, stride=ROWS), :] = value


def pack_z_kernel(field, to_pair, to_next, empty):
    empty[...] = jnp.zeros((8, X), f32)
    to_pair[8 * Q :, :] = jnp.zeros((Z_ROWS - 8 * Q, X), f32)
    to_next[8 * Q :, :] = jnp.zeros((Z_ROWS - 8 * Q, X), f32)
    even = lax.rem(lax.axis_index("gz"), 2) == 0
    for i in range(Q):
        q, d = SEND_LOW[i]
        low = field[q, pl.ds(d, CY, stride=CZ), :]
        q, d = SEND_HIGH[i]
        high = field[q, pl.ds(CZ - 1 - d, CY, stride=CZ), :]
        to_pair[8 * i : 8 * i + 8, :] = jnp.where(even, high, low)
        to_next[8 * i : 8 * i + 8, :] = jnp.where(even, low, high)


def own_channel(shape, axis, channels):
    place = lax.broadcasted_iota(jnp.int32, shape, axis) // 8
    channel = lax.broadcasted_iota(jnp.int32, shape, 1 - axis)
    hit = jnp.zeros(shape, f32)
    for i, q in enumerate(channels):
        hit = jnp.where(jnp.logical_and(place == i, channel == q), 1.0, hit)
    return hit.astype(bf16)


def spread_weights(collision, channels, width):
    rows = (
        lax.broadcasted_iota(jnp.int32, (K1, Q), 0) // 8
        == lax.broadcasted_iota(jnp.int32, (K1, Q), 1)
    ).astype(f32).astype(bf16)
    columns = own_channel((width, Q), 0, channels)
    same = (
        lax.broadcasted_iota(jnp.int32, (K1, width), 0) % 8
        == lax.broadcasted_iota(jnp.int32, (K1, width), 1) % 8
    )
    dims = (((1,), (1,)), ((), ()))
    parts = []
    for part in split(collision):
        turned = lax.dot_general(rows, part, dims, preferred_element_type=f32).astype(bf16)
        wide = lax.dot_general(turned, columns, dims, preferred_element_type=f32)
        parts.append(jnp.where(same, wide, 0.0))
    return jnp.concatenate([parts[0], parts[0], parts[1]], axis=1)


def bulk_rows_kernel(field, collision, empty, s0, s1, to_pair, to_next, w):
    nothing = empty[...]
    for q in range(Q):
        for y in range(CY):
            s0[q, 1 + y, Z0 : Z0 + CZ, :] = along_x(field[q, CZ * y : CZ * y + CZ, :], q)
    for q in Y_DOWN + Y_UP:
        for t in range(ROWS // 8):
            s0[q, 0 if DIRS[q][1] < 0 else CY + 1, 8 * t : 8 * t + 8, :] = nothing
    for q in range(Q):
        if DIRS[q][2]:
            for y in range(CY):
                s0[q, 1 + y, 0:Z0, :] = nothing
                s0[q, 1 + y, Z0 + CZ : ROWS, :] = nothing
    weights = spread_weights(collision[...], range(Q), K1)
    w[...] = weights
    weights = weights.astype(bf16)
    for y in (0, CY - 1):
        store_line(s1, y, mix(weights, read_row(s0, y)))
    even = lax.rem(lax.axis_index("gy"), 2) == 0
    for ref, base in ((s0, RAW), (s1, MIXED)):
        for i in range(5):
            low = ref[Y_UP[i], 1, Z0 : Z0 + CZ, :]
            high = ref[Y_DOWN[i], CY, Z0 : Z0 + CZ, :]
            at = base + CZ * i
            to_pair[at : at + CZ, :] = jnp.where(even, high, low)
            to_next[at : at + CZ, :] = jnp.where(even, low, high)


def end_cells_kernel(
    s0_in, s1_in, w, from_pair, from_next, s0, s1, to_pair, to_next, both
):
    del s0_in, s1_in
    iz = lax.axis_index("gz")
    even = lax.rem(iz, 2) == 0
    above = iz < lax.axis_size("gz") - 1
    below = iz > 0
    for i in range(Q):
        pair = from_pair[8 * i : 8 * i + 8, :]
        following = from_next[8 * i : 8 * i + 8, :]
        q, d = SEND_LOW[i]
        value = jnp.where(above, jnp.where(even, pair, following), 0.0)
        store_column(s0, q, 0, CZ + d, along_x(value, q))
        q, d = SEND_HIGH[i]
        value = jnp.where(below, jnp.where(even, following, pair), 0.0)
        store_column(s0, q, 0, -1 - d, along_x(value, q))
    last = CZ // 8 - 1
    spots = [(y, t) for y in (0, CY - 1) for t in (0, last)]
    tiles = []
    for p in range(Q):
        cx, cy, cz = DIRS[p]
        tiles.append(
            [s0[p, y + 1 + cy, pl.ds(Z0 + 8 * t + cz, 8), :] for y, t in spots]
            + [load_column(s0, p, cy, z + cz) for z in (-1, CZ)]
        )
    mixed = mix(w[...].astype(bf16), stacked(tiles + [None]))
    for q in range(Q):
        for c, (y, t) in enumerate(spots):
            s1[q, 1 + y, Z0 + 8 * t : Z0 + 8 * t + 8, :] = along_x(
                mixed[8 * q : 8 * q + 8, X * c : X * c + X], q
            )
    for c, (z, channels, valid) in enumerate(((-1, Z_DOWN, below), (CZ, Z_UP, above))):
        for q in channels:
            value = mixed[8 * q : 8 * q + 8, X * (4 + c) : X * (4 + c) + X]
            store_column(s1, q, 0, z, along_x(jnp.where(valid, value, 0.0), q))
    for side, (y, channels) in enumerate(((0, Y_UP), (CY - 1, Y_DOWN))):
        message = both.at[side]
        message[16:END_ROWS, :] = jnp.zeros((8, X), f32)
        for i, q in enumerate(channels):
            cz = DIRS[q][2]
            for e, z in enumerate(RAW_CELLS[cz]):
                message[pl.ds(RAW_ENDS + 2 * i + e, 1), :] = s0[q, 1 + y, pl.ds(Z0 + z, 1), :]
            for e, z in enumerate((0, CZ - 1)):
                message[pl.ds(MIXED_ENDS + 2 * i + e, 1), :] = s1[q, 1 + y, pl.ds(Z0 + z, 1), :]
            if cz:
                z, e = (CZ, 0) if cz > 0 else (-1, 1)
                message[pl.ds(CORNERS + e, 1), :] = s1[q, 1 + y, pl.ds(Z0 + z, 1), :]
    even_y = lax.rem(lax.axis_index("gy"), 2) == 0
    to_pair[...] = jnp.where(even_y, both[1], both[0])
    to_next[...] = jnp.where(even_y, both[0], both[1])


RAW_CELLS = {0: (-1, CZ), 1: (CZ, CZ + 1), -1: (-2, -1)}


def store_line(s1, y, out):
    for q in range(Q):
        for t in range(CZ // 8):
            s1[q, 1 + y, Z0 + 8 * t : Z0 + 8 * t + 8, :] = along_x(
                out[8 * q : 8 * q + 8, X * t : X * t + X], q
            )


def five_lines(ref, spare, lead, channels):
    tiles = []
    for i, p in enumerate(channels):
        cz = DIRS[p][2]
        line = ref[lead(i, p) + (pl.ds(Z0 + cz, CZ), slice(None))]
        for e, z in enumerate((-1, CZ)):
            spare[pl.ds(8 * i + e, 1), :] = ref[lead(i, p) + (pl.ds(Z0 + z + cz, 1), slice(None))]
        tiles.append(line_tiles(line) + [spare[8 * i : 8 * i + 8, :]])
    return stacked(tiles + [None])


def inner_rows_kernel(
    s0, w, s1_in, collision, panel, cell, direction,
    s1, w_up, w_down, out, scaled, rows, pick, kept, spare, numbers, sem,
):
    del s1_in
    iy = lax.axis_index("gy")
    iz = lax.axis_index("gz")
    above = iz < lax.axis_size("gz") - 1
    below = iz > 0
    weights = w[...].astype(bf16)
    for y in range(1, CY - 1):
        store_line(s1, y, mix(weights, read_row(s0, y)))
    for y in range(2, CY - 2):
        mixed = mix(weights, read_row(s1, y))
        for q in range(Q):
            for t in range(CZ // 8):
                value = mixed[8 * q : 8 * q + 8, X * t : X * t + X]
                kept[q, y - 2, 8 * t : 8 * t + 8, :] = value
                at = q * (CY * CZ) + y * CZ + 8 * t
                scaled[at : at + 8, :] = value * LINK_WEIGHTS[q]
    copy = pltpu.make_async_copy(kept, out.at[:, pl.ds(2, CY - 4), :, :], sem)
    copy.start()
    numbers[...] = jnp.zeros((numbers.shape[0], X), f32)
    numbers[:, 0:CAP] = panel[...].astype(f32).T
    pick[...] = direction[...] * (CY * CZ) + cell[...]

    @pl.loop(0, numbers.shape[0], unroll=8)
    def _(d):
        rows[pl.ds(d * (CAP + 1) + CAP, 1), 0, :] = numbers[pl.ds(d, 1), :]

    w_up[...] = spread_weights(collision[...], Y_UP, K2)
    w_down[...] = spread_weights(collision[...], Y_DOWN, K2)
    spare[...] = jnp.zeros((2, K2, X), f32)
    sides = (
        (0, CY - 1, CY, Y_UP, Y_DOWN, w_down, iy < lax.axis_size("gy") - 1),
        (1, 0, -1, Y_DOWN, Y_UP, w_up, iy > 0),
    )
    for side, y, halo, channels, sources, part, valid in sides:
        rows = [part[8 * q : 8 * q + 8, :] for q in channels]
        rows = jnp.concatenate(rows + [jnp.zeros_like(rows[0])], axis=0).astype(bf16)
        reads = five_lines(s0, spare.at[side], lambda i, p: (p, 1 + y), sources)
        mixed = jnp.where(valid, mix(rows, reads), 0.0)
        for i, q in enumerate(channels):
            for t in range(CZ // 8):
                s1[q, 1 + halo, Z0 + 8 * t : Z0 + 8 * t + 8, :] = along_x(
                    mixed[8 * i : 8 * i + 8, X * t : X * t + X], q
                )
            cz = DIRS[q][2]
            if cz:
                z, row, ok = (-1, 0, below) if cz < 0 else (CZ, 1, above)
                end = along_x(mixed[8 * i : 8 * i + 8, X * (CZ // 8) :], q)[row : row + 1, :]
                s1[q, 1 + halo, pl.ds(Z0 + z, 1), :] = jnp.where(ok, end, 0.0)
    copy.wait()


def outer_rows_kernel(
    s1_in, w, w_up, w_down, from_pair, from_next, ends_pair, ends_next, pick_in, scaled_in,
    rows_in, out_in,
    s1, scaled, rows, out, kept, raw, spare, pick, pick_sem, out_sem,
):
    del s1_in, scaled_in, rows_in, out_in
    fetch = pltpu.make_async_copy(pick_in, pick, pick_sem)
    fetch.start()
    iy = lax.axis_index("gy")
    iz = lax.axis_index("gz")
    weights = w[...].astype(bf16)
    z_ok = (iz > 0, iz < lax.axis_size("gz") - 1)
    first = lax.broadcasted_iota(jnp.int32, (8, X), 0) == 0
    final = lax.broadcasted_iota(jnp.int32, (8, X), 0) == 7
    spare[...] = jnp.zeros((2, K2, X), f32)
    even = lax.rem(iy, 2) == 0
    sides = (
        (0, CY - 1, CY, Y_UP, w_up, iy < lax.axis_size("gy") - 1),
        (1, 0, -1, Y_DOWN, w_down, iy > 0),
    )
    for side, y, halo, channels, part, valid in sides:
        arrived, others = ((from_pair, from_next), (from_next, from_pair))[side]
        ends, other_ends = ((ends_pair, ends_next), (ends_next, ends_pair))[side]
        ends = jnp.where(even, ends[...], other_ends[...])
        for i, q in enumerate(channels):
            cz = DIRS[q][2]
            at = pl.ds(RAW + CZ * i, CZ)
            line = jnp.where(even, arrived[at, :], others[at, :])
            raw[side, i, Z0 : Z0 + CZ, :] = jnp.where(valid, line, 0.0)
            for e, z in enumerate(RAW_CELLS[cz]):
                at = RAW_ENDS + 2 * i + e
                raw[side, i, pl.ds(Z0 + z, 1), :] = jnp.where(valid, ends[at : at + 1, :], 0.0)
        reads = five_lines(raw.at[side], spare.at[side], lambda i, p: (i,), channels)
        mixed = mix(part[...].astype(bf16), reads)
        for q in range(Q):
            for t in range(CZ // 8):
                at = pl.ds(Z0 + 8 * t, 8)
                s1[q, 1 + y, at, :] += along_x(mixed[8 * q : 8 * q + 8, X * t : X * t + X], q)
            cz = DIRS[q][2]
            if cz:
                row = 0 if cz < 0 else 1
                end = along_x(mixed[8 * q : 8 * q + 8, X * (CZ // 8) :], q)[row : row + 1, :]
                at = pl.ds(Z0 - 1 if cz < 0 else Z0 + CZ, 1)
                s1[q, 1 + y, at, :] += jnp.where(z_ok[row], end, 0.0)
        for i, q in enumerate(channels):
            for t in range(CZ // 8):
                at = pl.ds(MIXED + CZ * i + 8 * t, 8)
                value = jnp.where(even, arrived[at, :], others[at, :])
                at = MIXED_ENDS + 2 * i
                if t == 0:
                    value = jnp.where(first, ends[at : at + 1, :], value)
                if t == CZ // 8 - 1:
                    value = jnp.where(final, ends[at + 1 : at + 2, :], value)
                s1[q, 1 + halo, Z0 + 8 * t : Z0 + 8 * t + 8, :] += jnp.where(valid, value, 0.0)
            cz = DIRS[q][2]
            if cz:
                z, e = (CZ, 0) if cz > 0 else (-1, 1)
                value = ends[CORNERS + e : CORNERS + e + 1, :]
                s1[q, 1 + halo, pl.ds(Z0 + z, 1), :] += jnp.where(valid, value, 0.0)

    copies = [
        pltpu.make_async_copy(
            kept.at[:, pl.ds(2 * h, 2), :, :], out.at[:, pl.ds(6 * h, 2), :, :], out_sem.at[h]
        )
        for h in range(2)
    ]
    for k, y in enumerate((0, 1, CY - 2, CY - 1)):
        mixed = mix(weights, read_row(s1, y))
        for q in range(Q):
            for t in range(CZ // 8):
                value = mixed[8 * q : 8 * q + 8, X * t : X * t + X]
                kept[q, k, 8 * t : 8 * t + 8, :] = value
                at = q * (CY * CZ) + y * CZ + 8 * t
                scaled[at : at + 8, :] = value * LINK_WEIGHTS[q]
        if k % 2:
            copies[k // 2].start()
    fetch.wait()

    @pl.loop(0, pick.shape[1], unroll=4)
    def _(d):
        for k in range(CAP):
            rows[pl.ds(d * (CAP + 1) + k, 1), 0, :] = scaled[pl.ds(pick[k, d], 1), :]

    for copy in copies:
        copy.wait()


def sum_kernel(arrived, out):
    devices = arrived.shape[0] // (CAP + 1)
    numbers = arrived[pl.ds(CAP, devices, stride=CAP + 1), :].T
    panels = lax.broadcasted_iota(jnp.int32, (P_DEV, devices), 0).astype(f32)
    hot, rows = [], []
    for k in range(CAP):
        hot.append((numbers[k : k + 1, :] == panels).astype(f32).astype(bf16))
        rows.append(arrived[pl.ds(k, devices, stride=CAP + 1), :])
    hot = jnp.concatenate(hot, axis=1)
    high, low = split(jnp.concatenate(rows, axis=0))
    dot = functools.partial(jnp.dot, preferred_element_type=f32)
    out[...] = dot(hot, high) + dot(hot, low)


VMEM = pl.BlockSpec(memory_space=pltpu.VMEM)
HBM = pl.BlockSpec(memory_space=pltpu.HBM)
MIB = 1024 * 1024


def call(kernel, name, ins, outs, shapes, scratch=(), aliases=None, cost=None):
    return pl.pallas_call(
        kernel,
        out_shape=[jax.ShapeDtypeStruct(*s) for s in shapes],
        in_specs=ins,
        out_specs=outs,
        scratch_shapes=list(scratch),
        input_output_aliases=aliases or {},
        compiler_params=pltpu.CompilerParams(vmem_limit_bytes=32 * MIB),
        cost_estimate=cost
        and pl.CostEstimate(flops=cost, bytes_accessed=cost // 1000, transcendentals=cost // 1000),
        name=name,
    )


def pairings(gy, gz):
    def exchange(partner):
        found = []
        for y in range(gy):
            for z in range(gz):
                py, pz = partner(y, z)
                found.append((y * gz + z, py * gz + pz))
        return found

    def step(i, n):
        j = i - 1 if i % 2 == 0 else i + 1
        return j if 0 <= j < n else None

    def z_next(y, z):
        return (y ^ 1, z) if step(z, gz) is None else (y, step(z, gz))

    def y_next(y, z):
        return (y, z ^ 1) if step(y, gy) is None else (step(y, gy), z)

    return (
        exchange(lambda y, z: (y, z ^ 1)),
        exchange(z_next),
        exchange(lambda y, z: (y ^ 1, z)),
        exchange(y_next),
    )


def on_device(adjoint, collision, link_cell, link_dir, link_panel):
    gz = lax.axis_size("gz")
    gy = lax.axis_size("gy")
    devices = link_cell.shape[1]
    pad = (Q, CY + 2, ROWS, X)
    own = (Q, CY, CZ, X)
    flat = adjoint.reshape(Q, CY * CZ, X)
    dma = pltpu.SemaphoreType.DMA
    to_pair, to_next, empty = call(
        pack_z_kernel, "pack_z", [VMEM], [VMEM] * 3, [((Z_ROWS, X), f32)] * 2 + [((8, X), f32)],
        cost=4_000_000_000,
    )(flat)
    both = ("gy", "gz")
    z_pairs, z_nexts, y_pairs, y_nexts = pairings(gy, gz)
    from_pair = lax.ppermute(to_pair, both, z_pairs)
    from_next = lax.ppermute(to_next, both, z_nexts)
    lines = ((Y_ROWS, X), f32)
    wide = ((K1, 3 * K1), f32)
    narrow = ((K1, 3 * K2), f32)
    s0, s1, to_y_pair, to_y_next, w = call(
        bulk_rows_kernel, "bulk_rows", [VMEM] * 3, [VMEM] * 5,
        [(pad, f32), (pad, f32), lines, lines, wide],
    )(flat, collision, empty)
    from_y_pair = lax.ppermute(to_y_pair, both, y_pairs)
    from_y_next = lax.ppermute(to_y_next, both, y_nexts)
    s0, s1, to_y_pair, to_y_next = call(
        end_cells_kernel, "end_cells", [VMEM] * 5, [VMEM] * 4,
        [(pad, f32), (pad, f32), ((END_ROWS, X), f32), ((END_ROWS, X), f32)],
        scratch=[pltpu.VMEM((2, END_ROWS, X), f32)],
        aliases={0: 0, 1: 1},
    )(s0, s1, w, from_pair, from_next)
    ends_pair = lax.ppermute(to_y_pair, both, y_pairs)
    ends_next = lax.ppermute(to_y_next, both, y_nexts)
    table = ((Q * CY * CZ, X), f32)
    message = ((devices * (CAP + 1), 1, X), f32)
    s1, w_up, w_down, out, scaled, rows, pick = call(
        inner_rows_kernel, "inner_rows", [VMEM] * 7, [VMEM] * 3 + [HBM] + [VMEM] * 3,
        [(pad, f32), narrow, narrow, (own, f32), table]
        + [message, ((CAP, devices), jnp.int32)],
        scratch=[
            pltpu.VMEM((Q, CY - 4, CZ, X), f32),
            pltpu.VMEM((2, K2, X), f32),
            pltpu.VMEM((devices, X), f32),
            dma,
        ],
        aliases={2: 0},
    )(s0, w, s1, collision, link_panel[0].T, link_cell[0].T, link_dir[0].T)
    _, _, rows, out = call(
        outer_rows_kernel, "outer_rows", [VMEM] * 11 + [HBM], [VMEM] * 3 + [HBM],
        [(pad, f32), table, message, (own, f32)],
        scratch=[
            pltpu.VMEM((Q, 4, CZ, X), f32),
            pltpu.VMEM((2, 5, ROWS, X), f32),
            pltpu.VMEM((2, K2, X), f32),
            pltpu.SMEM((CAP, devices), jnp.int32),
            dma,
            dma((2,)),
        ],
        aliases={0: 0, 9: 1, 10: 2, 11: 3},
    )(s1, w, w_up, w_down, from_y_pair, from_y_next, ends_pair, ends_next, pick, scaled, rows, out)
    arrived = lax.all_to_all(
        rows.reshape(devices, CAP + 1, 1, X), ("gy", "gz"), split_axis=0, concat_axis=0, tiled=True
    )
    (panel_sens,) = call(sum_kernel, "sum_rows", [VMEM], [VMEM], [((P_DEV, X), f32)])(
        arrived.reshape(devices * (CAP + 1), X)
    )
    return out, panel_sens


def solution(mesh):
    placed = (
        P(None, "gy", "gz", None),
        P(),
        P(("gy", "gz"), None, None),
        P(("gy", "gz"), None, None),
        P(("gy", "gz"), None, None),
    )
    return jax.shard_map(
        on_device,
        mesh=mesh,
        in_specs=placed,
        out_specs=(P(None, "gy", "gz", None), P(("gy", "gz"), None)),
        check_vma=False,
    )
```

time: 47.8 us -> 43.7 us (0.914)
  waiting for transfers between devices: 6.44 us -> 1.06 us
  blocking collectives: 22.2 us -> 26.2 us
  starting transfers between devices: 8.31 us -> 6.71 us
  Pallas kernels: 8.28 us -> 7.15 us
    ppermute x4 -> x6, waiting for transfers between devices: 6.44 us -> 1.06 us  [the longest x1 1.05 us: on_device(): from_next = lax.ppermute(to_next, both, z_nexts)]
    all_to_all x1, blocking collectives: 22.2 us -> 26.2 us  [on_device(): lax.all_to_all(rows.reshape(devices, CAP + 1, 1, X), ('gy', 'gz'), split_...]
    ppermute x4 -> x6, starting transfers between devices: 8.31 us -> 6.71 us  [the longest x1 1.7 us: on_device(): from_next = lax.ppermute(to_next, both, z_nexts)]
    pallas_call x5, Pallas kernels: 7.38 us -> 6.25 us  [the longest x1 2.66 us: on_device(): call(outer_rows_kernel, 'outer_rows', [VMEM] * 11 + [HBM], [VMEM] * 3 + [...]
  transfers between devices with their start and end apart: 4 -> 6, of which waited for: 2 -> 1; matrix products, arithmetic and copies ran while one was open for 0% -> 0% of each run, Pallas kernels for 7% -> 8%
where the time goes in v2:
time: 43.7 us; the launch traced here: 43.5 us
  blocking collectives  26.2 us (60%)
  Pallas kernels  7.15 us (16%)
  starting transfers between devices  6.71 us (15%)
  local copies, waits for them, and re-layouts  1.71 us (4%)
  waiting for transfers between devices  1.06 us (2%)
  between operations  0.71 us (2%)
    all_to_all x1, blocking collectives, on_device(): lax.all_to_all(rows.reshape(devices, CAP + 1, 1, X), ('gy', 'gz'), split_...  26.2 us
    pallas_call x1, Pallas kernels, on_device(): call(outer_rows_kernel, 'outer_rows', [VMEM] * 11 + [HBM], [VMEM] * 3 + [...  2.66 us
    pallas_call x1, Pallas kernels, on_device(): call(inner_rows_kernel, 'inner_rows', [VMEM] * 7, [VMEM] * 3 + [HBM] + [V...  2.11 us
    unnamed x10, local copies, waits for them, and re-layouts  1.71 us
    ppermute x1, starting transfers between devices, on_device(): from_next = lax.ppermute(to_next, both, z_nexts)  1.7 us
    ppermute x1, starting transfers between devices, on_device(): from_pair = lax.ppermute(to_pair, both, z_pairs)  1.5 us
    ppermute x1, starting transfers between devices, on_device(): ends_pair = lax.ppermute(to_y_pair, both, y_pairs)  1.48 us
    ppermute x1, starting transfers between devices, on_device(): from_y_pair = lax.ppermute(to_y_pair, both, y_pairs)  1.38 us
  transfers between devices with their start and end apart: 6, of which 1 were waited for; matrix products, arithmetic and copies ran while one was open for 0% of the time, Pallas kernels for 8%

profile of v2, /device:TPU:1, one launch (start us, length us, event | category | flops | bytes accessed | tf_op | source)
XLA Modules:
  0.0 43.5 jit_solution(5328722807703890750)
XLA Ops:
  0.6 0.0 copy-start
  0.6 1.7 %copy-done = f32[19,8,32,128]{3,2,1,0:T(8,128)S(1)} copy-done((f32[19,8,32,128]{3,2,1,0:T(8,128)S(1)}, f32[19,8,32,128]{3,2,1,0:T(8,128)}, u32[]{:S(2)}) %copy-start) | copy-done | bytes 2490392
  2.3 0.0 copy-start.1
  2.3 0.1 pack_z.1
  2.4 1.5 %collective-permute-start = (f32[320,128]{1,0:T(8,128)S(1)}, f32[320,128]{1,0:T(8,128)S(1)}, u32[]{:S(2)}, u32[]{:S(2)}) collective-permute-start(f32[320,128]{1,0:T(8,128)S(1)} %get-tuple-element.27), channel_id=1, source_target_pairs={{0,1},{1,0},{2,3},{3,2},{4,5},{5,4},{6,7},{7,6},{8,9},{9,8},{10,11... | collective-permute-start | bytes 491528 | tf_op jit(solution)/shard_map/ppermute | solution.py:479
  3.9 1.7 %collective-permute-start.1 = (f32[320,128]{1,0:T(8,128)S(1)}, f32[320,128]{1,0:T(8,128)S(1)}, u32[]{:S(2)}, u32[]{:S(2)}) collective-permute-start(f32[320,128]{1,0:T(8,128)S(1)} %get-tuple-element.28), channel_id=1, source_target_pairs={{0,8},{1,2},{2,1},{3,4},{4,3},{5,6},{6,5},{7,15},{8,0},{9,10},{10,... | collective-permute-start | bytes 491528 | tf_op jit(solution)/shard_map/ppermute | solution.py:480
  5.6 0.0 copy-done.1
  5.6 0.9 %bulk_rows.1 = (f32[19,10,48,128]{3,2,1,0:T(8,128)S(1)}, f32[19,10,48,128]{3,2,1,0:T(8,128)S(1)}, f32[320,128]{1,0:T(8,128)S(1)}, f32[320,128]{1,0:T(8,128)S(1)}, f32[160,480]{1,0:T(8,128)S(1)}) custom-call(f32[19,256,128]{2,1,0:T(8,128)S(1)} %bitcast.13, f32[19,19]{1,0:T(8,128)S(1)} %copy-done.1, f32[8,128]{1,0:T(8,128)S(1)} %get-tuple-element.23.empty), custom_call_target="tpu_custom_call" | custom-call | tf_op jit(solution)/shard_map/bulk_rows/pallas_call | solution.py:484
  6.5 1.4 %collective-permute-start.2 = (f32[320,128]{1,0:T(8,128)S(1)}, f32[320,128]{1,0:T(8,128)S(1)}, u32[]{:S(2)}, u32[]{:S(2)}) collective-permute-start(f32[320,128]{1,0:T(8,128)S(1)} %get-tuple-element.34), channel_id=1, source_target_pairs={{0,8},{1,9},{2,10},{3,11},{4,12},{5,13},{6,14},{7,15},{8,0},{9,1},... | collective-permute-start | bytes 491528 | tf_op jit(solution)/shard_map/ppermute | solution.py:488
  7.9 0.0 collective-permute-start.3
  7.9 0.0 collective-permute-done.from_pair
  7.9 1.0 %collective-permute-done.1.from_next = f32[320,128]{1,0:T(8,128)S(1)} collective-permute-done((f32[320,128]{1,0:T(8,128)S(1)}, f32[320,128]{1,0:T(8,128)S(1)}, u32[]{:S(2)}, u32[]{:S(2)}) %collective-permute-start.1) | collective-permute-done | bytes 163872 | tf_op jit(solution)/shard_map/ppermute | solution.py:480
  9.0 0.0 copy-start.2
  9.0 0.0 copy-start.3
  9.0 0.0 copy-start.4
  9.0 0.5 %end_cells.1 = (f32[19,10,48,128]{3,2,1,0:T(8,128)S(1)}, f32[19,10,48,128]{3,2,1,0:T(8,128)S(1)}, f32[24,128]{1,0:T(8,128)S(1)}, f32[24,128]{1,0:T(8,128)S(1)}) custom-call(f32[19,10,48,128]{3,2,1,0:T(8,128)S(1)} %get-tuple-element.24.s0_in, f32[19,10,48,128]{3,2,1,0:T(8,128)S(1)} %get-tuple-element.25.s1_in, ...), custom_call_target="tpu_custom_call", output_to_operand_aliasing={{0}: (0, {}), {1}: (1, {})} | custom-call | tf_op jit(solution)/shard_map/end_cells/pallas_call | solution.py:490
  9.5 1.5 %collective-permute-start.4 = (f32[24,128]{1,0:T(8,128)S(1)}, f32[24,128]{1,0:T(8,128)S(1)}, u32[]{:S(2)}, u32[]{:S(2)}) collective-permute-start(f32[24,128]{1,0:T(8,128)S(1)} %get-tuple-element.36), channel_id=1, source_target_pairs={{0,8},{1,9},{2,10},{3,11},{4,12},{5,13},{6,14},{7,15},{8,0},{9,1},... | collective-permute-start | bytes 36872 | tf_op jit(solution)/shard_map/ppermute | solution.py:496
  10.9 0.7 %collective-permute-start.5 = (f32[24,128]{1,0:T(8,128)S(1)}, f32[24,128]{1,0:T(8,128)S(1)}, u32[]{:S(2)}, u32[]{:S(2)}) collective-permute-start(f32[24,128]{1,0:T(8,128)S(1)} %get-tuple-element.37), channel_id=1, source_target_pairs={{0,1},{1,0},{2,3},{3,2},{4,5},{5,4},{6,7},{7,6},{8,16},{9,17},{10,... | collective-permute-start | bytes 36872 | tf_op jit(solution)/shard_map/ppermute | solution.py:497
  11.6 0.0 copy-done.2
  11.6 0.0 copy-done.3
  11.6 0.0 copy-done.4
  11.6 2.1 %inner_rows.1 = (f32[19,10,48,128]{3,2,1,0:T(8,128)S(1)}, f32[160,144]{1,0:T(8,128)S(1)}, f32[160,144]{1,0:T(8,128)S(1)}, f32[19,8,32,128]{3,2,1,0:T(8,128)}, f3...) custom-call(f32[19,10,48,128]{3,2,1,0:T(8,128)S(1)} %get-tuple-eleme, ...), custom_call_target="tpu_custom_call", output_to_operand_aliasing={{0}: (2, {})} | custom-call | tf_op jit(solution)/shard_map/inner_rows/pallas_call | solution.py:500
  13.7 0.0 collective-permute-done.2.from_pair
  13.7 0.0 collective-permute-done.3.from_next
  13.7 0.0 collective-permute-done.4.ends_pair
  13.8 0.0 collective-permute-done.5.ends_next
  13.8 2.7 %outer_rows.1 = (f32[19,10,48,128]{3,2,1,0:T(8,128)S(1)}, f32[4864,128]{1,0:T(8,128)S(1)}, f32[1152,1,128]{2,1,0:T(1,128)S(1)}, f32[19,8,32,128]{3,2,1,0:T(8,128)}) custom-call(f32[19,10,48,128]{3,2,1,0:T(8,128)S(1)} %get-tuple-element.31.s1_in, ...), custom_call_target="tpu_custom_call", output_to_operand_aliasing={{0}: (0, {}), {1}: (9, {}), {2}: (10, {}), {3}: (11, {})} | custom-call | tf_op jit(solution)/shard_map/outer_rows/pallas_call | solution.py:512
  16.4 26.2 %all_to_all.5 = f32[128,9,1,128]{3,2,1,0:T(1,128)S(1)} all-to-all(f32[128,9,1,128]{3,2,1,0:T(1,128)S(1)} %bitcast.14), channel_id=1, replica_groups=mesh['gy'=16,'gz'=8] {'gy','gz'}, dimensions={0} | all-to-all | bytes 1179648 | tf_op jit(solution)/shard_map/all_to_all | solution.py:525
  42.6 0.9 %sum_rows.1 = f32[64,128]{1,0:T(8,128)} custom-call(f32[1152,128]{1,0:T(8,128)S(1)} %bitcast.15), custom_call_target="tpu_custom_call" | custom-call | tf_op jit(solution)/shard_map/sum_rows/pallas_call | solution.py:528
Async XLA Ops:
  0.6 1.7 %copy-start = (f32[19,8,32,128]{3,2,1,0:T(8,128)S(1)}, f32[19,8,32,128]{3,2,1,0:T(8,128)}, u32[]{:S(2)}) copy-start(f32[19,8,32,128]{3,2,1,0:T(8,128)} %param.5) | copy-start | bytes 7471108
  2.3 3.3 %copy-start.1 = (f32[19,19]{1,0:T(8,128)S(1)}, f32[19,19]{1,0:T(8,128)}, u32[]{:S(2)}) copy-start(f32[19,19]{1,0:T(8,128)} %collision.3) | copy-start | bytes 4336
  2.4 5.5 %collective-permute-start = (f32[320,128]{1,0:T(8,128)S(1)}, f32[320,128]{1,0:T(8,128)S(1)}, u32[]{:S(2)}, u32[]{:S(2)}) collective-permute-start(f32[320,128]{1,0:T(8,128)S(1)} %get-tuple-element.27), channel_id=1, source_target_pairs={{0,1},{1,0},{2,3},{3,2},{4,5},{5,4},{6,7},{7,6},{8,9},{9,8},{10,11... | collective-permute-start | bytes 491528 | tf_op jit(solution)/shard_map/ppermute | solution.py:479
  3.9 5.0 %collective-permute-start.1 = (f32[320,128]{1,0:T(8,128)S(1)}, f32[320,128]{1,0:T(8,128)S(1)}, u32[]{:S(2)}, u32[]{:S(2)}) collective-permute-start(f32[320,128]{1,0:T(8,128)S(1)} %get-tuple-element.28), channel_id=1, source_target_pairs={{0,8},{1,2},{2,1},{3,4},{4,3},{5,6},{6,5},{7,15},{8,0},{9,10},{10,... | collective-permute-start | bytes 491528 | tf_op jit(solution)/shard_map/ppermute | solution.py:480
  6.5 7.2 %collective-permute-start.2 = (f32[320,128]{1,0:T(8,128)S(1)}, f32[320,128]{1,0:T(8,128)S(1)}, u32[]{:S(2)}, u32[]{:S(2)}) collective-permute-start(f32[320,128]{1,0:T(8,128)S(1)} %get-tuple-element.34), channel_id=1, source_target_pairs={{0,8},{1,9},{2,10},{3,11},{4,12},{5,13},{6,14},{7,15},{8,0},{9,1},... | collective-permute-start | bytes 491528 | tf_op jit(solution)/shard_map/ppermute | solution.py:488
  7.9 5.8 %collective-permute-start.3 = (f32[320,128]{1,0:T(8,128)S(1)}, f32[320,128]{1,0:T(8,128)S(1)}, u32[]{:S(2)}, u32[]{:S(2)}) collective-permute-start(f32[320,128]{1,0:T(8,128)S(1)} %get-tuple-element.35), channel_id=1, source_target_pairs={{0,1},{1,0},{2,3},{3,2},{4,5},{5,4},{6,7},{7,6},{8,16},{9,17},{10,... | collective-permute-start | bytes 491528 | tf_op jit(solution)/shard_map/ppermute | solution.py:489
  9.0 2.6 %copy-start.2 = (s32[1,128,8]{1,2,0:T(8,128)S(1)}, s32[1,128,8]{1,2,0:T(8,128)}, u32[]{:S(2)}) copy-start(s32[1,128,8]{1,2,0:T(8,128)} %param.9) | copy-start | bytes 12292
  9.0 2.6 %copy-start.3 = (s32[1,128,8]{1,2,0:T(8,128)S(1)}, s32[1,128,8]{1,2,0:T(8,128)}, u32[]{:S(2)}) copy-start(s32[1,128,8]{1,2,0:T(8,128)} %param.7) | copy-start | bytes 12292
  9.0 2.6 %copy-start.4 = (s32[1,128,8]{1,2,0:T(8,128)S(1)}, s32[1,128,8]{1,2,0:T(8,128)}, u32[]{:S(2)}) copy-start(s32[1,128,8]{1,2,0:T(8,128)} %param.8) | copy-start | bytes 12292
  9.5 4.3 %collective-permute-start.4 = (f32[24,128]{1,0:T(8,128)S(1)}, f32[24,128]{1,0:T(8,128)S(1)}, u32[]{:S(2)}, u32[]{:S(2)}) collective-permute-start(f32[24,128]{1,0:T(8,128)S(1)} %get-tuple-element.36), channel_id=1, source_target_pairs={{0,8},{1,9},{2,10},{3,11},{4,12},{5,13},{6,14},{7,15},{8,0},{9,1},... | collective-permute-start | bytes 36872 | tf_op jit(solution)/shard_map/ppermute | solution.py:496
  10.9 2.8 %collective-permute-start.5 = (f32[24,128]{1,0:T(8,128)S(1)}, f32[24,128]{1,0:T(8,128)S(1)}, u32[]{:S(2)}, u32[]{:S(2)}) collective-permute-start(f32[24,128]{1,0:T(8,128)S(1)} %get-tuple-element.37), channel_id=1, source_target_pairs={{0,1},{1,0},{2,3},{3,2},{4,5},{5,4},{6,7},{7,6},{8,16},{9,17},{10,... | collective-permute-start | bytes 36872 | tf_op jit(solution)/shard_map/ppermute | solution.py:497

commit v3 on v2

--- a/solution.py
+++ b/solution.py
@@ -55,7 +55,7 @@
 MIXED_ENDS = 10
 CORNERS = 20
 END_ROWS = 24
-Z_ROWS = Y_ROWS
+Z_ROWS = 8 * Q
 K1 = QP * 8
 K2 = 6 * 8
 
@@ -114,10 +114,9 @@
     flat[q, pl.ds((1 + y) * ROWS + Z0 + z, CY, stride=ROWS), :] = value
 
 
-def pack_z_kernel(field, to_pair, to_next, empty):
+def pack_z_kernel(field, w, to_pair, to_next, empty):
+    del w
     empty[...] = jnp.zeros((8, X), f32)
-    to_pair[8 * Q :, :] = jnp.zeros((Z_ROWS - 8 * Q, X), f32)
-    to_next[8 * Q :, :] = jnp.zeros((Z_ROWS - 8 * Q, X), f32)
     even = lax.rem(lax.axis_index("gz"), 2) == 0
     for i in range(Q):
         q, d = SEND_LOW[i]
@@ -156,22 +155,29 @@
     return jnp.concatenate([parts[0], parts[0], parts[1]], axis=1)
 
 
-def bulk_rows_kernel(field, collision, empty, s0, s1, to_pair, to_next, w):
+def weights_kernel(collision, w, w_up, w_down):
+    w[...] = spread_weights(collision[...], range(Q), K1)
+    w_up[...] = spread_weights(collision[...], Y_UP, K2)
+    w_down[...] = spread_weights(collision[...], Y_DOWN, K2)
+
+
+EDGE_ROWS = (0, 1, CY - 2, CY - 1)
+
+
+def bulk_rows_kernel(field, w, empty, s0, s1, to_pair, to_next):
     nothing = empty[...]
     for q in range(Q):
-        for y in range(CY):
+        for y in EDGE_ROWS:
             s0[q, 1 + y, Z0 : Z0 + CZ, :] = along_x(field[q, CZ * y : CZ * y + CZ, :], q)
     for q in Y_DOWN + Y_UP:
         for t in range(ROWS // 8):
             s0[q, 0 if DIRS[q][1] < 0 else CY + 1, 8 * t : 8 * t + 8, :] = nothing
     for q in range(Q):
         if DIRS[q][2]:
-            for y in range(CY):
+            for y in EDGE_ROWS:
                 s0[q, 1 + y, 0:Z0, :] = nothing
                 s0[q, 1 + y, Z0 + CZ : ROWS, :] = nothing
-    weights = spread_weights(collision[...], range(Q), K1)
-    w[...] = weights
-    weights = weights.astype(bf16)
+    weights = w[...].astype(bf16)
     for y in (0, CY - 1):
         store_line(s1, y, mix(weights, read_row(s0, y)))
     even = lax.rem(lax.axis_index("gy"), 2) == 0
@@ -185,7 +191,7 @@
 
 
 def end_cells_kernel(
-    s0_in, s1_in, w, from_pair, from_next, s0, s1, to_pair, to_next, both
+    s0_in, s1_in, w, from_pair, from_next, s0, s1, to_pair, to_next, both, corner
 ):
     del s0_in, s1_in
     iz = lax.axis_index("gz")
@@ -203,12 +209,15 @@
         store_column(s0, q, 0, -1 - d, along_x(value, q))
     last = CZ // 8 - 1
     spots = [(y, t) for y in (0, CY - 1) for t in (0, last)]
+    corners = [(y, z) for y in (0, CY - 1) for z in (-1, CZ)]
+    corner[...] = jnp.zeros((Q, 8, X), f32)
     tiles = []
     for p in range(Q):
         cx, cy, cz = DIRS[p]
+        for c, (y, z) in enumerate(corners):
+            corner[p, pl.ds(c, 1), :] = s0[p, y + 1 + cy, pl.ds(Z0 + z + cz, 1), :]
         tiles.append(
-            [s0[p, y + 1 + cy, pl.ds(Z0 + 8 * t + cz, 8), :] for y, t in spots]
-            + [load_column(s0, p, cy, z + cz) for z in (-1, CZ)]
+            [s0[p, y + 1 + cy, pl.ds(Z0 + 8 * t + cz, 8), :] for y, t in spots] + [corner[p]]
         )
     mixed = mix(w[...].astype(bf16), stacked(tiles + [None]))
     for q in range(Q):
@@ -216,10 +225,12 @@
             s1[q, 1 + y, Z0 + 8 * t : Z0 + 8 * t + 8, :] = along_x(
                 mixed[8 * q : 8 * q + 8, X * c : X * c + X], q
             )
-    for c, (z, channels, valid) in enumerate(((-1, Z_DOWN, below), (CZ, Z_UP, above))):
-        for q in channels:
-            value = mixed[8 * q : 8 * q + 8, X * (4 + c) : X * (4 + c) + X]
-            store_column(s1, q, 0, z, along_x(jnp.where(valid, value, 0.0), q))
+        if DIRS[q][2]:
+            ends = along_x(mixed[8 * q : 8 * q + 8, X * 4 :], q)
+            for c, (y, z) in enumerate(corners):
+                if DIRS[q][2] == (1 if z > 0 else -1):
+                    value = jnp.where(above if z > 0 else below, ends[c : c + 1, :], 0.0)
+                    s1[q, 1 + y, pl.ds(Z0 + z, 1), :] = value
     for side, (y, channels) in enumerate(((0, Y_UP), (CY - 1, Y_DOWN))):
         message = both.at[side]
         message[16:END_ROWS, :] = jnp.zeros((8, X), f32)
@@ -260,15 +271,30 @@
 
 
 def inner_rows_kernel(
-    s0, w, s1_in, collision, panel, cell, direction,
-    s1, w_up, w_down, out, scaled, rows, pick, kept, spare, numbers, sem,
+    s0_in, w, s1_in, w_up, w_down, field, panel, cell, direction,
+    s0, s1, out, scaled, rows, pick, kept, spare, numbers, sem,
 ):
-    del s1_in
+    del s0_in, s1_in
     iy = lax.axis_index("gy")
     iz = lax.axis_index("gz")
     above = iz < lax.axis_size("gz") - 1
     below = iz > 0
     weights = w[...].astype(bf16)
+    for y in range(2, CY - 2):
+        for q in range(Q):
+            s0[q, 1 + y, Z0 : Z0 + CZ, :] = along_x(field[q, CZ * y : CZ * y + CZ, :], q)
+    reads = stacked(
+        [
+            [load_column(s0, p, DIRS[p][1], z + DIRS[p][2]) for z in (-1, CZ)]
+            for p in range(Q)
+        ]
+        + [None]
+    )
+    mixed = mix(weights, reads)
+    for c, (z, channels, valid) in enumerate(((-1, Z_DOWN, below), (CZ, Z_UP, above))):
+        for q in channels:
+            value = along_x(mixed[8 * q : 8 * q + 8, X * c : X * c + X], q)
+            store_column(s1, q, 0, z, jnp.where(valid, value, 0.0))
     for y in range(1, CY - 1):
         store_line(s1, y, mix(weights, read_row(s0, y)))
     for y in range(2, CY - 2):
@@ -289,8 +315,6 @@
     def _(d):
         rows[pl.ds(d * (CAP + 1) + CAP, 1), 0, :] = numbers[pl.ds(d, 1), :]
 
-    w_up[...] = spread_weights(collision[...], Y_UP, K2)
-    w_down[...] = spread_weights(collision[...], Y_DOWN, K2)
     spare[...] = jnp.zeros((2, K2, X), f32)
     sides = (
         (0, CY - 1, CY, Y_UP, Y_DOWN, w_down, iy < lax.axis_size("gy") - 1),
@@ -329,23 +353,44 @@
     first = lax.broadcasted_iota(jnp.int32, (8, X), 0) == 0
     final = lax.broadcasted_iota(jnp.int32, (8, X), 0) == 7
     spare[...] = jnp.zeros((2, K2, X), f32)
-    even = lax.rem(iy, 2) == 0
     sides = (
         (0, CY - 1, CY, Y_UP, w_up, iy < lax.axis_size("gy") - 1),
         (1, 0, -1, Y_DOWN, w_down, iy > 0),
     )
-    for side, y, halo, channels, part, valid in sides:
-        arrived, others = ((from_pair, from_next), (from_next, from_pair))[side]
-        ends, other_ends = ((ends_pair, ends_next), (ends_next, ends_pair))[side]
-        ends = jnp.where(even, ends[...], other_ends[...])
+
+    def take(side, bulk, ends):
+        _, _, halo, channels, _, _ = sides[side]
         for i, q in enumerate(channels):
             cz = DIRS[q][2]
-            at = pl.ds(RAW + CZ * i, CZ)
-            line = jnp.where(even, arrived[at, :], others[at, :])
-            raw[side, i, Z0 : Z0 + CZ, :] = jnp.where(valid, line, 0.0)
+            raw[side, i, Z0 : Z0 + CZ, :] = bulk[RAW + CZ * i : RAW + CZ * i + CZ, :]
             for e, z in enumerate(RAW_CELLS[cz]):
-                at = RAW_ENDS + 2 * i + e
-                raw[side, i, pl.ds(Z0 + z, 1), :] = jnp.where(valid, ends[at : at + 1, :], 0.0)
+                raw[side, i, pl.ds(Z0 + z, 1), :] = ends[pl.ds(RAW_ENDS + 2 * i + e, 1), :]
+            for t in range(CZ // 8):
+                value = bulk[MIXED + CZ * i + 8 * t : MIXED + CZ * i + 8 * t + 8, :]
+                at = MIXED_ENDS + 2 * i
+                if t == 0:
+                    value = jnp.where(first, ends[at : at + 1, :], value)
+                if t == CZ // 8 - 1:
+                    value = jnp.where(final, ends[at + 1 : at + 2, :], value)
+                s1[q, 1 + halo, Z0 + 8 * t : Z0 + 8 * t + 8, :] += value
+            if cz:
+                z, e = (CZ, 0) if cz > 0 else (-1, 1)
+                s1[q, 1 + halo, pl.ds(Z0 + z, 1), :] += ends[CORNERS + e : CORNERS + e + 1, :]
+
+    odd = lax.rem(iy, 2)
+    for side, (_, _, _, _, _, valid) in enumerate(sides):
+        pl.when(jnp.logical_and(valid, odd == side))(
+            functools.partial(take, side, from_pair, ends_pair)
+        )
+        pl.when(jnp.logical_and(valid, odd != side))(
+            functools.partial(take, side, from_next, ends_next)
+        )
+
+        @pl.when(jnp.logical_not(valid))
+        def _(side=side):
+            raw[side] = jnp.zeros((5, ROWS, X), f32)
+
+    for side, y, halo, channels, part, valid in sides:
         reads = five_lines(raw.at[side], spare.at[side], lambda i, p: (i,), channels)
         mixed = mix(part[...].astype(bf16), reads)
         for q in range(Q):
@@ -358,21 +403,6 @@
                 end = along_x(mixed[8 * q : 8 * q + 8, X * (CZ // 8) :], q)[row : row + 1, :]
                 at = pl.ds(Z0 - 1 if cz < 0 else Z0 + CZ, 1)
                 s1[q, 1 + y, at, :] += jnp.where(z_ok[row], end, 0.0)
-        for i, q in enumerate(channels):
-            for t in range(CZ // 8):
-                at = pl.ds(MIXED + CZ * i + 8 * t, 8)
-                value = jnp.where(even, arrived[at, :], others[at, :])
-                at = MIXED_ENDS + 2 * i
-                if t == 0:
-                    value = jnp.where(first, ends[at : at + 1, :], value)
-                if t == CZ // 8 - 1:
-                    value = jnp.where(final, ends[at + 1 : at + 2, :], value)
-                s1[q, 1 + halo, Z0 + 8 * t : Z0 + 8 * t + 8, :] += jnp.where(valid, value, 0.0)
-            cz = DIRS[q][2]
-            if cz:
-                z, e = (CZ, 0) if cz > 0 else (-1, 1)
-                value = ends[CORNERS + e : CORNERS + e + 1, :]
-                s1[q, 1 + halo, pl.ds(Z0 + z, 1), :] += jnp.where(valid, value, 0.0)
 
     copies = [
         pltpu.make_async_copy(
@@ -392,7 +422,7 @@
             copies[k // 2].start()
     fetch.wait()
 
-    @pl.loop(0, pick.shape[1], unroll=4)
+    @pl.loop(0, pick.shape[1], unroll=8)
     def _(d):
         for k in range(CAP):
             rows[pl.ds(d * (CAP + 1) + k, 1), 0, :] = scaled[pl.ds(pick[k, d], 1), :]
@@ -470,36 +500,39 @@
     own = (Q, CY, CZ, X)
     flat = adjoint.reshape(Q, CY * CZ, X)
     dma = pltpu.SemaphoreType.DMA
+    wide = ((K1, 3 * K1), f32)
+    narrow = ((K1, 3 * K2), f32)
+    w, w_up, w_down = call(
+        weights_kernel, "weights", [VMEM], [VMEM] * 3, [wide, narrow, narrow], cost=4_000_000_000
+    )(collision)
     to_pair, to_next, empty = call(
-        pack_z_kernel, "pack_z", [VMEM], [VMEM] * 3, [((Z_ROWS, X), f32)] * 2 + [((8, X), f32)],
+        pack_z_kernel, "pack_z", [VMEM] * 2, [VMEM] * 3, [((Z_ROWS, X), f32)] * 2 + [((8, X), f32)],
         cost=4_000_000_000,
-    )(flat)
+    )(flat, w)
     both = ("gy", "gz")
     z_pairs, z_nexts, y_pairs, y_nexts = pairings(gy, gz)
     from_pair = lax.ppermute(to_pair, both, z_pairs)
     from_next = lax.ppermute(to_next, both, z_nexts)
     lines = ((Y_ROWS, X), f32)
-    wide = ((K1, 3 * K1), f32)
-    narrow = ((K1, 3 * K2), f32)
-    s0, s1, to_y_pair, to_y_next, w = call(
-        bulk_rows_kernel, "bulk_rows", [VMEM] * 3, [VMEM] * 5,
-        [(pad, f32), (pad, f32), lines, lines, wide],
-    )(flat, collision, empty)
+    s0, s1, to_y_pair, to_y_next = call(
+        bulk_rows_kernel, "bulk_rows", [VMEM] * 3, [VMEM] * 4,
+        [(pad, f32), (pad, f32), lines, lines],
+    )(flat, w, empty)
     from_y_pair = lax.ppermute(to_y_pair, both, y_pairs)
     from_y_next = lax.ppermute(to_y_next, both, y_nexts)
     s0, s1, to_y_pair, to_y_next = call(
         end_cells_kernel, "end_cells", [VMEM] * 5, [VMEM] * 4,
         [(pad, f32), (pad, f32), ((END_ROWS, X), f32), ((END_ROWS, X), f32)],
-        scratch=[pltpu.VMEM((2, END_ROWS, X), f32)],
+        scratch=[pltpu.VMEM((2, END_ROWS, X), f32), pltpu.VMEM((Q, 8, X), f32)],
         aliases={0: 0, 1: 1},
     )(s0, s1, w, from_pair, from_next)
     ends_pair = lax.ppermute(to_y_pair, both, y_pairs)
     ends_next = lax.ppermute(to_y_next, both, y_nexts)
     table = ((Q * CY * CZ, X), f32)
     message = ((devices * (CAP + 1), 1, X), f32)
-    s1, w_up, w_down, out, scaled, rows, pick = call(
-        inner_rows_kernel, "inner_rows", [VMEM] * 7, [VMEM] * 3 + [HBM] + [VMEM] * 3,
-        [(pad, f32), narrow, narrow, (own, f32), table]
+    _, s1, out, scaled, rows, pick = call(
+        inner_rows_kernel, "inner_rows", [VMEM] * 9, [VMEM] * 2 + [HBM] + [VMEM] * 3,
+        [(pad, f32), (pad, f32), (own, f32), table]
         + [message, ((CAP, devices), jnp.int32)],
         scratch=[
             pltpu.VMEM((Q, CY - 4, CZ, X), f32),
@@ -507,8 +540,9 @@
             pltpu.VMEM((devices, X), f32),
             dma,
         ],
-        aliases={2: 0},
-    )(s0, w, s1, collision, link_panel[0].T, link_cell[0].T, link_dir[0].T)
+        cost=4_000_000_000,
+        aliases={0: 0, 2: 1},
+    )(s0, w, s1, w_up, w_down, flat, link_panel[0].T, link_cell[0].T, link_dir[0].T)
     _, _, rows, out = call(
         outer_rows_kernel, "outer_rows", [VMEM] * 11 + [HBM], [VMEM] * 3 + [HBM],
         [(pad, f32), table, message, (own, f32)],

time: 43.7 us -> 42.4 us (0.970)
  local copies, waits for them, and re-layouts: 1.71 us -> 1.12 us
  waiting for transfers between devices: 1.06 us -> 0.5 us
    unnamed x10, local copies, waits for them, and re-layouts: 1.71 us -> 1.12 us
    ppermute x1, waiting for transfers between devices: 1.05 us -> 0.49 us  [on_device(): from_next = lax.ppermute(to_next, both, z_nexts)]
    pallas_call x1, Pallas kernels: 2.66 us -> 2.18 us  [on_device(): call(outer_rows_kernel, 'outer_rows', [VMEM] * 11 + [HBM], [VMEM] * 3 + [...]
    pallas_call x3 -> x4, Pallas kernels: 3.09 us -> 3.48 us  [the longest x1 2.28 us: on_device(): call(inner_rows_kernel, 'inner_rows', [VMEM] * 9, [VMEM] * 2 + [HBM] + [V...]
where the time goes in v3:
time: 42.4 us; the launch traced here: 42.2 us
  blocking collectives  26.1 us (62%)
  Pallas kernels  7.04 us (17%)
  starting transfers between devices  6.71 us (16%)
  local copies, waits for them, and re-layouts  1.12 us (3%)
  between operations  0.72 us (2%)
  waiting for transfers between devices  0.5 us (1%)
    all_to_all x1, blocking collectives, on_device(): lax.all_to_all(rows.reshape(devices, CAP + 1, 1, X), ('gy', 'gz'), split_...  26.1 us
    pallas_call x1, Pallas kernels, on_device(): call(inner_rows_kernel, 'inner_rows', [VMEM] * 9, [VMEM] * 2 + [HBM] + [V...  2.28 us
    pallas_call x1, Pallas kernels, on_device(): call(outer_rows_kernel, 'outer_rows', [VMEM] * 11 + [HBM], [VMEM] * 3 + [...  2.18 us
    ppermute x1, starting transfers between devices, on_device(): ends_pair = lax.ppermute(to_y_pair, both, y_pairs)  1.91 us
    ppermute x1, starting transfers between devices, on_device(): from_next = lax.ppermute(to_next, both, z_nexts)  1.7 us
    ppermute x1, starting transfers between devices, on_device(): from_pair = lax.ppermute(to_pair, both, z_pairs)  1.5 us
    ppermute x1, starting transfers between devices, on_device(): from_y_pair = lax.ppermute(to_y_pair, both, y_pairs)  1.38 us
    unnamed x10, local copies, waits for them, and re-layouts  1.12 us
  transfers between devices with their start and end apart: 6, of which 1 were waited for; matrix products, arithmetic and copies ran while one was open for 0% of the time, Pallas kernels for 8%

profile of v3, /device:TPU:1, one launch (start us, length us, event | category | flops | bytes accessed | tf_op | source)
XLA Modules:
  0.0 42.2 jit_solution(3649052200857018936)
XLA Ops:
  0.6 0.0 copy-start
  0.6 0.0 copy-start.1
  0.6 0.8 %copy-done.1 = f32[19,19]{1,0:T(8,128)S(1)} copy-done((f32[19,19]{1,0:T(8,128)S(1)}, f32[19,19]{1,0:T(8,128)}, u32[]{:S(2)}) %copy-start.1) | copy-done | bytes 1468
  1.5 0.6 %weights.1 = (f32[160,480]{1,0:T(8,128)S(1)}, f32[160,144]{1,0:T(8,128)S(1)}, f32[160,144]{1,0:T(8,128)S(1)}) custom-call(f32[19,19]{1,0:T(8,128)S(1)} %copy-done.1), custom_call_target="tpu_custom_call" | custom-call | flops 4000000000 | bytes 4000000 | tf_op jit(solution)/shard_map/weights/pallas_call | solution.py:505
  2.1 0.3 copy-done
  2.3 0.1 pack_z.1
  2.4 1.5 %collective-permute-start = (f32[152,128]{1,0:T(8,128)S(1)}, f32[152,128]{1,0:T(8,128)S(1)}, u32[]{:S(2)}, u32[]{:S(2)}) collective-permute-start(f32[152,128]{1,0:T(8,128)S(1)} %get-tuple-element.27), channel_id=1, source_target_pairs={{0,1},{1,0},{2,3},{3,2},{4,5},{5,4},{6,7},{7,6},{8,9},{9,8},{10,11... | collective-permute-start | bytes 233480 | tf_op jit(solution)/shard_map/ppermute | solution.py:514
  3.9 1.7 %collective-permute-start.1 = (f32[152,128]{1,0:T(8,128)S(1)}, f32[152,128]{1,0:T(8,128)S(1)}, u32[]{:S(2)}, u32[]{:S(2)}) collective-permute-start(f32[152,128]{1,0:T(8,128)S(1)} %get-tuple-element.28), channel_id=1, source_target_pairs={{0,8},{1,2},{2,1},{3,4},{4,3},{5,6},{6,5},{7,15},{8,0},{9,10},{10,... | collective-permute-start | bytes 233480 | tf_op jit(solution)/shard_map/ppermute | solution.py:515
  5.6 0.5 %bulk_rows.1 = (f32[19,10,48,128]{3,2,1,0:T(8,128)S(1)}, f32[19,10,48,128]{3,2,1,0:T(8,128)S(1)}, f32[320,128]{1,0:T(8,128)S(1)}, f32[320,128]{1,0:T(8,128)S(1)}) custom-call(f32[19,256,128]{2,1,0:T(8,128)S(1)} %bitcast.13, f32[160,480]{1,0:T(8,128)S(1)} %get-tuple-element.23.w, f32[8,128]{1,0:T(8,128)S(1)} %get-tuple-element.24.empty), custom_call_target="tpu_custom_call" | custom-call | tf_op jit(solution)/shard_map/bulk_rows/pallas_call | solution.py:517
  6.2 1.4 %collective-permute-start.2 = (f32[320,128]{1,0:T(8,128)S(1)}, f32[320,128]{1,0:T(8,128)S(1)}, u32[]{:S(2)}, u32[]{:S(2)}) collective-permute-start(f32[320,128]{1,0:T(8,128)S(1)} %get-tuple-element.34), channel_id=1, source_target_pairs={{0,8},{1,9},{2,10},{3,11},{4,12},{5,13},{6,14},{7,15},{8,0},{9,1},... | collective-permute-start | bytes 491528 | tf_op jit(solution)/shard_map/ppermute | solution.py:521
  7.5 0.0 collective-permute-start.3
  7.5 0.0 collective-permute-done.from_pair
  7.6 0.5 %collective-permute-done.1.from_next = f32[152,128]{1,0:T(8,128)S(1)} collective-permute-done((f32[152,128]{1,0:T(8,128)S(1)}, f32[152,128]{1,0:T(8,128)S(1)}, u32[]{:S(2)}, u32[]{:S(2)}) %collective-permute-start.1) | collective-permute-done | bytes 77856 | tf_op jit(solution)/shard_map/ppermute | solution.py:515
  8.0 0.0 copy-start.2
  8.0 0.0 copy-start.3
  8.0 0.0 copy-start.4
  8.0 0.5 %end_cells.1 = (f32[19,10,48,128]{3,2,1,0:T(8,128)S(1)}, f32[19,10,48,128]{3,2,1,0:T(8,128)S(1)}, f32[24,128]{1,0:T(8,128)S(1)}, f32[24,128]{1,0:T(8,128)S(1)}) custom-call(f32[19,10,48,128]{3,2,1,0:T(8,128)S(1)} %get-tuple-element.25.s0_in, f32[19,10,48,128]{3,2,1,0:T(8,128)S(1)} %get-tuple-element.26.s1_in, ...), custom_call_target="tpu_custom_call", output_to_operand_aliasing={{0}: (0, {}), {1}: (1, {})} | custom-call | tf_op jit(solution)/shard_map/end_cells/pallas_call | solution.py:523
  8.5 1.9 %collective-permute-start.4 = (f32[24,128]{1,0:T(8,128)S(1)}, f32[24,128]{1,0:T(8,128)S(1)}, u32[]{:S(2)}, u32[]{:S(2)}) collective-permute-start(f32[24,128]{1,0:T(8,128)S(1)} %get-tuple-element.36), channel_id=1, source_target_pairs={{0,8},{1,9},{2,10},{3,11},{4,12},{5,13},{6,14},{7,15},{8,0},{9,1},... | collective-permute-start | bytes 36872 | tf_op jit(solution)/shard_map/ppermute | solution.py:529
  10.4 0.2 collective-permute-start.5
  10.7 0.0 copy-done.2
  10.7 0.0 copy-done.3
  10.7 0.0 copy-done.4
  10.7 2.3 %inner_rows.1 = (f32[19,10,48,128]{3,2,1,0:T(8,128)S(1)}, f32[19,10,48,128]{3,2,1,0:T(8,128)S(1)}, f32[19,8,32,128]{3,2,1,0:T(8,128)}, f32[4864,128]{1,0:T(8,128...) custom-call(f32[19,10,48,128]{3,2,1,0:T(8,128)S(1)} %get-tuple-element.29., ...), custom_call_target="tpu_custom_call", output_to_operand_aliasing={{0}: (0, {}), {1}: (2, {})} | custom-call | flops 4000000000 | bytes 4000000 | tf_op jit(solution)/shard_map/inner_rows/pallas_call | solution.py:533
  13.0 0.0 collective-permute-done.4.ends_pair
  13.0 0.0 collective-permute-done.5.ends_next
  13.0 0.0 collective-permute-done.2.from_pair
  13.0 0.0 collective-permute-done.3.from_next
  13.0 2.2 %outer_rows.1 = (f32[19,10,48,128]{3,2,1,0:T(8,128)S(1)}, f32[4864,128]{1,0:T(8,128)S(1)}, f32[1152,1,128]{2,1,0:T(1,128)S(1)}, f32[19,8,32,128]{3,2,1,0:T(8,128)}) custom-call(f32[19,10,48,128]{3,2,1,0:T(8,128)S(1)} %get-tuple-element.33.s1_in, ...), custom_call_target="tpu_custom_call", output_to_operand_aliasing={{0}: (0, {}), {1}: (9, {}), {2}: (10, {}), {3}: (11, {})} | custom-call | tf_op jit(solution)/shard_map/outer_rows/pallas_call | solution.py:546
  15.2 26.1 %all_to_all.5 = f32[128,9,1,128]{3,2,1,0:T(1,128)S(1)} all-to-all(f32[128,9,1,128]{3,2,1,0:T(1,128)S(1)} %bitcast.15), channel_id=1, replica_groups=mesh['gy'=16,'gz'=8] {'gy','gz'}, dimensions={0} | all-to-all | bytes 1179648 | tf_op jit(solution)/shard_map/all_to_all | solution.py:559
  41.3 0.9 %sum_rows.1 = f32[64,128]{1,0:T(8,128)} custom-call(f32[1152,128]{1,0:T(8,128)S(1)} %bitcast.16), custom_call_target="tpu_custom_call" | custom-call | tf_op jit(solution)/shard_map/sum_rows/pallas_call | solution.py:562
Async XLA Ops:
  0.6 1.7 %copy-start = (f32[19,8,32,128]{3,2,1,0:T(8,128)S(1)}, f32[19,8,32,128]{3,2,1,0:T(8,128)}, u32[]{:S(2)}) copy-start(f32[19,8,32,128]{3,2,1,0:T(8,128)} %param.5) | copy-start | bytes 7471108
  0.6 0.9 %copy-start.1 = (f32[19,19]{1,0:T(8,128)S(1)}, f32[19,19]{1,0:T(8,128)}, u32[]{:S(2)}) copy-start(f32[19,19]{1,0:T(8,128)} %collision.1) | copy-start | bytes 4336
  2.4 5.1 %collective-permute-start = (f32[152,128]{1,0:T(8,128)S(1)}, f32[152,128]{1,0:T(8,128)S(1)}, u32[]{:S(2)}, u32[]{:S(2)}) collective-permute-start(f32[152,128]{1,0:T(8,128)S(1)} %get-tuple-element.27), channel_id=1, source_target_pairs={{0,1},{1,0},{2,3},{3,2},{4,5},{5,4},{6,7},{7,6},{8,9},{9,8},{10,11... | collective-permute-start | bytes 233480 | tf_op jit(solution)/shard_map/ppermute | solution.py:514
  3.9 4.1 %collective-permute-start.1 = (f32[152,128]{1,0:T(8,128)S(1)}, f32[152,128]{1,0:T(8,128)S(1)}, u32[]{:S(2)}, u32[]{:S(2)}) collective-permute-start(f32[152,128]{1,0:T(8,128)S(1)} %get-tuple-element.28), channel_id=1, source_target_pairs={{0,8},{1,2},{2,1},{3,4},{4,3},{5,6},{6,5},{7,15},{8,0},{9,10},{10,... | collective-permute-start | bytes 233480 | tf_op jit(solution)/shard_map/ppermute | solution.py:515
  6.2 6.8 %collective-permute-start.2 = (f32[320,128]{1,0:T(8,128)S(1)}, f32[320,128]{1,0:T(8,128)S(1)}, u32[]{:S(2)}, u32[]{:S(2)}) collective-permute-start(f32[320,128]{1,0:T(8,128)S(1)} %get-tuple-element.34), channel_id=1, source_target_pairs={{0,8},{1,9},{2,10},{3,11},{4,12},{5,13},{6,14},{7,15},{8,0},{9,1},... | collective-permute-start | bytes 491528 | tf_op jit(solution)/shard_map/ppermute | solution.py:521
  7.5 5.4 %collective-permute-start.3 = (f32[320,128]{1,0:T(8,128)S(1)}, f32[320,128]{1,0:T(8,128)S(1)}, u32[]{:S(2)}, u32[]{:S(2)}) collective-permute-start(f32[320,128]{1,0:T(8,128)S(1)} %get-tuple-element.35), channel_id=1, source_target_pairs={{0,1},{1,0},{2,3},{3,2},{4,5},{5,4},{6,7},{7,6},{8,16},{9,17},{10,... | collective-permute-start | bytes 491528 | tf_op jit(solution)/shard_map/ppermute | solution.py:522
  8.0 2.6 %copy-start.2 = (s32[1,128,8]{1,2,0:T(8,128)S(1)}, s32[1,128,8]{1,2,0:T(8,128)}, u32[]{:S(2)}) copy-start(s32[1,128,8]{1,2,0:T(8,128)} %param.9) | copy-start | bytes 12292
  8.0 2.6 %copy-start.3 = (s32[1,128,8]{1,2,0:T(8,128)S(1)}, s32[1,128,8]{1,2,0:T(8,128)}, u32[]{:S(2)}) copy-start(s32[1,128,8]{1,2,0:T(8,128)} %param.7) | copy-start | bytes 12292
  8.0 2.6 %copy-start.4 = (s32[1,128,8]{1,2,0:T(8,128)S(1)}, s32[1,128,8]{1,2,0:T(8,128)}, u32[]{:S(2)}) copy-start(s32[1,128,8]{1,2,0:T(8,128)} %param.8) | copy-start | bytes 12292
  8.5 4.4 %collective-permute-start.4 = (f32[24,128]{1,0:T(8,128)S(1)}, f32[24,128]{1,0:T(8,128)S(1)}, u32[]{:S(2)}, u32[]{:S(2)}) collective-permute-start(f32[24,128]{1,0:T(8,128)S(1)} %get-tuple-element.36), channel_id=1, source_target_pairs={{0,8},{1,9},{2,10},{3,11},{4,12},{5,13},{6,14},{7,15},{8,0},{9,1},... | collective-permute-start | bytes 36872 | tf_op jit(solution)/shard_map/ppermute | solution.py:529
  10.4 2.5 %collective-permute-start.5 = (f32[24,128]{1,0:T(8,128)S(1)}, f32[24,128]{1,0:T(8,128)S(1)}, u32[]{:S(2)}, u32[]{:S(2)}) collective-permute-start(f32[24,128]{1,0:T(8,128)S(1)} %get-tuple-element.37), channel_id=1, source_target_pairs={{0,1},{1,0},{2,3},{3,2},{4,5},{5,4},{6,7},{7,6},{8,16},{9,17},{10,... | collective-permute-start | bytes 36872 | tf_op jit(solution)/shard_map/ppermute | solution.py:530

commit v4 on v3

--- a/solution.py
+++ b/solution.py
@@ -56,6 +56,7 @@
 CORNERS = 20
 END_ROWS = 24
 Z_ROWS = 8 * Q
+PAIR = 1 << 13
 K1 = QP * 8
 K2 = 6 * 8
 
@@ -309,7 +310,8 @@
     copy.start()
     numbers[...] = jnp.zeros((numbers.shape[0], X), f32)
     numbers[:, 0:CAP] = panel[...].astype(f32).T
-    pick[...] = direction[...] * (CY * CZ) + cell[...]
+    place = direction[...] * (CY * CZ) + cell[...]
+    pick[...] = place[: CAP // 2] + place[CAP // 2 :] * PAIR
 
     @pl.loop(0, numbers.shape[0], unroll=8)
     def _(d):
@@ -338,71 +340,132 @@
     copy.wait()
 
 
-def outer_rows_kernel(
-    s1_in, w, w_up, w_down, from_pair, from_next, ends_pair, ends_next, pick_in, scaled_in,
+def sides_of(iy, w_up, w_down):
+    return (
+        (CY - 1, CY, Y_UP, w_up, iy < lax.axis_size("gy") - 1),
+        (0, -1, Y_DOWN, w_down, iy > 0),
+    )
+
+
+def take_arrivals(iy, sides, take, from_pair, from_next):
+    odd = lax.rem(iy, 2)
+    for side in range(2):
+        valid = sides[side][-1]
+        pl.when(jnp.logical_and(valid, odd == side))(functools.partial(take, side, from_pair))
+        pl.when(jnp.logical_and(valid, odd != side))(functools.partial(take, side, from_next))
+
+
+def store_mixed(mixed, q, y, k, tiles, kept, scaled):
+    for c, t in enumerate(tiles):
+        value = mixed[8 * q : 8 * q + 8, X * c : X * c + X]
+        kept[q, k, 8 * t : 8 * t + 8, :] = value
+        at = q * (CY * CZ) + y * CZ + 8 * t
+        scaled[at : at + 8, :] = value * LINK_WEIGHTS[q]
+
+
+def read_tiles(ref, y, tiles):
+    return stacked(
+        [
+            [ref[p, y + 1 + DIRS[p][1], pl.ds(Z0 + 8 * t + DIRS[p][2], 8), :] for t in tiles]
+            for p in range(Q)
+        ]
+        + [None]
+    )
+
+
+MIDDLE = tuple(range(1, CZ // 8 - 1))
+OUTER = (0, CZ // 8 - 1)
+
+
+def middle_tiles_kernel(
+    s1_in, w, w_up, w_down, from_pair, from_next, scaled_in, s1, scaled, raw, kept
+):
+    del s1_in, scaled_in
+    iy = lax.axis_index("gy")
+    weights = w[...].astype(bf16)
+    cells = lax.broadcasted_iota(jnp.int32, (8, X), 0)
+    sides = sides_of(iy, w_up, w_down)
+    raw[...] = jnp.zeros((2, 5, ROWS, X), f32)
+
+    def take(side, bulk):
+        _, halo, channels, _, _ = sides[side]
+        for i, q in enumerate(channels):
+            raw[side, i, Z0 : Z0 + CZ, :] = bulk[RAW + CZ * i : RAW + CZ * i + CZ, :]
+            for t in range(CZ // 8):
+                value = bulk[MIXED + CZ * i + 8 * t : MIXED + CZ * i + 8 * t + 8, :]
+                if t == 0:
+                    value = jnp.where(cells > 0, value, 0.0)
+                if t == CZ // 8 - 1:
+                    value = jnp.where(cells < 7, value, 0.0)
+                s1[q, 1 + halo, Z0 + 8 * t : Z0 + 8 * t + 8, :] += value
+
+    take_arrivals(iy, sides, take, from_pair, from_next)
+    for side, (y, _, channels, part, _) in enumerate(sides):
+        tiles = [
+            line_tiles(raw[side, i, pl.ds(Z0 + DIRS[p][2], CZ), :])
+            for i, p in enumerate(channels)
+        ]
+        mixed = mix(part[...].astype(bf16), stacked(tiles + [None]))
+        for q in range(Q):
+            for t in range(CZ // 8):
+                s1[q, 1 + y, Z0 + 8 * t : Z0 + 8 * t + 8, :] += along_x(
+                    mixed[8 * q : 8 * q + 8, X * t : X * t + X], q
+                )
+    for k, y in enumerate(EDGE_ROWS):
+        mixed = mix(weights, read_tiles(s1, y, MIDDLE))
+        for q in range(Q):
+            store_mixed(mixed, q, y, k, MIDDLE, kept, scaled)
+
+
+def outer_tiles_kernel(
+    s1_in, w, w_up, w_down, ends_pair, ends_next, pick_in, scaled_in, raw_in, kept_in,
     rows_in, out_in,
-    s1, scaled, rows, out, kept, raw, spare, pick, pick_sem, out_sem,
+    s1, scaled, raw, kept, rows, out, spare, pick, pick_sem, out_sem,
 ):
-    del s1_in, scaled_in, rows_in, out_in
+    del s1_in, scaled_in, raw_in, kept_in, rows_in, out_in
     fetch = pltpu.make_async_copy(pick_in, pick, pick_sem)
     fetch.start()
     iy = lax.axis_index("gy")
     iz = lax.axis_index("gz")
     weights = w[...].astype(bf16)
     z_ok = (iz > 0, iz < lax.axis_size("gz") - 1)
-    first = lax.broadcasted_iota(jnp.int32, (8, X), 0) == 0
-    final = lax.broadcasted_iota(jnp.int32, (8, X), 0) == 7
+    sides = sides_of(iy, w_up, w_down)
     spare[...] = jnp.zeros((2, K2, X), f32)
-    sides = (
-        (0, CY - 1, CY, Y_UP, w_up, iy < lax.axis_size("gy") - 1),
-        (1, 0, -1, Y_DOWN, w_down, iy > 0),
-    )
-
-    def take(side, bulk, ends):
-        _, _, halo, channels, _, _ = sides[side]
+
+    def take(side, ends):
+        _, halo, channels, _, _ = sides[side]
         for i, q in enumerate(channels):
             cz = DIRS[q][2]
-            raw[side, i, Z0 : Z0 + CZ, :] = bulk[RAW + CZ * i : RAW + CZ * i + CZ, :]
             for e, z in enumerate(RAW_CELLS[cz]):
                 raw[side, i, pl.ds(Z0 + z, 1), :] = ends[pl.ds(RAW_ENDS + 2 * i + e, 1), :]
-            for t in range(CZ // 8):
-                value = bulk[MIXED + CZ * i + 8 * t : MIXED + CZ * i + 8 * t + 8, :]
-                at = MIXED_ENDS + 2 * i
-                if t == 0:
-                    value = jnp.where(first, ends[at : at + 1, :], value)
-                if t == CZ // 8 - 1:
-                    value = jnp.where(final, ends[at + 1 : at + 2, :], value)
-                s1[q, 1 + halo, Z0 + 8 * t : Z0 + 8 * t + 8, :] += value
+            for e, z in enumerate((0, CZ - 1)):
+                at = pl.ds(MIXED_ENDS + 2 * i + e, 1)
+                s1[q, 1 + halo, pl.ds(Z0 + z, 1), :] += ends[at, :]
             if cz:
                 z, e = (CZ, 0) if cz > 0 else (-1, 1)
                 s1[q, 1 + halo, pl.ds(Z0 + z, 1), :] += ends[CORNERS + e : CORNERS + e + 1, :]
 
-    odd = lax.rem(iy, 2)
-    for side, (_, _, _, _, _, valid) in enumerate(sides):
-        pl.when(jnp.logical_and(valid, odd == side))(
-            functools.partial(take, side, from_pair, ends_pair)
-        )
-        pl.when(jnp.logical_and(valid, odd != side))(
-            functools.partial(take, side, from_next, ends_next)
-        )
-
-        @pl.when(jnp.logical_not(valid))
-        def _(side=side):
-            raw[side] = jnp.zeros((5, ROWS, X), f32)
-
-    for side, y, halo, channels, part, valid in sides:
-        reads = five_lines(raw.at[side], spare.at[side], lambda i, p: (i,), channels)
-        mixed = mix(part[...].astype(bf16), reads)
+    take_arrivals(iy, sides, take, ends_pair, ends_next)
+    for side, (y, _, channels, part, _) in enumerate(sides):
+        for i, p in enumerate(channels):
+            cz = DIRS[p][2]
+            wanted = [(2, cz - 1), (3, CZ + cz)]
+            if cz < 0:
+                wanted.append((0, -1))
+            if cz > 0:
+                wanted.append((1, CZ))
+            for j, z in wanted:
+                spare[side, pl.ds(8 * i + j, 1), :] = raw[side, i, pl.ds(Z0 + z, 1), :]
+        mixed = mix(part[...].astype(bf16), spare[side])
         for q in range(Q):
-            for t in range(CZ // 8):
-                at = pl.ds(Z0 + 8 * t, 8)
-                s1[q, 1 + y, at, :] += along_x(mixed[8 * q : 8 * q + 8, X * t : X * t + X], q)
             cz = DIRS[q][2]
+            value = along_x(mixed[8 * q : 8 * q + 8, :], q)
+            for j, z in ((0, 0), (1, CZ - 1)):
+                s1[q, 1 + y, pl.ds(Z0 + z, 1), :] += value[j : j + 1, :]
             if cz:
-                row = 0 if cz < 0 else 1
-                end = along_x(mixed[8 * q : 8 * q + 8, X * (CZ // 8) :], q)[row : row + 1, :]
-                at = pl.ds(Z0 - 1 if cz < 0 else Z0 + CZ, 1)
-                s1[q, 1 + y, at, :] += jnp.where(z_ok[row], end, 0.0)
+                j, z = (2, -1) if cz < 0 else (3, CZ)
+                value = jnp.where(z_ok[j - 2], value[j : j + 1, :], 0.0)
+                s1[q, 1 + y, pl.ds(Z0 + z, 1), :] += value
 
     copies = [
         pltpu.make_async_copy(
@@ -410,22 +473,20 @@
         )
         for h in range(2)
     ]
-    for k, y in enumerate((0, 1, CY - 2, CY - 1)):
-        mixed = mix(weights, read_row(s1, y))
+    for k, y in enumerate(EDGE_ROWS):
+        mixed = mix(weights, read_tiles(s1, y, OUTER))
         for q in range(Q):
-            for t in range(CZ // 8):
-                value = mixed[8 * q : 8 * q + 8, X * t : X * t + X]
-                kept[q, k, 8 * t : 8 * t + 8, :] = value
-                at = q * (CY * CZ) + y * CZ + 8 * t
-                scaled[at : at + 8, :] = value * LINK_WEIGHTS[q]
+            store_mixed(mixed, q, y, k, OUTER, kept, scaled)
         if k % 2:
             copies[k // 2].start()
     fetch.wait()
 
     @pl.loop(0, pick.shape[1], unroll=8)
     def _(d):
-        for k in range(CAP):
-            rows[pl.ds(d * (CAP + 1) + k, 1), 0, :] = scaled[pl.ds(pick[k, d], 1), :]
+        for k in range(CAP // 2):
+            places = pick[k, d]
+            for j, at in ((k, places & (PAIR - 1)), (k + CAP // 2, places >> 13)):
+                rows[pl.ds(d * (CAP + 1) + j, 1), 0, :] = scaled[pl.ds(at, 1), :]
 
     for copy in copies:
         copy.wait()
@@ -533,7 +594,7 @@
     _, s1, out, scaled, rows, pick = call(
         inner_rows_kernel, "inner_rows", [VMEM] * 9, [VMEM] * 2 + [HBM] + [VMEM] * 3,
         [(pad, f32), (pad, f32), (own, f32), table]
-        + [message, ((CAP, devices), jnp.int32)],
+        + [message, ((CAP // 2, devices), jnp.int32)],
         scratch=[
             pltpu.VMEM((Q, CY - 4, CZ, X), f32),
             pltpu.VMEM((2, K2, X), f32),
@@ -543,19 +604,25 @@
         cost=4_000_000_000,
         aliases={0: 0, 2: 1},
     )(s0, w, s1, w_up, w_down, flat, link_panel[0].T, link_cell[0].T, link_dir[0].T)
-    _, _, rows, out = call(
-        outer_rows_kernel, "outer_rows", [VMEM] * 11 + [HBM], [VMEM] * 3 + [HBM],
-        [(pad, f32), table, message, (own, f32)],
+    edge = ((Q, 4, CZ, X), f32)
+    lines = ((2, 5, ROWS, X), f32)
+    s1, scaled, raw, kept = call(
+        middle_tiles_kernel, "middle_tiles", [VMEM] * 7, [VMEM] * 4,
+        [(pad, f32), table, lines, edge],
+        aliases={0: 0, 6: 1},
+        cost=1_000_000_000,
+    )(s1, w, w_up, w_down, from_y_pair, from_y_next, scaled)
+    _, _, _, _, rows, out = call(
+        outer_tiles_kernel, "outer_tiles", [VMEM] * 11 + [HBM], [VMEM] * 5 + [HBM],
+        [(pad, f32), table, lines, edge, message, (own, f32)],
         scratch=[
-            pltpu.VMEM((Q, 4, CZ, X), f32),
-            pltpu.VMEM((2, 5, ROWS, X), f32),
             pltpu.VMEM((2, K2, X), f32),
-            pltpu.SMEM((CAP, devices), jnp.int32),
+            pltpu.SMEM((CAP // 2, devices), jnp.int32),
             dma,
             dma((2,)),
         ],
-        aliases={0: 0, 9: 1, 10: 2, 11: 3},
-    )(s1, w, w_up, w_down, from_y_pair, from_y_next, ends_pair, ends_next, pick, scaled, rows, out)
+        aliases={0: 0, 7: 1, 8: 2, 9: 3, 10: 4, 11: 5},
+    )(s1, w, w_up, w_down, ends_pair, ends_next, pick, scaled, raw, kept, rows, out)
     arrived = lax.all_to_all(
         rows.reshape(devices, CAP + 1, 1, X), ("gy", "gz"), split_axis=0, concat_axis=0, tiled=True
     )

time: 42.4 us -> 42.5 us (level)
    pallas_call x1 -> x2, Pallas kernels: 2.18 us -> 2.48 us  [the longest x1 1.79 us: on_device(): call(outer_tiles_kernel, 'outer_tiles', [VMEM] * 11 + [HBM], [VMEM] * 5 +...]
  transfers between devices with their start and end apart: 6 -> 6, of which waited for: 1 -> 1; matrix products, arithmetic and copies ran while one was open for 0% -> 0% of each run, Pallas kernels for 8% -> 9%
where the time goes in v4:
time: 42.5 us; the launch traced here: 42.4 us
  blocking collectives  26 us (61%)
  Pallas kernels  7.34 us (17%)
  starting transfers between devices  6.71 us (16%)
  local copies, waits for them, and re-layouts  1.12 us (3%)
  between operations  0.72 us (2%)
  waiting for transfers between devices  0.5 us (1%)
    all_to_all x1, blocking collectives, on_device(): lax.all_to_all(rows.reshape(devices, CAP + 1, 1, X), ('gy', 'gz'), split_...  26 us
    pallas_call x1, Pallas kernels, on_device(): call(inner_rows_kernel, 'inner_rows', [VMEM] * 9, [VMEM] * 2 + [HBM] + [V...  2.28 us
    ppermute x1, starting transfers between devices, on_device(): ends_pair = lax.ppermute(to_y_pair, both, y_pairs)  1.91 us
    pallas_call x1, Pallas kernels, on_device(): call(outer_tiles_kernel, 'outer_tiles', [VMEM] * 11 + [HBM], [VMEM] * 5 +...  1.79 us
    ppermute x1, starting transfers between devices, on_device(): from_next = lax.ppermute(to_next, both, z_nexts)  1.7 us
    ppermute x1, starting transfers between devices, on_device(): from_pair = lax.ppermute(to_pair, both, z_pairs)  1.5 us
    ppermute x1, starting transfers between devices, on_device(): from_y_pair = lax.ppermute(to_y_pair, both, y_pairs)  1.38 us
    unnamed x10, local copies, waits for them, and re-layouts  1.12 us
  transfers between devices with their start and end apart: 6, of which 1 were waited for; matrix products, arithmetic and copies ran while one was open for 0% of the time, Pallas kernels for 9%

profile of v4, /device:TPU:1, one launch (start us, length us, event | category | flops | bytes accessed | tf_op | source)
XLA Modules:
  0.0 42.4 jit_solution(3116867068850005593)
XLA Ops:
  0.6 0.0 copy-start
  0.6 0.0 copy-start.1
  0.6 0.8 %copy-done.1 = f32[19,19]{1,0:T(8,128)S(1)} copy-done((f32[19,19]{1,0:T(8,128)S(1)}, f32[19,19]{1,0:T(8,128)}, u32[]{:S(2)}) %copy-start.1) | copy-done | bytes 1468
  1.5 0.6 %weights.1 = (f32[160,480]{1,0:T(8,128)S(1)}, f32[160,144]{1,0:T(8,128)S(1)}, f32[160,144]{1,0:T(8,128)S(1)}) custom-call(f32[19,19]{1,0:T(8,128)S(1)} %copy-done.1), custom_call_target="tpu_custom_call" | custom-call | flops 4000000000 | bytes 4000000 | tf_op jit(solution)/shard_map/weights/pallas_call | solution.py:566
  2.1 0.3 copy-done
  2.3 0.1 pack_z.1
  2.4 1.5 %collective-permute-start = (f32[152,128]{1,0:T(8,128)S(1)}, f32[152,128]{1,0:T(8,128)S(1)}, u32[]{:S(2)}, u32[]{:S(2)}) collective-permute-start(f32[152,128]{1,0:T(8,128)S(1)} %get-tuple-element.31), channel_id=1, source_target_pairs={{0,1},{1,0},{2,3},{3,2},{4,5},{5,4},{6,7},{7,6},{8,9},{9,8},{10,11... | collective-permute-start | bytes 233480 | tf_op jit(solution)/shard_map/ppermute | solution.py:575
  3.9 1.7 %collective-permute-start.1 = (f32[152,128]{1,0:T(8,128)S(1)}, f32[152,128]{1,0:T(8,128)S(1)}, u32[]{:S(2)}, u32[]{:S(2)}) collective-permute-start(f32[152,128]{1,0:T(8,128)S(1)} %get-tuple-element.32), channel_id=1, source_target_pairs={{0,8},{1,2},{2,1},{3,4},{4,3},{5,6},{6,5},{7,15},{8,0},{9,10},{10,... | collective-permute-start | bytes 233480 | tf_op jit(solution)/shard_map/ppermute | solution.py:576
  5.6 0.5 %bulk_rows.1 = (f32[19,10,48,128]{3,2,1,0:T(8,128)S(1)}, f32[19,10,48,128]{3,2,1,0:T(8,128)S(1)}, f32[320,128]{1,0:T(8,128)S(1)}, f32[320,128]{1,0:T(8,128)S(1)}) custom-call(f32[19,256,128]{2,1,0:T(8,128)S(1)} %bitcast.13, f32[160,480]{1,0:T(8,128)S(1)} %get-tuple-element.27.w, f32[8,128]{1,0:T(8,128)S(1)} %get-tuple-element.28.empty), custom_call_target="tpu_custom_call" | custom-call | tf_op jit(solution)/shard_map/bulk_rows/pallas_call | solution.py:578
  6.2 1.4 %collective-permute-start.2 = (f32[320,128]{1,0:T(8,128)S(1)}, f32[320,128]{1,0:T(8,128)S(1)}, u32[]{:S(2)}, u32[]{:S(2)}) collective-permute-start(f32[320,128]{1,0:T(8,128)S(1)} %get-tuple-element.38), channel_id=1, source_target_pairs={{0,8},{1,9},{2,10},{3,11},{4,12},{5,13},{6,14},{7,15},{8,0},{9,1},... | collective-permute-start | bytes 491528 | tf_op jit(solution)/shard_map/ppermute | solution.py:582
  7.5 0.0 collective-permute-start.3
  7.5 0.0 collective-permute-done.from_pair
  7.6 0.5 %collective-permute-done.1.from_next = f32[152,128]{1,0:T(8,128)S(1)} collective-permute-done((f32[152,128]{1,0:T(8,128)S(1)}, f32[152,128]{1,0:T(8,128)S(1)}, u32[]{:S(2)}, u32[]{:S(2)}) %collective-permute-start.1) | collective-permute-done | bytes 77856 | tf_op jit(solution)/shard_map/ppermute | solution.py:576
  8.0 0.0 copy-start.2
  8.0 0.0 copy-start.3
  8.0 0.0 copy-start.4
  8.0 0.5 %end_cells.1 = (f32[19,10,48,128]{3,2,1,0:T(8,128)S(1)}, f32[19,10,48,128]{3,2,1,0:T(8,128)S(1)}, f32[24,128]{1,0:T(8,128)S(1)}, f32[24,128]{1,0:T(8,128)S(1)}) custom-call(f32[19,10,48,128]{3,2,1,0:T(8,128)S(1)} %get-tuple-element.29.s0_in, f32[19,10,48,128]{3,2,1,0:T(8,128)S(1)} %get-tuple-element.30.s1_in, ...), custom_call_target="tpu_custom_call", output_to_operand_aliasing={{0}: (0, {}), {1}: (1, {})} | custom-call | tf_op jit(solution)/shard_map/end_cells/pallas_call | solution.py:584
  8.5 1.9 %collective-permute-start.4 = (f32[24,128]{1,0:T(8,128)S(1)}, f32[24,128]{1,0:T(8,128)S(1)}, u32[]{:S(2)}, u32[]{:S(2)}) collective-permute-start(f32[24,128]{1,0:T(8,128)S(1)} %get-tuple-element.42), channel_id=1, source_target_pairs={{0,8},{1,9},{2,10},{3,11},{4,12},{5,13},{6,14},{7,15},{8,0},{9,1},... | collective-permute-start | bytes 36872 | tf_op jit(solution)/shard_map/ppermute | solution.py:590
  10.4 0.2 collective-permute-start.5
  10.7 0.0 copy-done.2
  10.7 0.0 copy-done.3
  10.7 0.0 copy-done.4
  10.7 2.3 %inner_rows.1 = (f32[19,10,48,128]{3,2,1,0:T(8,128)S(1)}, f32[19,10,48,128]{3,2,1,0:T(8,128)S(1)}, f32[19,8,32,128]{3,2,1,0:T(8,128)}, f32[4864,128]{1,0:T(8,128...) custom-call(f32[19,10,48,128]{3,2,1,0:T(8,128)S(1)} %get-tuple-element.33., ...), custom_call_target="tpu_custom_call", output_to_operand_aliasing={{0}: (0, {}), {1}: (2, {})} | custom-call | flops 4000000000 | bytes 4000000 | tf_op jit(solution)/shard_map/inner_rows/pallas_call | solution.py:594
  13.0 0.0 collective-permute-done.2.from_pair
  13.0 0.0 collective-permute-done.3.from_next
  13.0 0.7 %middle_tiles.1 = (f32[19,10,48,128]{3,2,1,0:T(8,128)S(1)}, f32[4864,128]{1,0:T(8,128)S(1)}, f32[2,5,48,128]{3,2,1,0:T(8,128)S(1)}, f32[19,4,32,128]{3,2,1,0:T(8,128)S(1)}) custom-call(f32[19,10,48,128]{3,2,1,0:T(8,128)S(1)} %get-tuple-element.37.s1_in, f32[160,480]{1,0:T(8,128)S(1)} %get-tuple-element.27.w, ...), custom_call_target="tpu_custom_call", output_to_operand_aliasing={{0}: (0, {}), {1}: (6, {})} | custom-call | flops 1000000000 | bytes 1000000 | tf_op jit(solution)/shard_map/middle_tiles/pallas_call | solution.py:609
  13.7 0.0 collective-permute-done.4.ends_pair
  13.7 0.0 collective-permute-done.5.ends_next
  13.7 1.8 %outer_tiles.1 = (f32[19,10,48,128]{3,2,1,0:T(8,128)S(1)}, f32[4864,128]{1,0:T(8,128)S(1)}, f32[2,5,48,128]{3,2,1,0:T(8,128)S(1)}, f32[19,4,32,128]{3,2,1,0:T(8,...) custom-call(f32[19,10,48,128]{3,2,1,0:T(8,128)S(1)} %get-tuple-eleme, ...), custom_call_target="tpu_custom_call", output_to_operand_aliasing={{0}: (0, {}), {1}: (7, {}), {2}: (8, {}), {3}: (9, {}), {4}... | custom-call | tf_op jit(solution)/shard_map/outer_tiles/pallas_call | solution.py:615
  15.5 26.0 %all_to_all.5 = f32[128,9,1,128]{3,2,1,0:T(1,128)S(1)} all-to-all(f32[128,9,1,128]{3,2,1,0:T(1,128)S(1)} %bitcast.15), channel_id=1, replica_groups=mesh['gy'=16,'gz'=8] {'gy','gz'}, dimensions={0} | all-to-all | bytes 1179648 | tf_op jit(solution)/shard_map/all_to_all | solution.py:626
  41.5 0.9 %sum_rows.1 = f32[64,128]{1,0:T(8,128)} custom-call(f32[1152,128]{1,0:T(8,128)S(1)} %bitcast.16), custom_call_target="tpu_custom_call" | custom-call | tf_op jit(solution)/shard_map/sum_rows/pallas_call | solution.py:629
Async XLA Ops:
  0.6 1.7 %copy-start = (f32[19,8,32,128]{3,2,1,0:T(8,128)S(1)}, f32[19,8,32,128]{3,2,1,0:T(8,128)}, u32[]{:S(2)}) copy-start(f32[19,8,32,128]{3,2,1,0:T(8,128)} %param.5) | copy-start | bytes 7471108
  0.6 0.9 %copy-start.1 = (f32[19,19]{1,0:T(8,128)S(1)}, f32[19,19]{1,0:T(8,128)}, u32[]{:S(2)}) copy-start(f32[19,19]{1,0:T(8,128)} %collision.1) | copy-start | bytes 4336
  2.4 5.1 %collective-permute-start = (f32[152,128]{1,0:T(8,128)S(1)}, f32[152,128]{1,0:T(8,128)S(1)}, u32[]{:S(2)}, u32[]{:S(2)}) collective-permute-start(f32[152,128]{1,0:T(8,128)S(1)} %get-tuple-element.31), channel_id=1, source_target_pairs={{0,1},{1,0},{2,3},{3,2},{4,5},{5,4},{6,7},{7,6},{8,9},{9,8},{10,11... | collective-permute-start | bytes 233480 | tf_op jit(solution)/shard_map/ppermute | solution.py:575
  3.9 4.1 %collective-permute-start.1 = (f32[152,128]{1,0:T(8,128)S(1)}, f32[152,128]{1,0:T(8,128)S(1)}, u32[]{:S(2)}, u32[]{:S(2)}) collective-permute-start(f32[152,128]{1,0:T(8,128)S(1)} %get-tuple-element.32), channel_id=1, source_target_pairs={{0,8},{1,2},{2,1},{3,4},{4,3},{5,6},{6,5},{7,15},{8,0},{9,10},{10,... | collective-permute-start | bytes 233480 | tf_op jit(solution)/shard_map/ppermute | solution.py:576
  6.2 6.8 %collective-permute-start.2 = (f32[320,128]{1,0:T(8,128)S(1)}, f32[320,128]{1,0:T(8,128)S(1)}, u32[]{:S(2)}, u32[]{:S(2)}) collective-permute-start(f32[320,128]{1,0:T(8,128)S(1)} %get-tuple-element.38), channel_id=1, source_target_pairs={{0,8},{1,9},{2,10},{3,11},{4,12},{5,13},{6,14},{7,15},{8,0},{9,1},... | collective-permute-start | bytes 491528 | tf_op jit(solution)/shard_map/ppermute | solution.py:582
  7.5 5.4 %collective-permute-start.3 = (f32[320,128]{1,0:T(8,128)S(1)}, f32[320,128]{1,0:T(8,128)S(1)}, u32[]{:S(2)}, u32[]{:S(2)}) collective-permute-start(f32[320,128]{1,0:T(8,128)S(1)} %get-tuple-element.39), channel_id=1, source_target_pairs={{0,1},{1,0},{2,3},{3,2},{4,5},{5,4},{6,7},{7,6},{8,16},{9,17},{10,... | collective-permute-start | bytes 491528 | tf_op jit(solution)/shard_map/ppermute | solution.py:583
  8.0 2.6 %copy-start.2 = (s32[1,128,8]{1,2,0:T(8,128)S(1)}, s32[1,128,8]{1,2,0:T(8,128)}, u32[]{:S(2)}) copy-start(s32[1,128,8]{1,2,0:T(8,128)} %param.9) | copy-start | bytes 12292
  8.0 2.6 %copy-start.3 = (s32[1,128,8]{1,2,0:T(8,128)S(1)}, s32[1,128,8]{1,2,0:T(8,128)}, u32[]{:S(2)}) copy-start(s32[1,128,8]{1,2,0:T(8,128)} %param.7) | copy-start | bytes 12292
  8.0 2.6 %copy-start.4 = (s32[1,128,8]{1,2,0:T(8,128)S(1)}, s32[1,128,8]{1,2,0:T(8,128)}, u32[]{:S(2)}) copy-start(s32[1,128,8]{1,2,0:T(8,128)} %param.8) | copy-start | bytes 12292
  8.5 5.1 %collective-permute-start.4 = (f32[24,128]{1,0:T(8,128)S(1)}, f32[24,128]{1,0:T(8,128)S(1)}, u32[]{:S(2)}, u32[]{:S(2)}) collective-permute-start(f32[24,128]{1,0:T(8,128)S(1)} %get-tuple-element.42), channel_id=1, source_target_pairs={{0,8},{1,9},{2,10},{3,11},{4,12},{5,13},{6,14},{7,15},{8,0},{9,1},... | collective-permute-start | bytes 36872 | tf_op jit(solution)/shard_map/ppermute | solution.py:590
  10.4 3.2 %collective-permute-start.5 = (f32[24,128]{1,0:T(8,128)S(1)}, f32[24,128]{1,0:T(8,128)S(1)}, u32[]{:S(2)}, u32[]{:S(2)}) collective-permute-start(f32[24,128]{1,0:T(8,128)S(1)} %get-tuple-element.43), channel_id=1, source_target_pairs={{0,1},{1,0},{2,3},{3,2},{4,5},{5,4},{6,7},{7,6},{8,16},{9,17},{10,... | collective-permute-start | bytes 36872 | tf_op jit(solution)/shard_map/ppermute | solution.py:591

commit v5 on v3

--- a/solution.py
+++ b/solution.py
@@ -56,6 +56,7 @@
 CORNERS = 20
 END_ROWS = 24
 Z_ROWS = 8 * Q
+PAIR = 1 << 13
 K1 = QP * 8
 K2 = 6 * 8
 
@@ -309,7 +310,8 @@
     copy.start()
     numbers[...] = jnp.zeros((numbers.shape[0], X), f32)
     numbers[:, 0:CAP] = panel[...].astype(f32).T
-    pick[...] = direction[...] * (CY * CZ) + cell[...]
+    place = direction[...] * (CY * CZ) + cell[...]
+    pick[...] = place[: CAP // 2] + place[CAP // 2 :] * PAIR
 
     @pl.loop(0, numbers.shape[0], unroll=8)
     def _(d):
@@ -339,7 +341,7 @@
 
 
 def outer_rows_kernel(
-    s1_in, w, w_up, w_down, from_pair, from_next, ends_pair, ends_next, pick_in, scaled_in,
+    s1_in, w, w_up, w_down, from_next, from_pair, ends_next, ends_pair, pick_in, scaled_in,
     rows_in, out_in,
     s1, scaled, rows, out, kept, raw, spare, pick, pick_sem, out_sem,
 ):
@@ -424,8 +426,10 @@
 
     @pl.loop(0, pick.shape[1], unroll=8)
     def _(d):
-        for k in range(CAP):
-            rows[pl.ds(d * (CAP + 1) + k, 1), 0, :] = scaled[pl.ds(pick[k, d], 1), :]
+        for k in range(CAP // 2):
+            places = pick[k, d]
+            for j, at in ((k, places & (PAIR - 1)), (k + CAP // 2, places >> 13)):
+                rows[pl.ds(d * (CAP + 1) + j, 1), 0, :] = scaled[pl.ds(at, 1), :]
 
     for copy in copies:
         copy.wait()
@@ -533,7 +537,7 @@
     _, s1, out, scaled, rows, pick = call(
         inner_rows_kernel, "inner_rows", [VMEM] * 9, [VMEM] * 2 + [HBM] + [VMEM] * 3,
         [(pad, f32), (pad, f32), (own, f32), table]
-        + [message, ((CAP, devices), jnp.int32)],
+        + [message, ((CAP // 2, devices), jnp.int32)],
         scratch=[
             pltpu.VMEM((Q, CY - 4, CZ, X), f32),
             pltpu.VMEM((2, K2, X), f32),
@@ -550,12 +554,12 @@
             pltpu.VMEM((Q, 4, CZ, X), f32),
             pltpu.VMEM((2, 5, ROWS, X), f32),
             pltpu.VMEM((2, K2, X), f32),
-            pltpu.SMEM((CAP, devices), jnp.int32),
+            pltpu.SMEM((CAP // 2, devices), jnp.int32),
             dma,
             dma((2,)),
         ],
         aliases={0: 0, 9: 1, 10: 2, 11: 3},
-    )(s1, w, w_up, w_down, from_y_pair, from_y_next, ends_pair, ends_next, pick, scaled, rows, out)
+    )(s1, w, w_up, w_down, from_y_next, from_y_pair, ends_next, ends_pair, pick, scaled, rows, out)
     arrived = lax.all_to_all(
         rows.reshape(devices, CAP + 1, 1, X), ("gy", "gz"), split_axis=0, concat_axis=0, tiled=True
     )

time: 42.4 us -> 41.5 us (0.979)
  blocking collectives: 26.1 us -> 24.7 us
  starting transfers between devices: 6.71 us -> 7.82 us
  waiting for transfers between devices: 0.5 us -> 0.03 us
    all_to_all x1, blocking collectives: 26.1 us -> 24.7 us  [on_device(): lax.all_to_all(rows.reshape(devices, CAP + 1, 1, X), ('gy', 'gz'), split_...]
    ppermute x1, starting transfers between devices: 1.38 us -> 2.54 us  [on_device(): from_y_pair = lax.ppermute(to_y_pair, both, y_pairs)]
    ppermute x1, waiting for transfers between devices: 0.49 us -> 0.01 us  [on_device(): from_next = lax.ppermute(to_next, both, z_nexts)]
  transfers between devices with their start and end apart: 6 -> 6, of which waited for: 1 -> 0; matrix products, arithmetic and copies ran while one was open for 0% -> 0% of each run, Pallas kernels for 8% -> 8%
where the time goes in v5:
time: 41.5 us; the launch traced here: 41.3 us
  blocking collectives  24.7 us (60%)
  starting transfers between devices  7.82 us (19%)
  Pallas kernels  6.93 us (17%)
  local copies, waits for them, and re-layouts  1.13 us (3%)
  between operations  0.71 us (2%)
    all_to_all x1, blocking collectives, on_device(): lax.all_to_all(rows.reshape(devices, CAP + 1, 1, X), ('gy', 'gz'), split_...  24.7 us
    ppermute x1, starting transfers between devices, on_device(): from_y_pair = lax.ppermute(to_y_pair, both, y_pairs)  2.54 us
    pallas_call x1, Pallas kernels, on_device(): call(inner_rows_kernel, 'inner_rows', [VMEM] * 9, [VMEM] * 2 + [HBM] + [V...  2.28 us
    pallas_call x1, Pallas kernels, on_device(): call(outer_rows_kernel, 'outer_rows', [VMEM] * 11 + [HBM], [VMEM] * 3 + [...  2.07 us
    ppermute x1, starting transfers between devices, on_device(): from_next = lax.ppermute(to_next, both, z_nexts)  1.7 us
    ppermute x1, starting transfers between devices, on_device(): ends_pair = lax.ppermute(to_y_pair, both, y_pairs)  1.55 us
    ppermute x1, starting transfers between devices, on_device(): from_pair = lax.ppermute(to_pair, both, z_pairs)  1.5 us
    unnamed x10, local copies, waits for them, and re-layouts  1.13 us
  transfers between devices with their start and end apart: 6, of which 0 were waited for; matrix products, arithmetic and copies ran while one was open for 0% of the time, Pallas kernels for 8%

profile of v5, /device:TPU:1, one launch (start us, length us, event | category | flops | bytes accessed | tf_op | source)
XLA Modules:
  0.0 41.3 jit_solution(4613923009771281545)
XLA Ops:
  0.6 0.0 copy-start
  0.6 0.0 copy-start.1
  0.6 0.8 %copy-done.1 = f32[19,19]{1,0:T(8,128)S(1)} copy-done((f32[19,19]{1,0:T(8,128)S(1)}, f32[19,19]{1,0:T(8,128)}, u32[]{:S(2)}) %copy-start.1) | copy-done | bytes 1468
  1.5 0.6 %weights.1 = (f32[160,480]{1,0:T(8,128)S(1)}, f32[160,144]{1,0:T(8,128)S(1)}, f32[160,144]{1,0:T(8,128)S(1)}) custom-call(f32[19,19]{1,0:T(8,128)S(1)} %copy-done.1), custom_call_target="tpu_custom_call" | custom-call | flops 4000000000 | bytes 4000000 | tf_op jit(solution)/shard_map/weights/pallas_call | solution.py:509
  2.1 0.3 copy-done
  2.3 0.1 pack_z.1
  2.4 1.5 %collective-permute-start = (f32[152,128]{1,0:T(8,128)S(1)}, f32[152,128]{1,0:T(8,128)S(1)}, u32[]{:S(2)}, u32[]{:S(2)}) collective-permute-start(f32[152,128]{1,0:T(8,128)S(1)} %get-tuple-element.27), channel_id=1, source_target_pairs={{0,1},{1,0},{2,3},{3,2},{4,5},{5,4},{6,7},{7,6},{8,9},{9,8},{10,11... | collective-permute-start | bytes 233480 | tf_op jit(solution)/shard_map/ppermute | solution.py:518
  3.9 1.7 %collective-permute-start.1 = (f32[152,128]{1,0:T(8,128)S(1)}, f32[152,128]{1,0:T(8,128)S(1)}, u32[]{:S(2)}, u32[]{:S(2)}) collective-permute-start(f32[152,128]{1,0:T(8,128)S(1)} %get-tuple-element.28), channel_id=1, source_target_pairs={{0,8},{1,2},{2,1},{3,4},{4,3},{5,6},{6,5},{7,15},{8,0},{9,10},{10,... | collective-permute-start | bytes 233480 | tf_op jit(solution)/shard_map/ppermute | solution.py:519
  5.6 0.5 %bulk_rows.1 = (f32[19,10,48,128]{3,2,1,0:T(8,128)S(1)}, f32[19,10,48,128]{3,2,1,0:T(8,128)S(1)}, f32[320,128]{1,0:T(8,128)S(1)}, f32[320,128]{1,0:T(8,128)S(1)}) custom-call(f32[19,256,128]{2,1,0:T(8,128)S(1)} %bitcast.13, f32[160,480]{1,0:T(8,128)S(1)} %get-tuple-element.23.w, f32[8,128]{1,0:T(8,128)S(1)} %get-tuple-element.24.empty), custom_call_target="tpu_custom_call" | custom-call | tf_op jit(solution)/shard_map/bulk_rows/pallas_call | solution.py:521
  6.2 0.1 collective-permute-start.2
  6.3 2.5 %collective-permute-start.3 = (f32[320,128]{1,0:T(8,128)S(1)}, f32[320,128]{1,0:T(8,128)S(1)}, u32[]{:S(2)}, u32[]{:S(2)}) collective-permute-start(f32[320,128]{1,0:T(8,128)S(1)} %get-tuple-element.35), channel_id=1, source_target_pairs={{0,8},{1,9},{2,10},{3,11},{4,12},{5,13},{6,14},{7,15},{8,0},{9,1},... | collective-permute-start | bytes 491528 | tf_op jit(solution)/shard_map/ppermute | solution.py:525
  8.8 0.0 collective-permute-done.from_pair
  8.8 0.0 collective-permute-done.1.from_next
  8.8 0.0 copy-start.2
  8.9 0.0 copy-start.3
  8.9 0.0 copy-start.4
  8.9 0.5 %end_cells.1 = (f32[19,10,48,128]{3,2,1,0:T(8,128)S(1)}, f32[19,10,48,128]{3,2,1,0:T(8,128)S(1)}, f32[24,128]{1,0:T(8,128)S(1)}, f32[24,128]{1,0:T(8,128)S(1)}) custom-call(f32[19,10,48,128]{3,2,1,0:T(8,128)S(1)} %get-tuple-element.25.s0_in, f32[19,10,48,128]{3,2,1,0:T(8,128)S(1)} %get-tuple-element.26.s1_in, ...), custom_call_target="tpu_custom_call", output_to_operand_aliasing={{0}: (0, {}), {1}: (1, {})} | custom-call | tf_op jit(solution)/shard_map/end_cells/pallas_call | solution.py:527
  9.4 0.4 collective-permute-start.4
  9.8 1.6 %collective-permute-start.5 = (f32[24,128]{1,0:T(8,128)S(1)}, f32[24,128]{1,0:T(8,128)S(1)}, u32[]{:S(2)}, u32[]{:S(2)}) collective-permute-start(f32[24,128]{1,0:T(8,128)S(1)} %get-tuple-element.37), channel_id=1, source_target_pairs={{0,8},{1,9},{2,10},{3,11},{4,12},{5,13},{6,14},{7,15},{8,0},{9,1},... | collective-permute-start | bytes 36872 | tf_op jit(solution)/shard_map/ppermute | solution.py:533
  11.3 0.0 copy-done.2
  11.3 0.0 copy-done.3
  11.3 0.0 copy-done.4
  11.3 2.3 %inner_rows.1 = (f32[19,10,48,128]{3,2,1,0:T(8,128)S(1)}, f32[19,10,48,128]{3,2,1,0:T(8,128)S(1)}, f32[19,8,32,128]{3,2,1,0:T(8,128)}, f32[4864,128]{1,0:T(8,128...) custom-call(f32[19,10,48,128]{3,2,1,0:T(8,128)S(1)} %get-tuple-element.29., ...), custom_call_target="tpu_custom_call", output_to_operand_aliasing={{0}: (0, {}), {1}: (2, {})} | custom-call | flops 4000000000 | bytes 4000000 | tf_op jit(solution)/shard_map/inner_rows/pallas_call | solution.py:537
  13.6 0.0 collective-permute-done.4.ends_next
  13.6 0.0 collective-permute-done.5.ends_pair
  13.6 0.0 collective-permute-done.2.from_next
  13.6 0.0 collective-permute-done.3.from_pair
  13.6 2.1 %outer_rows.1 = (f32[19,10,48,128]{3,2,1,0:T(8,128)S(1)}, f32[4864,128]{1,0:T(8,128)S(1)}, f32[1152,1,128]{2,1,0:T(1,128)S(1)}, f32[19,8,32,128]{3,2,1,0:T(8,128)}) custom-call(f32[19,10,48,128]{3,2,1,0:T(8,128)S(1)} %get-tuple-element.33.s1_in, ...), custom_call_target="tpu_custom_call", output_to_operand_aliasing={{0}: (0, {}), {1}: (9, {}), {2}: (10, {}), {3}: (11, {})} | custom-call | tf_op jit(solution)/shard_map/outer_rows/pallas_call | solution.py:550
  15.7 24.7 %all_to_all.5 = f32[128,9,1,128]{3,2,1,0:T(1,128)S(1)} all-to-all(f32[128,9,1,128]{3,2,1,0:T(1,128)S(1)} %bitcast.16), channel_id=1, replica_groups=mesh['gy'=16,'gz'=8] {'gy','gz'}, dimensions={0} | all-to-all | bytes 1179648 | tf_op jit(solution)/shard_map/all_to_all | solution.py:563
  40.4 0.9 %sum_rows.1 = f32[64,128]{1,0:T(8,128)} custom-call(f32[1152,128]{1,0:T(8,128)S(1)} %bitcast.15), custom_call_target="tpu_custom_call" | custom-call | tf_op jit(solution)/shard_map/sum_rows/pallas_call | solution.py:566
Async XLA Ops:
  0.6 1.7 %copy-start = (f32[19,8,32,128]{3,2,1,0:T(8,128)S(1)}, f32[19,8,32,128]{3,2,1,0:T(8,128)}, u32[]{:S(2)}) copy-start(f32[19,8,32,128]{3,2,1,0:T(8,128)} %param.5) | copy-start | bytes 7471108
  0.6 0.9 %copy-start.1 = (f32[19,19]{1,0:T(8,128)S(1)}, f32[19,19]{1,0:T(8,128)}, u32[]{:S(2)}) copy-start(f32[19,19]{1,0:T(8,128)} %collision.1) | copy-start | bytes 4336
  2.4 6.4 %collective-permute-start = (f32[152,128]{1,0:T(8,128)S(1)}, f32[152,128]{1,0:T(8,128)S(1)}, u32[]{:S(2)}, u32[]{:S(2)}) collective-permute-start(f32[152,128]{1,0:T(8,128)S(1)} %get-tuple-element.27), channel_id=1, source_target_pairs={{0,1},{1,0},{2,3},{3,2},{4,5},{5,4},{6,7},{7,6},{8,9},{9,8},{10,11... | collective-permute-start | bytes 233480 | tf_op jit(solution)/shard_map/ppermute | solution.py:518
  3.9 4.9 %collective-permute-start.1 = (f32[152,128]{1,0:T(8,128)S(1)}, f32[152,128]{1,0:T(8,128)S(1)}, u32[]{:S(2)}, u32[]{:S(2)}) collective-permute-start(f32[152,128]{1,0:T(8,128)S(1)} %get-tuple-element.28), channel_id=1, source_target_pairs={{0,8},{1,2},{2,1},{3,4},{4,3},{5,6},{6,5},{7,15},{8,0},{9,10},{10,... | collective-permute-start | bytes 233480 | tf_op jit(solution)/shard_map/ppermute | solution.py:519
  6.2 7.5 %collective-permute-start.2 = (f32[320,128]{1,0:T(8,128)S(1)}, f32[320,128]{1,0:T(8,128)S(1)}, u32[]{:S(2)}, u32[]{:S(2)}) collective-permute-start(f32[320,128]{1,0:T(8,128)S(1)} %get-tuple-element.34), channel_id=1, source_target_pairs={{0,1},{1,0},{2,3},{3,2},{4,5},{5,4},{6,7},{7,6},{8,16},{9,17},{10,... | collective-permute-start | bytes 491528 | tf_op jit(solution)/shard_map/ppermute | solution.py:526
  6.3 7.3 %collective-permute-start.3 = (f32[320,128]{1,0:T(8,128)S(1)}, f32[320,128]{1,0:T(8,128)S(1)}, u32[]{:S(2)}, u32[]{:S(2)}) collective-permute-start(f32[320,128]{1,0:T(8,128)S(1)} %get-tuple-element.35), channel_id=1, source_target_pairs={{0,8},{1,9},{2,10},{3,11},{4,12},{5,13},{6,14},{7,15},{8,0},{9,1},... | collective-permute-start | bytes 491528 | tf_op jit(solution)/shard_map/ppermute | solution.py:525
  8.8 2.5 %copy-start.2 = (s32[1,128,8]{1,2,0:T(8,128)S(1)}, s32[1,128,8]{1,2,0:T(8,128)}, u32[]{:S(2)}) copy-start(s32[1,128,8]{1,2,0:T(8,128)} %param.9) | copy-start | bytes 12292
  8.9 2.5 %copy-start.3 = (s32[1,128,8]{1,2,0:T(8,128)S(1)}, s32[1,128,8]{1,2,0:T(8,128)}, u32[]{:S(2)}) copy-start(s32[1,128,8]{1,2,0:T(8,128)} %param.7) | copy-start | bytes 12292
  8.9 2.4 %copy-start.4 = (s32[1,128,8]{1,2,0:T(8,128)S(1)}, s32[1,128,8]{1,2,0:T(8,128)}, u32[]{:S(2)}) copy-start(s32[1,128,8]{1,2,0:T(8,128)} %param.8) | copy-start | bytes 12292
  9.4 4.2 %collective-permute-start.4 = (f32[24,128]{1,0:T(8,128)S(1)}, f32[24,128]{1,0:T(8,128)S(1)}, u32[]{:S(2)}, u32[]{:S(2)}) collective-permute-start(f32[24,128]{1,0:T(8,128)S(1)} %get-tuple-element.36), channel_id=1, source_target_pairs={{0,1},{1,0},{2,3},{3,2},{4,5},{5,4},{6,7},{7,6},{8,16},{9,17},{10,... | collective-permute-start | bytes 36872 | tf_op jit(solution)/shard_map/ppermute | solution.py:534
  9.8 3.9 %collective-permute-start.5 = (f32[24,128]{1,0:T(8,128)S(1)}, f32[24,128]{1,0:T(8,128)S(1)}, u32[]{:S(2)}, u32[]{:S(2)}) collective-permute-start(f32[24,128]{1,0:T(8,128)S(1)} %get-tuple-element.37), channel_id=1, source_target_pairs={{0,8},{1,9},{2,10},{3,11},{4,12},{5,13},{6,14},{7,15},{8,0},{9,1},... | collective-permute-start | bytes 36872 | tf_op jit(solution)/shard_map/ppermute | solution.py:533

commit v6 on v4

--- a/solution.py
+++ b/solution.py
@@ -378,7 +378,7 @@
 
 
 def middle_tiles_kernel(
-    s1_in, w, w_up, w_down, from_pair, from_next, scaled_in, s1, scaled, raw, kept
+    s1_in, w, w_up, w_down, from_next, from_pair, scaled_in, s1, scaled, raw, kept
 ):
     del s1_in, scaled_in
     iy = lax.axis_index("gy")
@@ -418,7 +418,7 @@
 
 
 def outer_tiles_kernel(
-    s1_in, w, w_up, w_down, ends_pair, ends_next, pick_in, scaled_in, raw_in, kept_in,
+    s1_in, w, w_up, w_down, ends_next, ends_pair, pick_in, scaled_in, raw_in, kept_in,
     rows_in, out_in,
     s1, scaled, raw, kept, rows, out, spare, pick, pick_sem, out_sem,
 ):
@@ -611,7 +611,7 @@
         [(pad, f32), table, lines, edge],
         aliases={0: 0, 6: 1},
         cost=1_000_000_000,
-    )(s1, w, w_up, w_down, from_y_pair, from_y_next, scaled)
+    )(s1, w, w_up, w_down, from_y_next, from_y_pair, scaled)
     _, _, _, _, rows, out = call(
         outer_tiles_kernel, "outer_tiles", [VMEM] * 11 + [HBM], [VMEM] * 5 + [HBM],
         [(pad, f32), table, lines, edge, message, (own, f32)],
@@ -622,7 +622,7 @@
             dma((2,)),
         ],
         aliases={0: 0, 7: 1, 8: 2, 9: 3, 10: 4, 11: 5},
-    )(s1, w, w_up, w_down, ends_pair, ends_next, pick, scaled, raw, kept, rows, out)
+    )(s1, w, w_up, w_down, ends_next, ends_pair, pick, scaled, raw, kept, rows, out)
     arrived = lax.all_to_all(
         rows.reshape(devices, CAP + 1, 1, X), ("gy", "gz"), split_axis=0, concat_axis=0, tiled=True
     )

time: 42.5 us -> 41.5 us (0.976)
  blocking collectives: 26 us -> 24.3 us
  starting transfers between devices: 6.71 us -> 7.82 us
  waiting for transfers between devices: 0.5 us -> 0.02 us
    all_to_all x1, blocking collectives: 26 us -> 24.3 us  [on_device(): lax.all_to_all(rows.reshape(devices, CAP + 1, 1, X), ('gy', 'gz'), split_...]
    ppermute x1, starting transfers between devices: 1.38 us -> 2.54 us  [on_device(): from_y_pair = lax.ppermute(to_y_pair, both, y_pairs)]
    ppermute x1, waiting for transfers between devices: 0.49 us -> 0.01 us  [on_device(): from_next = lax.ppermute(to_next, both, z_nexts)]
  transfers between devices with their start and end apart: 6 -> 6, of which waited for: 1 -> 0; matrix products, arithmetic and copies ran while one was open for 0% -> 0% of each run, Pallas kernels for 9% -> 10%
where the time goes in v6:
time: 41.5 us; the launch traced here: 41.4 us
  blocking collectives  24.3 us (59%)
  starting transfers between devices  7.82 us (19%)
  Pallas kernels  7.34 us (18%)
  local copies, waits for them, and re-layouts  1.13 us (3%)
  between operations  0.74 us (2%)
    all_to_all x1, blocking collectives, on_device(): lax.all_to_all(rows.reshape(devices, CAP + 1, 1, X), ('gy', 'gz'), split_...  24.3 us
    ppermute x1, starting transfers between devices, on_device(): from_y_pair = lax.ppermute(to_y_pair, both, y_pairs)  2.54 us
    pallas_call x1, Pallas kernels, on_device(): call(inner_rows_kernel, 'inner_rows', [VMEM] * 9, [VMEM] * 2 + [HBM] + [V...  2.28 us
    pallas_call x1, Pallas kernels, on_device(): call(outer_tiles_kernel, 'outer_tiles', [VMEM] * 11 + [HBM], [VMEM] * 5 +...  1.79 us
    ppermute x1, starting transfers between devices, on_device(): from_next = lax.ppermute(to_next, both, z_nexts)  1.7 us
    ppermute x1, starting transfers between devices, on_device(): ends_pair = lax.ppermute(to_y_pair, both, y_pairs)  1.55 us
    ppermute x1, starting transfers between devices, on_device(): from_pair = lax.ppermute(to_pair, both, z_pairs)  1.5 us
    unnamed x10, local copies, waits for them, and re-layouts  1.13 us
  transfers between devices with their start and end apart: 6, of which 0 were waited for; matrix products, arithmetic and copies ran while one was open for 0% of the time, Pallas kernels for 10%

profile of v6, /device:TPU:1, one launch (start us, length us, event | category | flops | bytes accessed | tf_op | source)
XLA Modules:
  0.0 41.4 jit_solution(9812221953544209183)
XLA Ops:
  0.6 0.0 copy-start
  0.6 0.0 copy-start.1
  0.6 0.8 %copy-done.1 = f32[19,19]{1,0:T(8,128)S(1)} copy-done((f32[19,19]{1,0:T(8,128)S(1)}, f32[19,19]{1,0:T(8,128)}, u32[]{:S(2)}) %copy-start.1) | copy-done | bytes 1468
  1.5 0.6 %weights.1 = (f32[160,480]{1,0:T(8,128)S(1)}, f32[160,144]{1,0:T(8,128)S(1)}, f32[160,144]{1,0:T(8,128)S(1)}) custom-call(f32[19,19]{1,0:T(8,128)S(1)} %copy-done.1), custom_call_target="tpu_custom_call" | custom-call | flops 4000000000 | bytes 4000000 | tf_op jit(solution)/shard_map/weights/pallas_call | solution.py:566
  2.1 0.3 copy-done
  2.3 0.1 pack_z.1
  2.4 1.5 %collective-permute-start = (f32[152,128]{1,0:T(8,128)S(1)}, f32[152,128]{1,0:T(8,128)S(1)}, u32[]{:S(2)}, u32[]{:S(2)}) collective-permute-start(f32[152,128]{1,0:T(8,128)S(1)} %get-tuple-element.31), channel_id=1, source_target_pairs={{0,1},{1,0},{2,3},{3,2},{4,5},{5,4},{6,7},{7,6},{8,9},{9,8},{10,11... | collective-permute-start | bytes 233480 | tf_op jit(solution)/shard_map/ppermute | solution.py:575
  3.9 1.7 %collective-permute-start.1 = (f32[152,128]{1,0:T(8,128)S(1)}, f32[152,128]{1,0:T(8,128)S(1)}, u32[]{:S(2)}, u32[]{:S(2)}) collective-permute-start(f32[152,128]{1,0:T(8,128)S(1)} %get-tuple-element.32), channel_id=1, source_target_pairs={{0,8},{1,2},{2,1},{3,4},{4,3},{5,6},{6,5},{7,15},{8,0},{9,10},{10,... | collective-permute-start | bytes 233480 | tf_op jit(solution)/shard_map/ppermute | solution.py:576
  5.6 0.5 %bulk_rows.1 = (f32[19,10,48,128]{3,2,1,0:T(8,128)S(1)}, f32[19,10,48,128]{3,2,1,0:T(8,128)S(1)}, f32[320,128]{1,0:T(8,128)S(1)}, f32[320,128]{1,0:T(8,128)S(1)}) custom-call(f32[19,256,128]{2,1,0:T(8,128)S(1)} %bitcast.13, f32[160,480]{1,0:T(8,128)S(1)} %get-tuple-element.27.w, f32[8,128]{1,0:T(8,128)S(1)} %get-tuple-element.28.empty), custom_call_target="tpu_custom_call" | custom-call | tf_op jit(solution)/shard_map/bulk_rows/pallas_call | solution.py:578
  6.2 0.1 collective-permute-start.2
  6.3 2.5 %collective-permute-start.3 = (f32[320,128]{1,0:T(8,128)S(1)}, f32[320,128]{1,0:T(8,128)S(1)}, u32[]{:S(2)}, u32[]{:S(2)}) collective-permute-start(f32[320,128]{1,0:T(8,128)S(1)} %get-tuple-element.39), channel_id=1, source_target_pairs={{0,8},{1,9},{2,10},{3,11},{4,12},{5,13},{6,14},{7,15},{8,0},{9,1},... | collective-permute-start | bytes 491528 | tf_op jit(solution)/shard_map/ppermute | solution.py:582
  8.8 0.0 collective-permute-done.from_pair
  8.8 0.0 collective-permute-done.1.from_next
  8.8 0.0 copy-start.2
  8.9 0.0 copy-start.3
  8.9 0.0 copy-start.4
  8.9 0.5 %end_cells.1 = (f32[19,10,48,128]{3,2,1,0:T(8,128)S(1)}, f32[19,10,48,128]{3,2,1,0:T(8,128)S(1)}, f32[24,128]{1,0:T(8,128)S(1)}, f32[24,128]{1,0:T(8,128)S(1)}) custom-call(f32[19,10,48,128]{3,2,1,0:T(8,128)S(1)} %get-tuple-element.29.s0_in, f32[19,10,48,128]{3,2,1,0:T(8,128)S(1)} %get-tuple-element.30.s1_in, ...), custom_call_target="tpu_custom_call", output_to_operand_aliasing={{0}: (0, {}), {1}: (1, {})} | custom-call | tf_op jit(solution)/shard_map/end_cells/pallas_call | solution.py:584
  9.4 0.4 collective-permute-start.4
  9.8 1.6 %collective-permute-start.5 = (f32[24,128]{1,0:T(8,128)S(1)}, f32[24,128]{1,0:T(8,128)S(1)}, u32[]{:S(2)}, u32[]{:S(2)}) collective-permute-start(f32[24,128]{1,0:T(8,128)S(1)} %get-tuple-element.43), channel_id=1, source_target_pairs={{0,8},{1,9},{2,10},{3,11},{4,12},{5,13},{6,14},{7,15},{8,0},{9,1},... | collective-permute-start | bytes 36872 | tf_op jit(solution)/shard_map/ppermute | solution.py:590
  11.3 0.0 copy-done.2
  11.3 0.0 copy-done.3
  11.3 0.0 copy-done.4
  11.3 2.3 %inner_rows.1 = (f32[19,10,48,128]{3,2,1,0:T(8,128)S(1)}, f32[19,10,48,128]{3,2,1,0:T(8,128)S(1)}, f32[19,8,32,128]{3,2,1,0:T(8,128)}, f32[4864,128]{1,0:T(8,128...) custom-call(f32[19,10,48,128]{3,2,1,0:T(8,128)S(1)} %get-tuple-element.33., ...), custom_call_target="tpu_custom_call", output_to_operand_aliasing={{0}: (0, {}), {1}: (2, {})} | custom-call | flops 4000000000 | bytes 4000000 | tf_op jit(solution)/shard_map/inner_rows/pallas_call | solution.py:594
  13.6 0.0 collective-permute-done.2.from_next
  13.6 0.0 collective-permute-done.3.from_pair
  13.6 0.7 %middle_tiles.1 = (f32[19,10,48,128]{3,2,1,0:T(8,128)S(1)}, f32[4864,128]{1,0:T(8,128)S(1)}, f32[2,5,48,128]{3,2,1,0:T(8,128)S(1)}, f32[19,4,32,128]{3,2,1,0:T(8,128)S(1)}) custom-call(f32[19,10,48,128]{3,2,1,0:T(8,128)S(1)} %get-tuple-element.37.s1_in, f32[160,480]{1,0:T(8,128)S(1)} %get-tuple-element.27.w, ...), custom_call_target="tpu_custom_call", output_to_operand_aliasing={{0}: (0, {}), {1}: (6, {})} | custom-call | flops 1000000000 | bytes 1000000 | tf_op jit(solution)/shard_map/middle_tiles/pallas_call | solution.py:609
  14.3 0.0 collective-permute-done.4.ends_next
  14.3 0.0 collective-permute-done.5.ends_pair
  14.3 1.8 %outer_tiles.1 = (f32[19,10,48,128]{3,2,1,0:T(8,128)S(1)}, f32[4864,128]{1,0:T(8,128)S(1)}, f32[2,5,48,128]{3,2,1,0:T(8,128)S(1)}, f32[19,4,32,128]{3,2,1,0:T(8,...) custom-call(f32[19,10,48,128]{3,2,1,0:T(8,128)S(1)} %get-tuple-eleme, ...), custom_call_target="tpu_custom_call", output_to_operand_aliasing={{0}: (0, {}), {1}: (7, {}), {2}: (8, {}), {3}: (9, {}), {4}... | custom-call | tf_op jit(solution)/shard_map/outer_tiles/pallas_call | solution.py:615
  16.1 24.3 %all_to_all.5 = f32[128,9,1,128]{3,2,1,0:T(1,128)S(1)} all-to-all(f32[128,9,1,128]{3,2,1,0:T(1,128)S(1)} %bitcast.15), channel_id=1, replica_groups=mesh['gy'=16,'gz'=8] {'gy','gz'}, dimensions={0} | all-to-all | bytes 1179648 | tf_op jit(solution)/shard_map/all_to_all | solution.py:626
  40.5 0.9 %sum_rows.1 = f32[64,128]{1,0:T(8,128)} custom-call(f32[1152,128]{1,0:T(8,128)S(1)} %bitcast.16), custom_call_target="tpu_custom_call" | custom-call | tf_op jit(solution)/shard_map/sum_rows/pallas_call | solution.py:629
Async XLA Ops:
  0.6 1.7 %copy-start = (f32[19,8,32,128]{3,2,1,0:T(8,128)S(1)}, f32[19,8,32,128]{3,2,1,0:T(8,128)}, u32[]{:S(2)}) copy-start(f32[19,8,32,128]{3,2,1,0:T(8,128)} %param.5) | copy-start | bytes 7471108
  0.6 0.9 %copy-start.1 = (f32[19,19]{1,0:T(8,128)S(1)}, f32[19,19]{1,0:T(8,128)}, u32[]{:S(2)}) copy-start(f32[19,19]{1,0:T(8,128)} %collision.1) | copy-start | bytes 4336
  2.4 6.4 %collective-permute-start = (f32[152,128]{1,0:T(8,128)S(1)}, f32[152,128]{1,0:T(8,128)S(1)}, u32[]{:S(2)}, u32[]{:S(2)}) collective-permute-start(f32[152,128]{1,0:T(8,128)S(1)} %get-tuple-element.31), channel_id=1, source_target_pairs={{0,1},{1,0},{2,3},{3,2},{4,5},{5,4},{6,7},{7,6},{8,9},{9,8},{10,11... | collective-permute-start | bytes 233480 | tf_op jit(solution)/shard_map/ppermute | solution.py:575
  3.9 4.9 %collective-permute-start.1 = (f32[152,128]{1,0:T(8,128)S(1)}, f32[152,128]{1,0:T(8,128)S(1)}, u32[]{:S(2)}, u32[]{:S(2)}) collective-permute-start(f32[152,128]{1,0:T(8,128)S(1)} %get-tuple-element.32), channel_id=1, source_target_pairs={{0,8},{1,2},{2,1},{3,4},{4,3},{5,6},{6,5},{7,15},{8,0},{9,10},{10,... | collective-permute-start | bytes 233480 | tf_op jit(solution)/shard_map/ppermute | solution.py:576
  6.2 7.4 %collective-permute-start.2 = (f32[320,128]{1,0:T(8,128)S(1)}, f32[320,128]{1,0:T(8,128)S(1)}, u32[]{:S(2)}, u32[]{:S(2)}) collective-permute-start(f32[320,128]{1,0:T(8,128)S(1)} %get-tuple-element.38), channel_id=1, source_target_pairs={{0,1},{1,0},{2,3},{3,2},{4,5},{5,4},{6,7},{7,6},{8,16},{9,17},{10,... | collective-permute-start | bytes 491528 | tf_op jit(solution)/shard_map/ppermute | solution.py:583
  6.3 7.3 %collective-permute-start.3 = (f32[320,128]{1,0:T(8,128)S(1)}, f32[320,128]{1,0:T(8,128)S(1)}, u32[]{:S(2)}, u32[]{:S(2)}) collective-permute-start(f32[320,128]{1,0:T(8,128)S(1)} %get-tuple-element.39), channel_id=1, source_target_pairs={{0,8},{1,9},{2,10},{3,11},{4,12},{5,13},{6,14},{7,15},{8,0},{9,1},... | collective-permute-start | bytes 491528 | tf_op jit(solution)/shard_map/ppermute | solution.py:582
  8.8 2.5 %copy-start.2 = (s32[1,128,8]{1,2,0:T(8,128)S(1)}, s32[1,128,8]{1,2,0:T(8,128)}, u32[]{:S(2)}) copy-start(s32[1,128,8]{1,2,0:T(8,128)} %param.9) | copy-start | bytes 12292
  8.9 2.5 %copy-start.3 = (s32[1,128,8]{1,2,0:T(8,128)S(1)}, s32[1,128,8]{1,2,0:T(8,128)}, u32[]{:S(2)}) copy-start(s32[1,128,8]{1,2,0:T(8,128)} %param.7) | copy-start | bytes 12292
  8.9 2.4 %copy-start.4 = (s32[1,128,8]{1,2,0:T(8,128)S(1)}, s32[1,128,8]{1,2,0:T(8,128)}, u32[]{:S(2)}) copy-start(s32[1,128,8]{1,2,0:T(8,128)} %param.8) | copy-start | bytes 12292
  9.4 5.0 %collective-permute-start.4 = (f32[24,128]{1,0:T(8,128)S(1)}, f32[24,128]{1,0:T(8,128)S(1)}, u32[]{:S(2)}, u32[]{:S(2)}) collective-permute-start(f32[24,128]{1,0:T(8,128)S(1)} %get-tuple-element.42), channel_id=1, source_target_pairs={{0,1},{1,0},{2,3},{3,2},{4,5},{5,4},{6,7},{7,6},{8,16},{9,17},{10,... | collective-permute-start | bytes 36872 | tf_op jit(solution)/shard_map/ppermute | solution.py:591
  9.8 4.6 %collective-permute-start.5 = (f32[24,128]{1,0:T(8,128)S(1)}, f32[24,128]{1,0:T(8,128)S(1)}, u32[]{:S(2)}, u32[]{:S(2)}) collective-permute-start(f32[24,128]{1,0:T(8,128)S(1)} %get-tuple-element.43), channel_id=1, source_target_pairs={{0,8},{1,9},{2,10},{3,11},{4,12},{5,13},{6,14},{7,15},{8,0},{9,1},... | collective-permute-start | bytes 36872 | tf_op jit(solution)/shard_map/ppermute | solution.py:590

commit v7 on v5

--- a/solution.py
+++ b/solution.py
@@ -199,15 +199,20 @@
     even = lax.rem(iz, 2) == 0
     above = iz < lax.axis_size("gz") - 1
     below = iz > 0
-    for i in range(Q):
-        pair = from_pair[8 * i : 8 * i + 8, :]
-        following = from_next[8 * i : 8 * i + 8, :]
-        q, d = SEND_LOW[i]
-        value = jnp.where(above, jnp.where(even, pair, following), 0.0)
-        store_column(s0, q, 0, CZ + d, along_x(value, q))
-        q, d = SEND_HIGH[i]
-        value = jnp.where(below, jnp.where(even, following, pair), 0.0)
-        store_column(s0, q, 0, -1 - d, along_x(value, q))
+
+    def insert(sends, place, arrived):
+        for i, (q, d) in enumerate(sends):
+            value = 0.0 if arrived is None else along_x(arrived[8 * i : 8 * i + 8, :], q)
+            store_column(s0, q, 0, place(d), jnp.broadcast_to(value, (CY, X)))
+
+    for sends, place, valid, when_even, when_odd in (
+        (SEND_LOW, lambda d: CZ + d, above, from_pair, from_next),
+        (SEND_HIGH, lambda d: -1 - d, below, from_next, from_pair),
+    ):
+        put = functools.partial(insert, sends, place)
+        pl.when(jnp.logical_and(valid, even))(functools.partial(put, when_even))
+        pl.when(jnp.logical_and(valid, jnp.logical_not(even)))(functools.partial(put, when_odd))
+        pl.when(jnp.logical_not(valid))(functools.partial(put, None))
     last = CZ // 8 - 1
     spots = [(y, t) for y in (0, CY - 1) for t in (0, last)]
     corners = [(y, z) for y in (0, CY - 1) for z in (-1, CZ)]

time: 41.5 us -> 41.5 us (level)
  no operation moved by 1% of the time
where the time goes in v7:
time: 41.5 us; the launch traced here: 41.3 us
  blocking collectives  24.7 us (60%)
  starting transfers between devices  7.82 us (19%)
  Pallas kernels  7 us (17%)
  local copies, waits for them, and re-layouts  1.13 us (3%)
  between operations  0.73 us (2%)
    all_to_all x1, blocking collectives, on_device(): lax.all_to_all(rows.reshape(devices, CAP + 1, 1, X), ('gy', 'gz'), split_...  24.7 us
    ppermute x1, starting transfers between devices, on_device(): from_y_pair = lax.ppermute(to_y_pair, both, y_pairs)  2.54 us
    pallas_call x1, Pallas kernels, on_device(): call(inner_rows_kernel, 'inner_rows', [VMEM] * 9, [VMEM] * 2 + [HBM] + [V...  2.28 us
    pallas_call x1, Pallas kernels, on_device(): call(outer_rows_kernel, 'outer_rows', [VMEM] * 11 + [HBM], [VMEM] * 3 + [...  2.07 us
    ppermute x1, starting transfers between devices, on_device(): from_next = lax.ppermute(to_next, both, z_nexts)  1.7 us
    ppermute x1, starting transfers between devices, on_device(): ends_pair = lax.ppermute(to_y_pair, both, y_pairs)  1.59 us
    ppermute x1, starting transfers between devices, on_device(): from_pair = lax.ppermute(to_pair, both, z_pairs)  1.5 us
    unnamed x10, local copies, waits for them, and re-layouts  1.13 us
  transfers between devices with their start and end apart: 6, of which 0 were waited for; matrix products, arithmetic and copies ran while one was open for 0% of the time, Pallas kernels for 8%

profile of v7, /device:TPU:1, one launch (start us, length us, event | category | flops | bytes accessed | tf_op | source)
XLA Modules:
  0.0 41.3 jit_solution(3619069165141738054)
XLA Ops:
  0.6 0.0 copy-start
  0.6 0.0 copy-start.1
  0.6 0.8 %copy-done.1 = f32[19,19]{1,0:T(8,128)S(1)} copy-done((f32[19,19]{1,0:T(8,128)S(1)}, f32[19,19]{1,0:T(8,128)}, u32[]{:S(2)}) %copy-start.1) | copy-done | bytes 1468
  1.5 0.6 %weights.1 = (f32[160,480]{1,0:T(8,128)S(1)}, f32[160,144]{1,0:T(8,128)S(1)}, f32[160,144]{1,0:T(8,128)S(1)}) custom-call(f32[19,19]{1,0:T(8,128)S(1)} %copy-done.1), custom_call_target="tpu_custom_call" | custom-call | flops 4000000000 | bytes 4000000 | tf_op jit(solution)/shard_map/weights/pallas_call | solution.py:514
  2.1 0.3 copy-done
  2.3 0.1 pack_z.1
  2.4 1.5 %collective-permute-start = (f32[152,128]{1,0:T(8,128)S(1)}, f32[152,128]{1,0:T(8,128)S(1)}, u32[]{:S(2)}, u32[]{:S(2)}) collective-permute-start(f32[152,128]{1,0:T(8,128)S(1)} %get-tuple-element.27), channel_id=1, source_target_pairs={{0,1},{1,0},{2,3},{3,2},{4,5},{5,4},{6,7},{7,6},{8,9},{9,8},{10,11... | collective-permute-start | bytes 233480 | tf_op jit(solution)/shard_map/ppermute | solution.py:523
  3.9 1.7 %collective-permute-start.1 = (f32[152,128]{1,0:T(8,128)S(1)}, f32[152,128]{1,0:T(8,128)S(1)}, u32[]{:S(2)}, u32[]{:S(2)}) collective-permute-start(f32[152,128]{1,0:T(8,128)S(1)} %get-tuple-element.28), channel_id=1, source_target_pairs={{0,8},{1,2},{2,1},{3,4},{4,3},{5,6},{6,5},{7,15},{8,0},{9,10},{10,... | collective-permute-start | bytes 233480 | tf_op jit(solution)/shard_map/ppermute | solution.py:524
  5.6 0.5 %bulk_rows.1 = (f32[19,10,48,128]{3,2,1,0:T(8,128)S(1)}, f32[19,10,48,128]{3,2,1,0:T(8,128)S(1)}, f32[320,128]{1,0:T(8,128)S(1)}, f32[320,128]{1,0:T(8,128)S(1)}) custom-call(f32[19,256,128]{2,1,0:T(8,128)S(1)} %bitcast.13, f32[160,480]{1,0:T(8,128)S(1)} %get-tuple-element.23.w, f32[8,128]{1,0:T(8,128)S(1)} %get-tuple-element.24.empty), custom_call_target="tpu_custom_call" | custom-call | tf_op jit(solution)/shard_map/bulk_rows/pallas_call | solution.py:526
  6.2 0.1 collective-permute-start.2
  6.3 2.5 %collective-permute-start.3 = (f32[320,128]{1,0:T(8,128)S(1)}, f32[320,128]{1,0:T(8,128)S(1)}, u32[]{:S(2)}, u32[]{:S(2)}) collective-permute-start(f32[320,128]{1,0:T(8,128)S(1)} %get-tuple-element.35), channel_id=1, source_target_pairs={{0,8},{1,9},{2,10},{3,11},{4,12},{5,13},{6,14},{7,15},{8,0},{9,1},... | collective-permute-start | bytes 491528 | tf_op jit(solution)/shard_map/ppermute | solution.py:530
  8.8 0.0 collective-permute-done.from_pair
  8.8 0.0 collective-permute-done.1.from_next
  8.8 0.0 copy-start.2
  8.9 0.0 copy-start.3
  8.9 0.0 copy-start.4
  8.9 0.6 %end_cells.1 = (f32[19,10,48,128]{3,2,1,0:T(8,128)S(1)}, f32[19,10,48,128]{3,2,1,0:T(8,128)S(1)}, f32[24,128]{1,0:T(8,128)S(1)}, f32[24,128]{1,0:T(8,128)S(1)}) custom-call(f32[19,10,48,128]{3,2,1,0:T(8,128)S(1)} %get-tuple-element.25.s0_in, f32[19,10,48,128]{3,2,1,0:T(8,128)S(1)} %get-tuple-element.26.s1_in, ...), custom_call_target="tpu_custom_call", output_to_operand_aliasing={{0}: (0, {}), {1}: (1, {})} | custom-call | tf_op jit(solution)/shard_map/end_cells/pallas_call | solution.py:532
  9.4 0.4 collective-permute-start.4
  9.8 1.6 %collective-permute-start.5 = (f32[24,128]{1,0:T(8,128)S(1)}, f32[24,128]{1,0:T(8,128)S(1)}, u32[]{:S(2)}, u32[]{:S(2)}) collective-permute-start(f32[24,128]{1,0:T(8,128)S(1)} %get-tuple-element.37), channel_id=1, source_target_pairs={{0,8},{1,9},{2,10},{3,11},{4,12},{5,13},{6,14},{7,15},{8,0},{9,1},... | collective-permute-start | bytes 36872 | tf_op jit(solution)/shard_map/ppermute | solution.py:538
  11.4 0.0 copy-done.2
  11.4 0.0 copy-done.3
  11.4 0.0 copy-done.4
  11.4 2.3 %inner_rows.1 = (f32[19,10,48,128]{3,2,1,0:T(8,128)S(1)}, f32[19,10,48,128]{3,2,1,0:T(8,128)S(1)}, f32[19,8,32,128]{3,2,1,0:T(8,128)}, f32[4864,128]{1,0:T(8,128...) custom-call(f32[19,10,48,128]{3,2,1,0:T(8,128)S(1)} %get-tuple-element.29., ...), custom_call_target="tpu_custom_call", output_to_operand_aliasing={{0}: (0, {}), {1}: (2, {})} | custom-call | flops 4000000000 | bytes 4000000 | tf_op jit(solution)/shard_map/inner_rows/pallas_call | solution.py:542
  13.7 0.0 collective-permute-done.4.ends_next
  13.7 0.0 collective-permute-done.5.ends_pair
  13.7 0.0 collective-permute-done.2.from_next
  13.7 0.0 collective-permute-done.3.from_pair
  13.7 2.1 %outer_rows.1 = (f32[19,10,48,128]{3,2,1,0:T(8,128)S(1)}, f32[4864,128]{1,0:T(8,128)S(1)}, f32[1152,1,128]{2,1,0:T(1,128)S(1)}, f32[19,8,32,128]{3,2,1,0:T(8,128)}) custom-call(f32[19,10,48,128]{3,2,1,0:T(8,128)S(1)} %get-tuple-element.33.s1_in, ...), custom_call_target="tpu_custom_call", output_to_operand_aliasing={{0}: (0, {}), {1}: (9, {}), {2}: (10, {}), {3}: (11, {})} | custom-call | tf_op jit(solution)/shard_map/outer_rows/pallas_call | solution.py:555
  15.8 24.7 %all_to_all.5 = f32[128,9,1,128]{3,2,1,0:T(1,128)S(1)} all-to-all(f32[128,9,1,128]{3,2,1,0:T(1,128)S(1)} %bitcast.16), channel_id=1, replica_groups=mesh['gy'=16,'gz'=8] {'gy','gz'}, dimensions={0} | all-to-all | bytes 1179648 | tf_op jit(solution)/shard_map/all_to_all | solution.py:568
  40.5 0.9 %sum_rows.1 = f32[64,128]{1,0:T(8,128)} custom-call(f32[1152,128]{1,0:T(8,128)S(1)} %bitcast.15), custom_call_target="tpu_custom_call" | custom-call | tf_op jit(solution)/shard_map/sum_rows/pallas_call | solution.py:571
Async XLA Ops:
  0.6 1.7 %copy-start = (f32[19,8,32,128]{3,2,1,0:T(8,128)S(1)}, f32[19,8,32,128]{3,2,1,0:T(8,128)}, u32[]{:S(2)}) copy-start(f32[19,8,32,128]{3,2,1,0:T(8,128)} %param.5) | copy-start | bytes 7471108
  0.6 0.9 %copy-start.1 = (f32[19,19]{1,0:T(8,128)S(1)}, f32[19,19]{1,0:T(8,128)}, u32[]{:S(2)}) copy-start(f32[19,19]{1,0:T(8,128)} %collision.1) | copy-start | bytes 4336
  2.4 6.4 %collective-permute-start = (f32[152,128]{1,0:T(8,128)S(1)}, f32[152,128]{1,0:T(8,128)S(1)}, u32[]{:S(2)}, u32[]{:S(2)}) collective-permute-start(f32[152,128]{1,0:T(8,128)S(1)} %get-tuple-element.27), channel_id=1, source_target_pairs={{0,1},{1,0},{2,3},{3,2},{4,5},{5,4},{6,7},{7,6},{8,9},{9,8},{10,11... | collective-permute-start | bytes 233480 | tf_op jit(solution)/shard_map/ppermute | solution.py:523
  3.9 4.9 %collective-permute-start.1 = (f32[152,128]{1,0:T(8,128)S(1)}, f32[152,128]{1,0:T(8,128)S(1)}, u32[]{:S(2)}, u32[]{:S(2)}) collective-permute-start(f32[152,128]{1,0:T(8,128)S(1)} %get-tuple-element.28), channel_id=1, source_target_pairs={{0,8},{1,2},{2,1},{3,4},{4,3},{5,6},{6,5},{7,15},{8,0},{9,10},{10,... | collective-permute-start | bytes 233480 | tf_op jit(solution)/shard_map/ppermute | solution.py:524
  6.2 7.5 %collective-permute-start.2 = (f32[320,128]{1,0:T(8,128)S(1)}, f32[320,128]{1,0:T(8,128)S(1)}, u32[]{:S(2)}, u32[]{:S(2)}) collective-permute-start(f32[320,128]{1,0:T(8,128)S(1)} %get-tuple-element.34), channel_id=1, source_target_pairs={{0,1},{1,0},{2,3},{3,2},{4,5},{5,4},{6,7},{7,6},{8,16},{9,17},{10,... | collective-permute-start | bytes 491528 | tf_op jit(solution)/shard_map/ppermute | solution.py:531
  6.3 7.4 %collective-permute-start.3 = (f32[320,128]{1,0:T(8,128)S(1)}, f32[320,128]{1,0:T(8,128)S(1)}, u32[]{:S(2)}, u32[]{:S(2)}) collective-permute-start(f32[320,128]{1,0:T(8,128)S(1)} %get-tuple-element.35), channel_id=1, source_target_pairs={{0,8},{1,9},{2,10},{3,11},{4,12},{5,13},{6,14},{7,15},{8,0},{9,1},... | collective-permute-start | bytes 491528 | tf_op jit(solution)/shard_map/ppermute | solution.py:530
  8.8 2.5 %copy-start.2 = (s32[1,128,8]{1,2,0:T(8,128)S(1)}, s32[1,128,8]{1,2,0:T(8,128)}, u32[]{:S(2)}) copy-start(s32[1,128,8]{1,2,0:T(8,128)} %param.9) | copy-start | bytes 12292
  8.9 2.5 %copy-start.3 = (s32[1,128,8]{1,2,0:T(8,128)S(1)}, s32[1,128,8]{1,2,0:T(8,128)}, u32[]{:S(2)}) copy-start(s32[1,128,8]{1,2,0:T(8,128)} %param.7) | copy-start | bytes 12292
  8.9 2.5 %copy-start.4 = (s32[1,128,8]{1,2,0:T(8,128)S(1)}, s32[1,128,8]{1,2,0:T(8,128)}, u32[]{:S(2)}) copy-start(s32[1,128,8]{1,2,0:T(8,128)} %param.8) | copy-start | bytes 12292
  9.4 4.2 %collective-permute-start.4 = (f32[24,128]{1,0:T(8,128)S(1)}, f32[24,128]{1,0:T(8,128)S(1)}, u32[]{:S(2)}, u32[]{:S(2)}) collective-permute-start(f32[24,128]{1,0:T(8,128)S(1)} %get-tuple-element.36), channel_id=1, source_target_pairs={{0,1},{1,0},{2,3},{3,2},{4,5},{5,4},{6,7},{7,6},{8,16},{9,17},{10,... | collective-permute-start | bytes 36872 | tf_op jit(solution)/shard_map/ppermute | solution.py:539
  9.8 3.9 %collective-permute-start.5 = (f32[24,128]{1,0:T(8,128)S(1)}, f32[24,128]{1,0:T(8,128)S(1)}, u32[]{:S(2)}, u32[]{:S(2)}) collective-permute-start(f32[24,128]{1,0:T(8,128)S(1)} %get-tuple-element.37), channel_id=1, source_target_pairs={{0,8},{1,9},{2,10},{3,11},{4,12},{5,13},{6,14},{7,15},{8,0},{9,1},... | collective-permute-start | bytes 36872 | tf_op jit(solution)/shard_map/ppermute | solution.py:538
